TPU v7x, 128 devices: a whole 4x4x4 slice. The times are simulated.
128 devices in a mesh: seq: 8 (over z, core), expert: 16 (over y, x).
Axes of the slice: x: 4, y: 4, z: 4, core: 2. Of those that a mesh axis runs over, the one named last changes fastest.
Arguments:
- residual: bfloat16 [16, 1024, 2048], P('expert', 'seq'), may hold values from -6 to 6
- queries: bfloat16 [16, 1024, 2048], P('expert', 'seq'), may hold values from -400 to 400
- key_input: bfloat16 [16, 1024, 512], P('expert', 'seq'), may hold values from -4 to 4
- value_input: bfloat16 [16, 1024, 512], P('expert', 'seq'), may hold values from -6 to 6
- routes: int32 [16, 1024, 6], P('expert', 'seq'), may hold values from 0 to 31, all different within a row; in each aligned block of 128 rows (0 to 127, 128 to 255, ..., all dimensions but the last counted through in order) at most 30 rows name the same one
- mix_weights: float32 [16, 1024, 6], P('expert', 'seq'), may hold values from 0.1 to 1
- gate_weight: bfloat16 [32, 2048, 704], P('expert'), may hold values from -0.125 to 0.125
- up_weight: bfloat16 [32, 2048, 704], P('expert'), may hold values from -0.125 to 0.125
- down_weight: bfloat16 [32, 704, 2048], P('expert'), may hold values from -0.21875 to 0.21875
- grad_out: bfloat16 [16, 1024, 2048], P('expert', 'seq'), may hold values from -6 to 6
Outputs:
- layer_out: bfloat16 [16, 1024, 2048], P('expert', 'seq')
- residual_grad: bfloat16 [16, 1024, 2048], P('expert', 'seq')
- query_grad: bfloat16 [16, 1024, 2048], P('expert', 'seq')
- key_grad: bfloat16 [16, 1024, 512], P('expert', 'seq')
- value_grad: bfloat16 [16, 1024, 512], P('expert', 'seq')
- mix_grad: float32 [16, 1024, 6], P('expert', 'seq')
- gate_weight_grad: bfloat16 [32, 2048, 704], P('expert', 'seq')
- up_weight_grad: bfloat16 [32, 2048, 704], P('expert', 'seq')
- down_weight_grad: bfloat16 [32, 704, 2048], P('expert', None, 'seq')
Inputs may be any that keep to these rules, and one draw needn't show every extreme that they name: `routes`: each row names 6 different experts. Among the rows of one device no expert is named by more than 30 rows, and in every draw some expert is named by exactly 30 rows of some device.
All inputs are finite; a program needn't handle non-finite values.
Results may differ from a plain program's by a relative error of at most 0.04.
Values may be sent and summed in bfloat16 or wider, within the bound.
No kernel may reach another device: no remote copies, remote signals or barrier semaphores. Data moves between devices by JAX's collectives and lax.ppermute only.
A program may use at most 192 MiB of HBM per device.

v0:
```python
import math

import jax
import jax.numpy as jnp
from jax import lax
from jax.sharding import PartitionSpec as P

DH = 128


neg_big = -1e30
norm_eps = 1e-06


def fold_keys(key_rows, value_rows, combine, initial):
    return combine(
        initial,
        (
            lax.all_gather(key_rows, "seq", axis=0, tiled=True),
            lax.all_gather(value_rows, "seq", axis=0, tiled=True),
        ),
        jnp.int32(0),
    )


def collect_rows(results):
    return lax.all_to_all(results, "expert", split_axis=1, concat_axis=1, tiled=True)


def silu_grads(act_grad, gate_pre, up_pre):
    sigmoid = jax.nn.sigmoid(gate_pre)
    gate_grad = (act_grad * up_pre * sigmoid * (1.0 + gate_pre * (1.0 - sigmoid))).astype(
        jnp.bfloat16
    )
    up_grad = (act_grad * gate_pre * sigmoid).astype(jnp.bfloat16)
    return (gate_grad, up_grad)


def dense_forward(expert_rows, gate_weight, up_weight, down_weight):
    gate_pre = jnp.einsum(
        "erd,edf->erf", expert_rows, gate_weight, preferred_element_type=jnp.float32
    )
    up_pre = jnp.einsum("erd,edf->erf", expert_rows, up_weight, preferred_element_type=jnp.float32)
    activation = (jax.nn.silu(gate_pre) * up_pre).astype(jnp.bfloat16)
    results = jnp.einsum(
        "erf,efd->erd", activation, down_weight, preferred_element_type=jnp.float32
    ).astype(jnp.bfloat16)
    return (results, (gate_pre, up_pre, activation))


def dense_backward(expert_rows, grad_rows, kept_values, gate_weight, up_weight, down_weight):
    gate_pre, up_pre, activation = kept_values
    act_grad = jnp.einsum(
        "erd,efd->erf", grad_rows, down_weight, preferred_element_type=jnp.float32
    )
    gate_grad, up_grad = silu_grads(act_grad, gate_pre, up_pre)
    input_grad = jnp.einsum(
        "erf,edf->erd", gate_grad, gate_weight, preferred_element_type=jnp.float32
    )
    input_grad = (
        input_grad
        + jnp.einsum("erf,edf->erd", up_grad, up_weight, preferred_element_type=jnp.float32)
    ).astype(jnp.bfloat16)
    gate_sum = jnp.einsum(
        "erd,erf->edf", expert_rows, gate_grad, preferred_element_type=jnp.float32
    )
    up_sum = jnp.einsum("erd,erf->edf", expert_rows, up_grad, preferred_element_type=jnp.float32)
    down_sum = jnp.einsum("erf,erd->efd", activation, grad_rows, preferred_element_type=jnp.float32)
    return (input_grad, (gate_sum, up_sum, down_sum))


def expert_forward(expert_rows, gate_weight, up_weight, down_weight):
    results, kept_values = dense_forward(expert_rows, gate_weight, up_weight, down_weight)
    return (results, (None, kept_values))


def expert_backward(expert_rows, grad_rows, kept_state, gate_weight, up_weight, down_weight):
    tile_plan, kept_values = kept_state
    return dense_backward(expert_rows, grad_rows, kept_values, gate_weight, up_weight, down_weight)


def on_device(
    residual,
    queries,
    key_input,
    value_input,
    routes,
    mix_weights,
    gate_weight,
    up_weight,
    down_weight,
    grad_out,
):
    tokens = residual.shape[1]
    width = residual.shape[2]
    kv_width = key_input.shape[2]
    kv_heads = kv_width // DH
    q_heads = queries.shape[2] // DH
    group_size = q_heads // kv_heads
    expert_local = gate_weight.shape[0]
    expert_ranks = lax.axis_size("expert")
    experts_all = expert_local * expert_ranks
    top_count = routes.shape[2]
    capacity = tokens * top_count * 5 // (4 * experts_all)
    total_slots = experts_all * capacity
    inv_scale = 1.0 / math.sqrt(DH)
    query_rows = queries.reshape(tokens, kv_heads, group_size, DH)
    key_rows = key_input.reshape(tokens, kv_width)
    value_rows = value_input.reshape(tokens, kv_width)
    row_pos = lax.axis_index("seq") * tokens + jnp.arange(tokens, dtype=jnp.int32)

    def block_scores(key_part):
        piece_rows = key_part.shape[0]
        key_heads = key_part.reshape(piece_rows, kv_heads, DH)
        scores = (
            jnp.einsum("tkgd,jkd->tkgj", query_rows, key_heads, preferred_element_type=jnp.float32)
            * inv_scale
        )
        key_pos = jnp.arange(piece_rows, dtype=jnp.int32)
        visible = (key_pos[None, :] <= row_pos[:, None])[:, None, None, :]
        return (key_heads, scores, visible)

    def attend(carried, pieces, offset):
        run_max, run_sum, accumulated = carried
        key_part, value_part = pieces
        key_heads, scores, visible = block_scores(key_part)
        masked = jnp.where(visible, scores, neg_big)
        new_max = jnp.maximum(run_max, jnp.max(masked, axis=3))
        weights = jnp.where(visible, jnp.exp(masked - new_max[..., None]), 0.0)
        value_heads = value_part.reshape(key_part.shape[0], kv_heads, DH)
        update = jnp.einsum(
            "tkgj,jkd->tkgd",
            weights.astype(jnp.bfloat16),
            value_heads,
            preferred_element_type=jnp.float32,
        )
        return (new_max, jnp.sum(weights, axis=3), update)

    state_shape = (tokens, kv_heads, group_size)
    initial = (
        jnp.full(state_shape, neg_big, jnp.float32),
        jnp.zeros(state_shape, jnp.float32),
        jnp.zeros(state_shape + (DH,), jnp.float32),
    )
    run_max, run_sum, accumulated = fold_keys(key_rows, value_rows, attend, initial)
    attention = (accumulated / run_sum[..., None]).astype(jnp.bfloat16)
    log_total = run_max + jnp.log(run_sum)
    hidden_state = residual.reshape(tokens, width).astype(jnp.float32) + attention.reshape(
        tokens, width
    ).astype(jnp.float32)
    inv_rms = lax.rsqrt(jnp.mean(hidden_state * hidden_state, axis=1, keepdims=True) + norm_eps)
    normed = hidden_state * inv_rms
    normed_bf = normed.astype(jnp.bfloat16)
    picked_experts = routes.reshape(tokens, top_count)
    expert_ids = jnp.arange(experts_all, dtype=jnp.int32)
    onehot = (picked_experts[:, :, None] == expert_ids[None, None, :]).astype(jnp.int32)
    per_token = jnp.sum(onehot, axis=1)
    earlier = jnp.cumsum(per_token, axis=0) - per_token
    slot_rank = jnp.sum(onehot * earlier[:, None, :], axis=2)
    owner_rank = picked_experts // expert_local
    local_id = picked_experts % expert_local
    slot_index = ((local_id * expert_ranks + owner_rank) * capacity + slot_rank).reshape(-1)
    pair_ids = jnp.arange(tokens * top_count, dtype=jnp.int32)
    slot_pair = jnp.zeros((total_slots,), jnp.int32).at[slot_index].set(pair_ids)
    slot_live = jnp.zeros((total_slots,), jnp.bool_).at[slot_index].set(True)
    slot_token = slot_pair // top_count
    block_shape = (expert_local, expert_ranks, capacity, width)
    zero_bf = jnp.zeros((), jnp.bfloat16)
    outgoing = jnp.where(
        slot_live[:, None], jnp.take(normed_bf, slot_token, axis=0), zero_bf
    ).reshape(block_shape)
    arrived = lax.all_to_all(outgoing, "expert", split_axis=1, concat_axis=1, tiled=True)
    expert_rows = arrived.reshape(expert_local, expert_ranks * capacity, width)
    results, kept_state = expert_forward(expert_rows, gate_weight, up_weight, down_weight)
    returned = collect_rows(results.reshape(block_shape)).reshape(total_slots, width)
    pair_out = jnp.take(returned, slot_index, axis=0).reshape(tokens, top_count, width)
    mix_rows = mix_weights.reshape(tokens, top_count)
    combined = hidden_state + jnp.sum(mix_rows[:, :, None] * pair_out.astype(jnp.float32), axis=1)
    layer_out = combined.astype(jnp.bfloat16)
    grad_rows = grad_out.reshape(tokens, width)
    mix_grad = jnp.einsum("td,tcd->tc", grad_rows, pair_out, preferred_element_type=jnp.float32)
    pair_grad = (
        (mix_rows[:, :, None] * grad_rows.astype(jnp.float32)[:, None, :])
        .astype(jnp.bfloat16)
        .reshape(tokens * top_count, width)
    )
    outgoing_grad = jnp.where(
        slot_live[:, None], jnp.take(pair_grad, slot_pair, axis=0), zero_bf
    ).reshape(block_shape)
    grads_arrived = lax.all_to_all(outgoing_grad, "expert", split_axis=1, concat_axis=1, tiled=True)
    grads_arrived = grads_arrived.reshape(expert_local, expert_ranks * capacity, width)
    input_grad, weight_sums = expert_backward(
        expert_rows, grads_arrived, kept_state, gate_weight, up_weight, down_weight
    )
    input_back = collect_rows(input_grad.reshape(block_shape)).reshape(total_slots, width)
    normed_grad = jnp.sum(
        jnp.take(input_back, slot_index, axis=0)
        .reshape(tokens, top_count, width)
        .astype(jnp.float32),
        axis=1,
    )
    dot_mean = jnp.mean(normed_grad * normed, axis=1, keepdims=True)
    hidden_grad = grad_rows.astype(jnp.float32) + inv_rms * (normed_grad - normed * dot_mean)
    residual_grad = hidden_grad.astype(jnp.bfloat16)
    gate_sum, up_sum, down_sum = weight_sums
    gate_share, up_share, down_share = (
        lax.psum_scatter(
            gate_sum.astype(jnp.bfloat16), "seq", scatter_dimension=1, tiled=True
        ).astype(jnp.float32),
        lax.psum_scatter(
            up_sum.astype(jnp.bfloat16), "seq", scatter_dimension=1, tiled=True
        ).astype(jnp.float32),
        lax.psum_scatter(
            down_sum.astype(jnp.bfloat16), "seq", scatter_dimension=2, tiled=True
        ).astype(jnp.float32),
    )
    out_grad_heads = residual_grad.reshape(tokens, kv_heads, group_size, DH)
    row_delta = jnp.einsum(
        "tkgd,tkgd->tkg", out_grad_heads, attention, preferred_element_type=jnp.float32
    )
    full_len = tokens * lax.axis_size("seq")

    def attend_back(carried, pieces, offset):
        key_part, value_part = pieces
        piece_rows = key_part.shape[0]
        key_heads, scores, visible = block_scores(key_part)
        probabilities = jnp.where(visible, jnp.exp(scores - log_total[..., None]), 0.0)
        value_heads = value_part.reshape(piece_rows, kv_heads, DH)
        prob_grad = jnp.einsum(
            "tkgd,jkd->tkgj", out_grad_heads, value_heads, preferred_element_type=jnp.float32
        )
        score_grad = (probabilities * (prob_grad - row_delta[..., None])).astype(jnp.bfloat16)
        query_acc = (
            jnp.einsum("tkgj,jkd->tkgd", score_grad, key_heads, preferred_element_type=jnp.float32)
            * inv_scale
        )
        key_piece = (
            jnp.einsum("tkgj,tkgd->jkd", score_grad, query_rows, preferred_element_type=jnp.float32)
            * inv_scale
        )
        value_piece = jnp.einsum(
            "tkgj,tkgd->jkd",
            probabilities.astype(jnp.bfloat16),
            out_grad_heads,
            preferred_element_type=jnp.float32,
        )
        return (query_acc, key_piece, value_piece)

    initial_back = (
        jnp.zeros(state_shape + (DH,), jnp.float32),
        jnp.zeros((full_len, kv_heads, DH), jnp.float32),
        jnp.zeros((full_len, kv_heads, DH), jnp.float32),
    )
    query_acc, key_acc, value_acc = fold_keys(key_rows, value_rows, attend_back, initial_back)
    key_share, value_share = (
        lax.psum_scatter(
            key_acc.reshape(full_len, kv_width).astype(jnp.bfloat16),
            "seq",
            scatter_dimension=0,
            tiled=True,
        ).astype(jnp.float32),
        lax.psum_scatter(
            value_acc.reshape(full_len, kv_width).astype(jnp.bfloat16),
            "seq",
            scatter_dimension=0,
            tiled=True,
        ).astype(jnp.float32),
    )
    return (
        layer_out.reshape(1, tokens, width),
        residual_grad.reshape(1, tokens, width),
        query_acc.reshape(1, tokens, q_heads * DH).astype(jnp.bfloat16),
        key_share.astype(jnp.bfloat16).reshape(1, tokens, kv_width),
        value_share.astype(jnp.bfloat16).reshape(1, tokens, kv_width),
        mix_grad.reshape(1, tokens, top_count),
        gate_share.astype(jnp.bfloat16),
        up_share.astype(jnp.bfloat16),
        down_share.astype(jnp.bfloat16),
    )


def solution(mesh):
    placed = (
        P("expert", "seq", None),
        P("expert", "seq", None),
        P("expert", "seq", None),
        P("expert", "seq", None),
        P("expert", "seq", None),
        P("expert", "seq", None),
        P("expert", None, None),
        P("expert", None, None),
        P("expert", None, None),
        P("expert", "seq", None),
    )
    return jax.shard_map(
        on_device,
        mesh=mesh,
        in_specs=placed,
        out_specs=(
            P("expert", "seq", None),
            P("expert", "seq", None),
            P("expert", "seq", None),
            P("expert", "seq", None),
            P("expert", "seq", None),
            P("expert", "seq", None),
            P("expert", "seq", None),
            P("expert", "seq", None),
            P("expert", None, "seq"),
        ),
        check_vma=False,
    )
```

profile of v0, /device:TPU:1, one launch (start us, length us, event | category | flops | bytes accessed | tf_op | source)
XLA Modules:
  0.0 624.6 jit_solution(15787198087478532550)
XLA Ops:
  7.2 1.7 copy.114
  12.0 3.4 scatter_custom_fusion.1
  17.5 4.3 mul.196
  21.8 8.3 %mul.197 = f32[768,2048]{1,0:T(8,128)} reshape(f32[128,6,2048]{2,1,0:T(8,128)} %mul.196) | data formatting | bytes 12582912 | tf_op jit(solution)/shard_map/mul | solution.py:183
  30.1 3.3 multiply_convert_fusion
  33.4 3.4 scatter_custom_fusion
  37.1 2.0 copy.180
  39.2 6.0 gather_fusion.1
  45.2 5.1 gather.18
  50.5 2.6 fusion.4
  53.1 3.2 copy-done
  56.3 2.0 fusion.6
  58.4 5.3 all-gather.7.cloned.1.call-done
  63.7 1.5 copy.117
  65.2 5.9 fusion.42
  71.8 5.9 gather_fusion
  77.7 5.0 gather.16
  82.8 5.3 select_select_fusion
  88.1 6.0 copy.129
  94.1 6.8 %all-to-all-start = ((bf16[2,16,30,2048]{3,0,2,1:T(2,128)(2,1)}), bf16[2,16,30,2048]{3,0,2,1:T(2,128)(2,1)}, u32[]{:S(2)}, u32[]{:S(2)}) async-start(bf16[2,16,30,2048]{3,0,2,1:T(2,128)(2,1)} %copy.129), calls=%async_computation | async-start | bytes 7864320 | tf_op jit(solution)/shard_map/all_to_all | solution.py:172
  100.9 8.1 %copy.135 = bf16[2,16,30,2048]{3,0,2,1:T(2,128)(2,1)} copy(bf16[2,16,30,2048]{3,2,1,0:T(8,128)(2,1)} %get-tuple-element.57) | data formatting | bytes 7864320 | tf_op jit(solution)/shard_map/jit(_where)/select_n | solution.py:187
  109.0 50.9 %all-to-all-done = bf16[2,16,30,2048]{3,0,2,1:T(2,128)(2,1)} async-done(((bf16[2,16,30,2048]{3,0,2,1:T(2,128)(2,1)}), bf16[2,16,30,2048]{3,0,2,1:T(2,128)(2,1)}, u32[]{:S(2)}, u32[]{:S(2)}) %all-to-all-start) | async-done | bytes 3932192 | tf_op jit(solution)/shard_map/all_to_all | solution.py:172
  159.9 5.0 all-to-all-start.2
  164.9 8.8 %fusion.22 = f32[2,480,704]{1,2,0:T(8,128)} fusion(bf16[2,2048,704]{1,2,0:T(8,128)(2,1)} %param.19, bf16[2,480,2048]{2,0,1:T(2,128)(2,1)} %bitcast.11), kind=kOutput, calls=%fused_computation.45 | convolution fusion | flops 2768240640 | bytes 12402688 | tf_op jit(solution)/shard_map/erd,edf->erf/dot_general | solution.py:43
  173.6 8.8 %fusion.24 = f32[2,480,704]{1,2,0:T(8,128)} fusion(bf16[2,2048,704]{1,2,0:T(8,128)(2,1)} %param.18, bf16[2,480,2048]{2,0,1:T(2,128)(2,1)} %bitcast.11), kind=kOutput, calls=%fused_computation.47 | convolution fusion | flops 2768240640 | bytes 12402688 | tf_op jit(solution)/shard_map/erd,edf->erf/dot_general | solution.py:40
  182.4 39.0 %all-to-all-done.2 = bf16[2,16,30,2048]{3,0,2,1:T(2,128)(2,1)} async-done(((bf16[2,16,30,2048]{3,0,2,1:T(2,128)(2,1)}), bf16[2,16,30,2048]{3,0,2,1:T(2,128)(2,1)}, u32[]{:S(2)}, u32[]{:S(2)}) %all-to-all-start.2) | async-done | bytes 3932192 | tf_op jit(solution)/shard_map/all_to_all | solution.py:190
  221.5 11.7 %multiply_convert_fusion.1 = (bf16[2,480,704]{1,2,0:T(8,128)(2,1)}, bf16[2,480,704]{1,2,0:T(8,128)(2,1)}, bf16[2,480,704]{1,2,0:T(8,128)(2,1)S(1)}) fusion(f32[2,480,704]{1,2,0:T(8,128)} %fusion.24, f32[2,480,704]{1,2,0:T(8,128)} %fusion.22, bf16[2,704,2048]{2,1,0:T(8,128)(2,1)} %param.20, bf16[2,480,2048]{2,0,1:T(2,128)(2,1)} %bitcast.15), kind=kOutput, calls=%fused_computation.39 | convolution fusion | flops 2779054080 | bytes 19161088 | tf_op jit(solution)/shard_map/erd,efd->erf/dot_general | solution.py:53
  233.2 6.9 %convolution_convert_fusion.3 = bf16[2,480,2048]{2,1,0:T(8,128)(2,1)S(1)} fusion(bf16[2,480,704]{1,2,0:T(8,128)(2,1)S(1)} %get-tuple-element.54, bf16[2,704,2048]{2,1,0:T(8,128)(2,1)} %param.20), kind=kOutput, calls=%fused_computation.33 | convolution fusion | flops 2770206720 | bytes 11051008 | tf_op jit(solution)/shard_map/erf,efd->erd/dot_general | solution.py:45
  240.1 5.9 copy.132
  246.0 4.5 all-to-all-start.1
  250.5 5.9 fusion.66
  256.4 6.5 %add_convert_fusion = bf16[2,480,2048]{2,1,0:T(8,128)(2,1)S(1)} fusion(f32[2,480,2048]{2,1,0:T(8,128)S(1)} %fusion.66, bf16[2,480,704]{1,2,0:T(8,128)(2,1)S(1)} %copy-done.14, bf16[2,2048,704]{1,2,0:T(8,128)(2,1)} %param.19), kind=kOutput, calls=%fused_computation.16 | convolution fusion | flops 2772172800 | bytes 18915328 | tf_op jit(solution)/shard_map/erf,edf->erd/dot_general | solution.py:62
  263.0 5.9 copy.137
  268.9 35.1 %all-to-all-done.1 = bf16[2,16,30,2048]{3,0,2,1:T(2,128)(2,1)} async-done(((bf16[2,16,30,2048]{3,0,2,1:T(2,128)(2,1)}), bf16[2,16,30,2048]{3,0,2,1:T(2,128)(2,1)}, u32[]{:S(2)}, u32[]{:S(2)}) %all-to-all-start.1) | async-done | bytes 3932192 | tf_op jit(solution)/shard_map/all_to_all | solution.py:27
  304.0 4.5 all-to-all-start.3
  311.3 5.9 copy.133
  317.2 5.4 reshape.398
  322.6 35.5 %all-to-all-done.3 = bf16[2,16,30,2048]{3,0,2,1:T(2,128)(2,1)} async-done(((bf16[2,16,30,2048]{3,0,2,1:T(2,128)(2,1)}), bf16[2,16,30,2048]{3,0,2,1:T(2,128)(2,1)}, u32[]{:S(2)}, u32[]{:S(2)}) %all-to-all-start.3) | async-done | bytes 3932192 | tf_op jit(solution)/shard_map/all_to_all | solution.py:27
  358.2 5.9 copy.138
  364.0 5.1 reshape.404
  369.1 9.7 %gather_fusion.2 = bf16[768,2048]{1,0:T(8,128)(2,1)} fusion(bf16[960,2048]{1,0:T(8,128)(2,1)} %reshape.398, s32[1024]{0:T(1024)S(1)} %pad_clamp_fusion.1), kind=kCustom, calls=%fused_computation.clone | custom fusion | bytes 6294528 | tf_op jit(solution)/shard_map/jit(_take)/gather | solution.py:176
  378.8 9.7 %gather_fusion.3 = bf16[768,2048]{1,0:T(8,128)(2,1)} fusion(bf16[960,2048]{1,0:T(8,128)(2,1)} %reshape.404, s32[1024]{0:T(1024)S(1)} %pad_clamp_fusion.1), kind=kCustom, calls=%fused_computation.1.clone | custom fusion | bytes 6294528 | tf_op jit(solution)/shard_map/jit(_take)/gather | solution.py:197
  388.6 7.1 %select_convert_fusion = (f32[768,2048]{1,0:T(8,128)}, bf16[768,2048]{1,0:T(8,128)(2,1)}) fusion(bf16[768,2048]{1,0:T(8,128)(2,1)} %gather_fusion.3, pred[768]{0:T(1024)(128)(4,1)S(1)} %get-tuple-element.48, bf16[768,2048]{1,0:T(8,128)(2,1)} %gather_fusion.2), kind=kLoop, calls=%fused_computation.37 | loop fusion | flops 4718592 | bytes 15729408 | tf_op jit(solution)/shard_map/convert_element_type | solution.py:199
  395.7 8.0 %reshape.411 = f32[128,6,2048]{2,1,0:T(8,128)} reshape(f32[768,2048]{1,0:T(8,128)} %get-tuple-element.60) | data formatting | bytes 12582912 | tf_op jit(solution)/shard_map/convert_element_type | solution.py:199
  403.7 6.0 reduce_sum.81
  410.4 2.3 fusion.33
  412.7 6.3 %bitcast_convert_fusion = bf16[4,128,1024]{2,1,0:T(8,128)(2,1)} fusion(bf16[128,4,4,128]{0,3,2,1:T(8,128)(2,1)S(1)} %get-tuple-element.47, f32[4,1024,128,4]{2,1,3,0:T(8,128)} %copy-done, f32[128,4,4]{0,2,1:T(4,128)S(1)} %log_add_fusion, pred[128,1024]{0,1:T(8,128)(4,1)S(1)} %iota_compare_fusion), kind=kOutput, calls=%fused_computation.49 | convolution fusion | flops 545783808 | bytes 10100736 | tf_op jit(solution)/shard_map/tkgj,tkgd->jkd/dot_general | solution.py:241
  419.0 2.3 copy.150
  421.4 5.2 fusion.1
  426.6 1.5 fusion.26
  428.6 1.3 copy.148
  430.0 8.6 %convolution_convert_fusion.2 = bf16[2,704,2048]{2,1,0:T(8,128)(2,1)} fusion(bf16[2,480,704]{1,2,0:T(8,128)(2,1)} %copy-done.17, bf16[2,480,2048]{2,0,1:T(2,128)(2,1)} %bitcast.15), kind=kOutput, calls=%fused_computation.23 | convolution fusion | flops 2771124224 | bytes 11051008 | tf_op jit(solution)/shard_map/erf,erd->efd/dot_general | solution.py:68
  440.0 9.8 %convolution_convert_fusion = bf16[2,2048,704]{1,2,0:T(8,128)(2,1)} fusion(bf16[2,480,704]{1,2,0:T(8,128)(2,1)S(1)} %copy-done.15, bf16[2,480,2048]{2,0,1:T(2,128)(2,1)} %bitcast.11), kind=kOutput, calls=%fused_computation.21 | convolution fusion | flops 2771124224 | bytes 11051008 | tf_op jit(solution)/shard_map/erd,erf->edf/dot_general | solution.py:67
  449.8 1.3 copy-done.16
  451.1 9.6 %convolution_convert_fusion.1 = bf16[2,2048,704]{1,2,0:T(8,128)(2,1)} fusion(bf16[2,480,704]{1,2,0:T(8,128)(2,1)S(1)} %copy-done.16, bf16[2,480,2048]{2,0,1:T(2,128)(2,1)} %bitcast.11), kind=kOutput, calls=%fused_computation.22 | convolution fusion | flops 2771124224 | bytes 11051008 | tf_op jit(solution)/shard_map/erd,erf->edf/dot_general | solution.py:64
  461.9 1.3 copy.119
  463.2 3.3 fusion.32
  467.6 6.3 %reshape.400 = bf16[128,6,2048]{2,1,0:T(8,128)(2,1)} reshape(bf16[768,2048]{1,0:T(8,128)(2,1)} %get-tuple-element.61) | data formatting | bytes 6291456 | tf_op jit(solution)/shard_map/reshape | solution.py:176
  473.9 5.1 fusion.38
  479.7 5.6 multiply_reduce_fusion
  485.2 1.4 fusion.36
  486.7 42.9 %reduce-scatter.14.cloned.1.call-done = bf16[2,704,256]{2,1,0:T(8,128)(2,1)} async-done(((bf16[2,704,2048]{2,1,0:T(8,128)(2,1)}), bf16[2,704,256]{2,1,0:T(8,128)(2,1)}) %reduce-scatter.14.cloned.1.call-update) | async-done | bytes 720912 | tf_op jit(solution)/shard_map/reduce_scatter | solution.py:213
  529.5 43.7 %reduce-scatter.12.cloned.1.call-done = bf16[2,256,704]{1,2,0:T(8,128)(2,1)} async-done(((bf16[2,2048,704]{1,2,0:T(8,128)(2,1)}), bf16[2,256,704]{1,2,0:T(8,128)(2,1)}) %reduce-scatter.12.cloned.1.call-update) | async-done | bytes 720912 | tf_op jit(solution)/shard_map/reduce_scatter | solution.py:210
  573.2 44.2 %reduce-scatter.10.cloned.1.call-done = bf16[2,256,704]{1,2,0:T(8,128)(2,1)} async-done(((bf16[2,2048,704]{1,2,0:T(8,128)(2,1)}), bf16[2,256,704]{1,2,0:T(8,128)(2,1)}) %reduce-scatter.10.cloned.1.call-update) | async-done | bytes 720912 | tf_op jit(solution)/shard_map/reduce_scatter | solution.py:207
  (95 shorter events, 14.7 us)
Async XLA Ops:
  7.2 43.3 %all-gather.5.cloned.1.call-start = ((), (), s32[]{:S(2)}) async-start(), calls=%async_computation.14 | async-start | bytes 1179648 | tf_op jit(solution)/shard_map/all_gather | solution.py:19
  8.9 54.8 %all-gather.7.cloned.1.call-start = ((), (), s32[]{:S(2)}) async-start(), calls=%async_computation.15 | async-start | bytes 1179648 | tf_op jit(solution)/shard_map/all_gather | solution.py:20
  16.2 5.6 copy-start.12
  45.2 5.3 copy-start.8
  53.1 3.2 copy-start
  65.2 5.9 copy-start.10
  65.2 6.2 copy-start.1
  71.1 6.7 %copy-start.2 = (f32[128,4,4,128]{0,3,2,1:T(8,128)}, f32[128,4,4,128]{0,3,2,1:T(8,128)S(1)}, u32[]{:S(2)}) copy-start(f32[128,4,4,128]{0,3,2,1:T(8,128)S(1)} %fusion.42) | copy-start | bytes 3145732
  94.1 65.8 %all-to-all-start = ((bf16[2,16,30,2048]{3,0,2,1:T(2,128)(2,1)}), bf16[2,16,30,2048]{3,0,2,1:T(2,128)(2,1)}, u32[]{:S(2)}, u32[]{:S(2)}) async-start(bf16[2,16,30,2048]{3,0,2,1:T(2,128)(2,1)} %copy.129), calls=%async_computation | async-start | bytes 7864320 | tf_op jit(solution)/shard_map/all_to_all | solution.py:172
  159.9 61.6 %all-to-all-start.2 = ((bf16[2,16,30,2048]{3,0,2,1:T(2,128)(2,1)}), bf16[2,16,30,2048]{3,0,2,1:T(2,128)(2,1)}, u32[]{:S(2)}, u32[]{:S(2)}) async-start(bf16[2,16,30,2048]{3,0,2,1:T(2,128)(2,1)} %copy.135), calls=%async_computation.2 | async-start | bytes 7864320 | tf_op jit(solution)/shard_map/all_to_all | solution.py:190
  233.2 6.9 %copy-start.17 = (bf16[2,480,704]{1,2,0:T(8,128)(2,1)}, bf16[2,480,704]{1,2,0:T(8,128)(2,1)S(1)}, u32[]{:S(2)}) copy-start(bf16[2,480,704]{1,2,0:T(8,128)(2,1)S(1)} %get-tuple-element.54) | copy-start | bytes 4055044
  246.0 58.0 %all-to-all-start.1 = ((bf16[2,16,30,2048]{3,0,2,1:T(2,128)(2,1)}), bf16[2,16,30,2048]{3,0,2,1:T(2,128)(2,1)}, u32[]{:S(2)}, u32[]{:S(2)}) async-start(bf16[2,16,30,2048]{3,0,2,1:T(2,128)(2,1)} %bitcast.143), calls=%async_computation.1 | async-start | bytes 7864320 | tf_op jit(solution)/shard_map/all_to_all | solution.py:27
  250.5 5.9 copy-start.14
  268.9 40.0 %copy-start.4 = (bf16[1,128,2048]{2,1,0:T(8,128)(2,1)S(1)}, bf16[1,128,2048]{2,1,0:T(8,128)(2,1)}, u32[]{:S(2)}) copy-start(bf16[1,128,2048]{2,1,0:T(8,128)(2,1)} %param.21) | copy-start | bytes 1572868
  304.0 54.2 %all-to-all-start.3 = ((bf16[2,16,30,2048]{3,0,2,1:T(2,128)(2,1)}), bf16[2,16,30,2048]{3,0,2,1:T(2,128)(2,1)}, u32[]{:S(2)}, u32[]{:S(2)}) async-start(bf16[2,16,30,2048]{3,0,2,1:T(2,128)(2,1)} %bitcast.142), calls=%async_computation.3 | async-start | bytes 7864320 | tf_op jit(solution)/shard_map/all_to_all | solution.py:27
  308.5 178.1 %reduce-scatter.8.cloned.1.call-start = ((), (), s32[]{:S(2)}) async-start(), calls=%async_computation.10 | async-start | bytes 1179648 | tf_op jit(solution)/shard_map/reduce_scatter | solution.py:262
  412.7 8.7 %copy-start.11 = (bf16[1,1024,512]{1,2,0:T(8,128)(2,1)S(1)}, bf16[1,1024,512]{1,2,0:T(8,128)(2,1)}, u32[]{:S(2)}) copy-start(bf16[1,1024,512]{1,2,0:T(8,128)(2,1)} %copy-done.10) | copy-start | bytes 3145732
  421.3 65.3 %reduce-scatter.6.cloned.1.call-start = ((), (), s32[]{:S(2)}) async-start(), calls=%async_computation.9 | async-start | bytes 1179648 | tf_op jit(solution)/shard_map/reduce_scatter | solution.py:256
  421.4 5.2 copy-start.9
  426.6 2.0 copy-start.6
  429.9 99.6 %reduce-scatter.14.cloned.1.call-start = ((), (), s32[]{:S(2)}) async-start(), calls=%async_computation.13 | async-start | bytes 6488064 | tf_op jit(solution)/shard_map/reduce_scatter | solution.py:213
  438.6 1.4 copy-start.15
  438.6 134.6 %reduce-scatter.12.cloned.1.call-start = ((), (), s32[]{:S(2)}) async-start(), calls=%async_computation.12 | async-start | bytes 6488064 | tf_op jit(solution)/shard_map/reduce_scatter | solution.py:210
  449.8 1.4 copy-start.16
  449.8 167.7 %reduce-scatter.10.cloned.1.call-start = ((), (), s32[]{:S(2)}) async-start(), calls=%async_computation.11 | async-start | bytes 6488064 | tf_op jit(solution)/shard_map/reduce_scatter | solution.py:207
  460.7 1.2 copy-start.3
  466.6 7.3 %copy-start.5 = (bf16[1,128,2048]{2,1,0:T(8,128)(2,1)S(1)}, bf16[1,128,2048]{2,1,0:T(8,128)(2,1)}, u32[]{:S(2)}) copy-start(bf16[1,128,2048]{2,1,0:T(8,128)(2,1)} %param.21) | copy-start | bytes 1572868
  473.9 5.8 copy-start.13
  479.0 6.3 %copy-start.7 = (f32[1,128,2048]{2,1,0:T(8,128)S(1)}, f32[1,128,2048]{2,1,0:T(8,128)}, u32[]{:S(2)}) copy-start(f32[1,128,2048]{2,1,0:T(8,128)} %copy.119) | copy-start | bytes 3145732
Sparse Core Ops, SparseCore 0:
  10.3 27.1 all-gather.4
  39.2 24.4 all-gather.6
  421.4 30.3 reduce-scatter.7
  454.6 30.8 reduce-scatter.5
  488.3 41.1 reduce-scatter.13
  532.4 40.8 reduce-scatter.11
  576.2 41.2 reduce-scatter.9
where the time goes:
time: 633 us; the launch traced here: 625 us
  waiting for transfers between devices  297 us (47%)
  local copies, waits for them, and re-layouts  149 us (24%)
  matrix products  106 us (17%)
  other arithmetic  35.3 us (6%)
  starting transfers between devices  21.2 us (3%)
  between operations  14.9 us (2%)
    all_to_all x2, waiting for transfers between devices, collect_rows(): lax.all_to_all(results, 'expert', split_axis=1, concat_axis=1, tiled=True)  70.6 us
    all_to_all x1, waiting for transfers between devices, on_device(): lax.all_to_all(outgoing, 'expert', split_axis=1, concat_axis=1, tiled=True)  50.9 us
    reduce_scatter x1, waiting for transfers between devices, on_device(): lax.psum_scatter(gate_sum.astype(jnp.bfloat16), 'seq', scatter_dimension=...  44.2 us
    reduce_scatter x1, waiting for transfers between devices, on_device(): lax.psum_scatter(up_sum.astype(jnp.bfloat16), 'seq', scatter_dimension=1,...  43.7 us
    reduce_scatter x1, waiting for transfers between devices, on_device(): lax.psum_scatter(down_sum.astype(jnp.bfloat16), 'seq', scatter_dimension=...  42.9 us
    all_to_all x1, waiting for transfers between devices, on_device(): lax.all_to_all(outgoing_grad, 'expert', split_axis=1, concat_axis=1, tile...  39 us
  transfers between devices with their start and end apart: 11, of which 8 were waited for; matrix products, arithmetic and copies ran while one was open for 26% of the time, Pallas kernels for 0%

commit v1 on v0

v1 whole, which is shorter than its diff:
```python
import math

import jax
import jax.numpy as jnp
from jax import lax
from jax.experimental import pallas as pl
from jax.experimental.pallas import tpu as pltpu
from jax.sharding import PartitionSpec as P

DH = 128
TOK = 128
WIDTH = 2048
HEADS = 16
KV_HEADS = 4
GROUP = 4
KV_WIDTH = 512
TOP = 6
SEQ = 8
PLANES = 4
RANKS = 16
EXPERTS = 32
SLOTS = 32
ROWS = EXPERTS * SLOTS
HIDDEN = 704
FULL = TOK * SEQ
SCALE = 1.0 / math.sqrt(DH)
NEG_BIG = -1e30
NORM_EPS = 1e-06
VMEM_BYTES = 56 * 1024 * 1024

bf16 = jnp.bfloat16
f32 = jnp.float32

PLANE_GROUPS = [
    [(2 * z + core) * RANKS + rank for core in range(2) for rank in range(RANKS)]
    for z in range(PLANES)
]
Z_GROUPS = [[2 * z + core for z in range(PLANES)] for core in range(2)]


def params(**kw):
    return pltpu.CompilerParams(vmem_limit_bytes=VMEM_BYTES, **kw)


def whole(shape):
    return pl.BlockSpec(shape, lambda *_: (0,) * len(shape))


def dot_nn(a, b):
    return lax.dot_general(a, b, (((1,), (0,)), ((), ())), preferred_element_type=f32)


def dot_nt(a, b):
    return lax.dot_general(a, b, (((1,), (1,)), ((), ())), preferred_element_type=f32)


def dot_tn(a, b):
    return lax.dot_general(a, b, (((0,), (0,)), ((), ())), preferred_element_type=f32)


def expert_ids():
    row = lax.broadcasted_iota(jnp.int32, (EXPERTS, TOK), 0)
    return 2 * (row & (RANKS - 1)) + (row >> 4)


def plan_kernel(routes, mix, grad, pick_out, mixed_out, rows_out):
    ids = expert_ids()
    member = jnp.zeros((EXPERTS, TOK), f32)
    weight = jnp.zeros((EXPERTS, TOK), f32)
    for c in range(TOP):
        hit = routes[c : c + 1, :] == ids
        member = member + jnp.where(hit, 1.0, 0.0)
        weight = weight + jnp.where(hit, mix[c : c + 1, :], 0.0)
    before = lax.broadcasted_iota(jnp.int32, (TOK, TOK), 0) < lax.broadcasted_iota(
        jnp.int32, (TOK, TOK), 1
    )
    rank = dot_nn(member.astype(bf16), jnp.where(before, 1.0, 0.0).astype(bf16))
    slot = jnp.where(member > 0.0, rank, -1.0)
    place = lax.broadcasted_iota(jnp.int32, (EXPERTS, SLOTS, TOK), 1).astype(f32)
    pick = jnp.where(slot[:, None, :] == place, 1.0, 0.0)
    mixed = (pick * weight[:, None, :]).reshape(ROWS, TOK)
    pick = pick.reshape(ROWS, TOK)
    pick_out[...] = pick.astype(bf16)
    mixed_out[...] = mixed
    step = 256
    for i in range(0, ROWS, step):
        rows = dot_nn(pick[i : i + step].astype(bf16), grad[...])
        scale = jnp.sum(mixed[i : i + step], axis=1, keepdims=True)
        rows_out[i : i + step, :] = (rows * scale).astype(bf16)


def make_plan(routes, mix, grad):
    return pl.pallas_call(
        plan_kernel,
        out_shape=(
            jax.ShapeDtypeStruct((ROWS, TOK), bf16),
            jax.ShapeDtypeStruct((ROWS, TOK), f32),
            jax.ShapeDtypeStruct((ROWS, WIDTH), bf16),
        ),
        compiler_params=params(),
        cost_estimate=pl.CostEstimate(
            flops=2 * ROWS * TOK * WIDTH, bytes_accessed=8 << 20, transcendentals=0
        ),
    )(routes, mix, grad)


def visible_keys(seq_ref):
    row = seq_ref[0] * TOK + lax.broadcasted_iota(jnp.int32, (TOK, FULL), 0)
    return lax.broadcasted_iota(jnp.int32, (TOK, FULL), 1) <= row


def norm_parts(residual, attention):
    hidden = residual.astype(f32) + attention.astype(f32)
    inv_rms = lax.rsqrt(jnp.mean(hidden * hidden, axis=1, keepdims=True) + NORM_EPS)
    return hidden, inv_rms


def attend_kernel(seq_ref, q_ref, k_ref, v_ref, residual, pick, att_out, lse_out, rows_out):
    head = pl.program_id(0)
    keys, values = k_ref[...], v_ref[...]
    visible = visible_keys(seq_ref)
    outs, totals = [], []
    for g in range(GROUP):
        scores = dot_nt(q_ref[:, g * DH : (g + 1) * DH], keys) * SCALE
        masked = jnp.where(visible, scores, NEG_BIG)
        row_max = jnp.max(masked, axis=1, keepdims=True)
        weights = jnp.exp(masked - row_max)
        row_sum = jnp.sum(weights, axis=1, keepdims=True)
        mixed = dot_nn(weights.astype(bf16), values)
        outs.append((mixed / row_sum).astype(bf16))
        totals.append(jnp.broadcast_to(row_max + jnp.log(row_sum), (TOK, DH)))
    columns = pl.ds(pl.multiple_of(head * GROUP * DH, GROUP * DH), GROUP * DH)
    att_out[:, columns] = jnp.concatenate(outs, axis=1)
    lse_out[...] = jnp.concatenate(totals, axis=1)

    @pl.when(head == KV_HEADS - 1)
    def _():
        hidden, inv_rms = norm_parts(residual[...], att_out[...])
        normed = (hidden * inv_rms).astype(bf16)
        for i in range(0, ROWS, 256):
            rows_out[i : i + 256, :] = dot_nn(pick[i : i + 256, :], normed).astype(bf16)


def attend(seq_index, queries, pairs, residual, pick):
    return pl.pallas_call(
        attend_kernel,
        grid_spec=pltpu.PrefetchScalarGridSpec(
            num_scalar_prefetch=1,
            grid=(KV_HEADS,),
            in_specs=[
                pl.BlockSpec((TOK, GROUP * DH), lambda h, s: (0, h)),
                pl.BlockSpec((FULL, DH), lambda h, s: (0, h)),
                pl.BlockSpec((FULL, DH), lambda h, s: (0, KV_HEADS + h)),
                whole((TOK, WIDTH)),
                whole((ROWS, TOK)),
            ],
            out_specs=[
                whole((TOK, WIDTH)),
                pl.BlockSpec((TOK, GROUP * DH), lambda h, s: (0, h)),
                whole((ROWS, WIDTH)),
            ],
        ),
        out_shape=(
            jax.ShapeDtypeStruct((TOK, WIDTH), bf16),
            jax.ShapeDtypeStruct((TOK, WIDTH), f32),
            jax.ShapeDtypeStruct((ROWS, WIDTH), bf16),
        ),
        compiler_params=params(),
        cost_estimate=pl.CostEstimate(
            flops=4 * TOK * FULL * WIDTH + 2 * ROWS * TOK * WIDTH,
            bytes_accessed=10 << 20,
            transcendentals=HEADS * TOK * FULL,
        ),
    )(seq_index, queries, pairs, pairs, residual, pick)


def expert_kernel(core, rows, pairs, gate_w, up_w, down_w, back_out, act_out, gate_out, up_out):
    gate = dot_nt(rows[...], gate_w[0])
    up = dot_nt(rows[...], up_w[0])
    sig = jax.nn.sigmoid(gate)
    silu = gate * sig
    act_out[...] = (silu * up).astype(bf16)
    act_grad = dot_nt(pairs[...], down_w[0])
    gate_grad = (act_grad * up * sig * (1.0 + gate * (1.0 - sig))).astype(bf16)
    up_grad = (act_grad * silu).astype(bf16)
    gate_out[...] = gate_grad
    up_out[...] = up_grad
    back_out[...] = (dot_nn(gate_grad, gate_w[0]) + dot_nn(up_grad, up_w[0])).astype(bf16)


def expert_rows(core, rows, pairs, gate_w, up_w, down_w):
    step = 256
    tile = pl.BlockSpec((step, WIDTH), lambda i, c: (i, 0))
    thin = pl.BlockSpec((step, HIDDEN), lambda i, c: (i, 0))
    weight = pl.BlockSpec((1, HIDDEN, WIDTH), lambda i, c: (c[0], 0, 0))
    return pl.pallas_call(
        expert_kernel,
        grid_spec=pltpu.PrefetchScalarGridSpec(
            num_scalar_prefetch=1,
            grid=(ROWS // step,),
            in_specs=[tile, tile, weight, weight, weight],
            out_specs=[tile, thin, thin, thin],
        ),
        out_shape=(
            jax.ShapeDtypeStruct((ROWS, WIDTH), bf16),
            jax.ShapeDtypeStruct((ROWS, HIDDEN), bf16),
            jax.ShapeDtypeStruct((ROWS, HIDDEN), bf16),
            jax.ShapeDtypeStruct((ROWS, HIDDEN), bf16),
        ),
        compiler_params=params(),
        cost_estimate=pl.CostEstimate(
            flops=10 * ROWS * HIDDEN * WIDTH,
            bytes_accessed=24 << 20,
            transcendentals=ROWS * HIDDEN,
        ),
    )(core, rows, pairs, gate_w, up_w, down_w)


def sums_kernel(rows, pairs, act, gate, up, gate_out, up_out, down_out):
    gate_out[0] = dot_tn(gate[...], rows[...]).astype(bf16)
    up_out[0] = dot_tn(up[...], rows[...]).astype(bf16)
    down_out[0] = dot_tn(act[...], pairs[...]).astype(bf16)


def weight_sums(rows, pairs, act, gate, up):
    part = WIDTH // PLANES
    columns = pl.BlockSpec((ROWS, part), lambda i: (0, i))
    thin = whole((ROWS, HIDDEN))
    out = pl.BlockSpec((1, HIDDEN, part), lambda i: (i, 0, 0))
    shape = jax.ShapeDtypeStruct((PLANES, HIDDEN, part), bf16)
    return pl.pallas_call(
        sums_kernel,
        grid=(PLANES,),
        in_specs=[columns, columns, thin, thin, thin],
        out_specs=[out, out, out],
        out_shape=(shape, shape, shape),
        compiler_params=params(),
        cost_estimate=pl.CostEstimate(
            flops=6 * ROWS * HIDDEN * WIDTH, bytes_accessed=22 << 20, transcendentals=0
        ),
    )(rows, pairs, act, gate, up)


def result_kernel(core, act, down_w, out):
    out[...] = dot_nn(act[...], down_w[0]).astype(bf16)


def expert_results(core, act, down_w):
    step = 256
    return pl.pallas_call(
        result_kernel,
        grid_spec=pltpu.PrefetchScalarGridSpec(
            num_scalar_prefetch=1,
            grid=(ROWS // step,),
            in_specs=[
                pl.BlockSpec((step, HIDDEN), lambda i, c: (i, 0)),
                pl.BlockSpec((1, HIDDEN, WIDTH), lambda i, c: (c[0], 0, 0)),
            ],
            out_specs=pl.BlockSpec((step, WIDTH), lambda i, c: (i, 0)),
        ),
        out_shape=jax.ShapeDtypeStruct((ROWS, WIDTH), bf16),
        compiler_params=params(),
        cost_estimate=pl.CostEstimate(
            flops=2 * ROWS * HIDDEN * WIDTH, bytes_accessed=9 << 20, transcendentals=0
        ),
    )(core, act, down_w)


def attend_back_kernel(
    seq_ref, q_ref, k_ref, v_ref, lse, back, pick, residual, att, grad, res_out, q_out, kv_out
):
    head = pl.program_id(0)

    @pl.when(head == 0)
    def _():
        normed_grad = dot_tn(pick[...], back[...])
        hidden, inv_rms = norm_parts(residual[...], att[...])
        normed = hidden * inv_rms
        dot_mean = jnp.mean(normed_grad * normed, axis=1, keepdims=True)
        total = grad[...].astype(f32) + inv_rms * (normed_grad - normed * dot_mean)
        res_out[...] = total.astype(bf16)

    keys, values = k_ref[...], v_ref[...]
    visible = visible_keys(seq_ref)
    score_parts, prob_parts, query_parts, grad_parts = [], [], [], []
    for g in range(GROUP):
        query = q_ref[:, g * DH : (g + 1) * DH]
        columns = pl.ds(pl.multiple_of(head * GROUP * DH + g * DH, DH), DH)
        out_grad = res_out[:, columns]
        delta = jnp.sum(
            out_grad.astype(f32) * att[:, columns].astype(f32), axis=1, keepdims=True
        )
        scores = dot_nt(query, keys) * SCALE
        total = lse[:, g * DH : g * DH + 1]
        probs = jnp.exp(jnp.where(visible, scores - total, NEG_BIG))
        prob_grad = dot_nt(out_grad, values)
        score_grad = (probs * (prob_grad - delta)).astype(bf16)
        q_out[:, g * DH : (g + 1) * DH] = (dot_nn(score_grad, keys) * SCALE).astype(bf16)
        score_parts.append(score_grad)
        prob_parts.append(probs.astype(bf16))
        query_parts.append(query)
        grad_parts.append(out_grad)
    key_sum = dot_tn(jnp.concatenate(score_parts, axis=0), jnp.concatenate(query_parts, axis=0))
    value_sum = dot_tn(jnp.concatenate(prob_parts, axis=0), jnp.concatenate(grad_parts, axis=0))
    kv_out[:, pl.ds(pl.multiple_of(head * DH, DH), DH)] = (key_sum * SCALE).astype(bf16)
    kv_out[:, pl.ds(pl.multiple_of(KV_WIDTH + head * DH, DH), DH)] = value_sum.astype(bf16)


def attend_back(seq_index, queries, pairs, lse, back, pick, residual, att, grad):
    return pl.pallas_call(
        attend_back_kernel,
        grid_spec=pltpu.PrefetchScalarGridSpec(
            num_scalar_prefetch=1,
            grid=(KV_HEADS,),
            in_specs=[
                pl.BlockSpec((TOK, GROUP * DH), lambda h, s: (0, h)),
                pl.BlockSpec((FULL, DH), lambda h, s: (0, h)),
                pl.BlockSpec((FULL, DH), lambda h, s: (0, KV_HEADS + h)),
                pl.BlockSpec((TOK, GROUP * DH), lambda h, s: (0, h)),
                whole((ROWS, WIDTH)),
                whole((ROWS, TOK)),
                whole((TOK, WIDTH)),
                whole((TOK, WIDTH)),
                whole((TOK, WIDTH)),
            ],
            out_specs=[
                whole((TOK, WIDTH)),
                pl.BlockSpec((TOK, GROUP * DH), lambda h, s: (0, h)),
                whole((FULL, 2 * KV_WIDTH)),
            ],
        ),
        out_shape=(
            jax.ShapeDtypeStruct((TOK, WIDTH), bf16),
            jax.ShapeDtypeStruct((TOK, WIDTH), bf16),
            jax.ShapeDtypeStruct((FULL, 2 * KV_WIDTH), bf16),
        ),
        compiler_params=params(),
        cost_estimate=pl.CostEstimate(
            flops=10 * TOK * FULL * WIDTH + 2 * ROWS * TOK * WIDTH,
            bytes_accessed=12 << 20,
            transcendentals=HEADS * TOK * FULL,
        ),
    )(seq_index, queries, pairs, pairs, lse, back, pick, residual, att, grad)


def combine_kernel(routes, pick, mixed, returned, residual, att, grad, layer_out, mix_out):
    hidden = residual[...].astype(f32) + att[...].astype(f32)
    coarse = mixed[...].astype(bf16)
    fine = (mixed[...] - coarse.astype(f32)).astype(bf16)
    total = hidden + dot_tn(coarse, returned[...]) + dot_tn(fine, returned[...])
    layer_out[...] = total.astype(bf16)
    sums = []
    for i in range(0, ROWS, 256):
        rows = dot_nn(pick[i : i + 256, :], grad[...])
        inner = jnp.sum(rows * returned[i : i + 256, :].astype(f32), axis=1, keepdims=True)
        spread = pick[i : i + 256, :].astype(f32) * inner
        sums.append(jnp.sum(spread.reshape(256 // SLOTS, SLOTS, TOK), axis=1))
    by_expert = jnp.concatenate(sums, axis=0)
    ids = expert_ids()
    for c in range(TOP):
        hit = routes[c : c + 1, :] == ids
        mix_out[c : c + 1, :] = jnp.sum(jnp.where(hit, by_expert, 0.0), axis=0, keepdims=True)


def combine(routes, pick, mixed, returned, residual, att, grad):
    return pl.pallas_call(
        combine_kernel,
        out_shape=(
            jax.ShapeDtypeStruct((TOK, WIDTH), bf16),
            jax.ShapeDtypeStruct((TOP, TOK), f32),
        ),
        compiler_params=params(),
        cost_estimate=pl.CostEstimate(
            flops=6 * ROWS * TOK * WIDTH, bytes_accessed=8 << 20, transcendentals=0
        ),
    )(routes, pick, mixed, returned, residual, att, grad)


def exchange(rows):
    blocks = rows.reshape(EXPERTS, SLOTS, WIDTH)
    moved = lax.all_to_all(
        blocks, ("seq", "expert"), 0, 0, tiled=True, axis_index_groups=PLANE_GROUPS
    )
    return moved.reshape(ROWS, WIDTH)


def swap_cores(values):
    return lax.ppermute(values, "seq", [(i, i ^ 1) for i in range(SEQ)])


def on_device(
    residual,
    queries,
    key_input,
    value_input,
    routes,
    mix_weights,
    gate_weight,
    up_weight,
    down_weight,
    grad_out,
):
    seq = lax.axis_index("seq")
    seq_index = seq.astype(jnp.int32).reshape(1)
    core = (seq & 1).astype(jnp.int32)
    core_index = core.reshape(1)
    residual = residual.reshape(TOK, WIDTH)
    queries = queries.reshape(TOK, WIDTH)
    grad = grad_out.reshape(TOK, WIDTH)
    routes = routes.reshape(TOK, TOP).T
    mix = mix_weights.reshape(TOK, TOP).T
    gate_w = jnp.swapaxes(gate_weight, 1, 2)
    up_w = jnp.swapaxes(up_weight, 1, 2)
    pairs = jnp.concatenate(
        [key_input.reshape(TOK, KV_WIDTH), value_input.reshape(TOK, KV_WIDTH)], axis=1
    )
    pairs = lax.all_gather(pairs, "seq", axis=0, tiled=True)
    pick, mixed, grad_rows = make_plan(routes, mix, grad)
    grad_rows = exchange(grad_rows)
    att, lse, rows = attend(seq_index, queries, pairs, residual, pick)
    rows = exchange(rows)
    back, act, gate_grad, up_grad = expert_rows(
        core_index, rows, grad_rows, gate_w, up_w, down_weight
    )
    back = exchange(back)
    sums = weight_sums(rows, grad_rows, act, gate_grad, up_grad)
    results = expert_results(core_index, act, down_weight)
    res_grad, query_grad, kv_parts = attend_back(
        seq_index, queries, pairs, lse, back, pick, residual, att, grad
    )
    kv_parts = lax.all_to_all(kv_parts.reshape(SEQ, TOK, 2 * KV_WIDTH), "seq", 0, 0, tiled=True)
    kv_grad = jnp.sum(kv_parts.astype(f32), axis=0).astype(bf16)
    results = exchange(results)
    layer_out, mix_grad = combine(routes, pick, mixed, results, residual, att, grad)
    shares = [
        lax.psum_scatter(s, "seq", scatter_dimension=0, axis_index_groups=Z_GROUPS) for s in sums
    ]
    weight_grads = []
    for share in shares:
        low, high = share[:, :256], share[:, 256:]
        mine = jnp.where(core == 0, low, high)
        other = swap_cores(jnp.where(core == 0, high, low))
        weight_grads.append(
            jnp.stack([jnp.where(core == 0, mine, other), jnp.where(core == 0, other, mine)])
        )
    return (
        layer_out.reshape(1, TOK, WIDTH),
        res_grad.reshape(1, TOK, WIDTH),
        query_grad.reshape(1, TOK, WIDTH),
        kv_grad[:, :KV_WIDTH].reshape(1, TOK, KV_WIDTH),
        kv_grad[:, KV_WIDTH:].reshape(1, TOK, KV_WIDTH),
        mix_grad.T.reshape(1, TOK, TOP),
        jnp.swapaxes(weight_grads[0], 1, 2),
        jnp.swapaxes(weight_grads[1], 1, 2),
        weight_grads[2],
    )


def solution(mesh):
    rows = P("expert", "seq", None)
    weights = P("expert", None, None)
    return jax.shard_map(
        on_device,
        mesh=mesh,
        in_specs=(rows, rows, rows, rows, rows, rows, weights, weights, weights, rows),
        out_specs=(rows, rows, rows, rows, rows, rows, rows, rows, P("expert", None, "seq")),
        check_vma=False,
    )
```

time: 633 us -> 348 us (0.55); the launches traced: 625 us -> 347 us
  local copies, waits for them, and re-layouts: 149 us -> 5.59 us
  matrix products: 106 us -> 0 us
  waiting for transfers between devices: 297 us -> 200 us
  Pallas kernels: 0 us -> 83.3 us
  other arithmetic: 35.3 us -> 13.5 us
  starting transfers between devices: 21.2 us -> 30.6 us
    reduce_scatter x5 -> x3, waiting for transfers between devices: 131 us -> 0.01 us  [on_device(): lax.psum_scatter(s, 'seq', scatter_dimension=0, axis_index_groups=Z_GROUPS)]
    dot_general x16 -> x0, matrix products: 106 us -> none  [the longest x1 11.7 us: dense_backward(): jnp.einsum('erd,efd->erf', grad_rows, down_weight, preferred_element_type...]
    pallas_call x0 -> x7, Pallas kernels: none -> 83.3 us  [the longest x1 25.7 us: expert_rows(): pl.pallas_call(expert_kernel, grid_spec=pltpu.PrefetchScalarGridSpec(num_...]
    gather x6 -> x0, local copies, waits for them, and re-layouts: 41.6 us -> none  [the longest x2 11.2 us: on_device(): jnp.take(pair_grad, slot_pair, axis=0)]
    convert_element_type x9 -> x0, local copies, waits for them, and re-layouts: 27.5 us -> none  [the longest x1 8 us: on_device(): normed_grad = jnp.sum(jnp.take(input_back, slot_index, axis=0).reshape(to...]
    all_gather x2 -> x1, waiting for transfers between devices: 5.32 us -> 30.1 us  [on_device(): pairs = lax.all_gather(pairs, 'seq', axis=0, tiled=True)]
    reshape x7 -> x1, local copies, waits for them, and re-layouts: 19.7 us -> 1.75 us  [on_device(): kv_grad[:, KV_WIDTH:].reshape(1, TOK, KV_WIDTH)]
    select_n x2 -> x0, local copies, waits for them, and re-layouts: 14.1 us -> none  [the longest x1 8.14 us: on_device(): jnp.where(slot_live[:, None], jnp.take(pair_grad, slot_pair, axis=0), zer...]
  transfers between devices with their start and end apart: 11 -> 12, of which waited for: 8 -> 6; matrix products, arithmetic and copies ran while one was open for 26% -> 4% of each run, Pallas kernels for 0% -> 11%
where the time goes in v1:
time: 348 us; the launch traced here: 347 us
  waiting for transfers between devices  200 us (57%)
  Pallas kernels  83.3 us (24%)
  starting transfers between devices  30.6 us (9%)
  between operations  13.9 us (4%)
  other arithmetic  13.5 us (4%)
  local copies, waits for them, and re-layouts  5.59 us (2%)
    all_to_all x4, waiting for transfers between devices, exchange(): lax.all_to_all(blocks, ('seq', 'expert'), 0, 0, tiled=True, axis_index_gr...  156 us
    all_gather x1, waiting for transfers between devices, on_device(): pairs = lax.all_gather(pairs, 'seq', axis=0, tiled=True)  30.1 us
    pallas_call x1, Pallas kernels, expert_rows(): pl.pallas_call(expert_kernel, grid_spec=pltpu.PrefetchScalarGridSpec(num_...  25.7 us
    all_to_all x4, starting transfers between devices, exchange(): lax.all_to_all(blocks, ('seq', 'expert'), 0, 0, tiled=True, axis_index_gr...  24.2 us
    pallas_call x1, Pallas kernels, attend_back(): pl.pallas_call(attend_back_kernel, grid_spec=pltpu.PrefetchScalarGridSpec...  14.4 us
    pallas_call x1, Pallas kernels, weight_sums(): pl.pallas_call(sums_kernel, grid=(PLANES,), in_specs=[columns, columns, t...  13.7 us
    all_to_all x1, waiting for transfers between devices, on_device(): lax.all_to_all(kv_parts.reshape(SEQ, TOK, 2 * KV_WIDTH), 'seq', 0, 0, til...  12.9 us
    pallas_call x1, Pallas kernels, attend(): pl.pallas_call(attend_kernel, grid_spec=pltpu.PrefetchScalarGridSpec(num_...  11.7 us
  transfers between devices with their start and end apart: 12, of which 6 were waited for; matrix products, arithmetic and copies ran while one was open for 4% of the time, Pallas kernels for 11%

profile of v1, /device:TPU:1, one launch (start us, length us, event | category | flops | bytes accessed | tf_op | source)
XLA Modules:
  0.0 346.8 jit_solution(11195966009128028279)
XLA Ops:
  7.2 1.3 copy.25
  8.5 1.3 copy.24
  9.7 4.5 %shard_map.169 = (bf16[1024,128]{1,0:T(8,128)(2,1)}, f32[1024,128]{1,0:T(8,128)}, bf16[1024,2048]{1,0:T(8,128)(2,1)}) custom-call(s32[6,128]{1,0:T(8,128)} %bitcast.76, f32[6,128]{1,0:T(8,128)} %bitcast.79, bf16[128,2048]{1,0:T(8,128)(2,1)} %bitcast.68), custom_call_target="tpu_custom_call" | custom-call | flops 536870912 | bytes 8388608 | tf_op jit(solution)/shard_map/pallas_call | solution.py:93
  14.3 0.0 copy-start.3
  14.3 0.0 copy-start.4
  14.3 8.8 %all-to-all-start.1 = ((bf16[32,32,2048]{2,1,0:T(8,128)(2,1)}), bf16[32,32,2048]{2,1,0:T(8,128)(2,1)}, u32[]{:S(2)}, u32[]{:S(2)}) async-start(bf16[32,32,2048]{2,1,0:T(8,128)(2,1)} %bitcast.59), calls=%async_computation.1 | async-start | bytes 8388608 | tf_op jit(solution)/shard_map/all_to_all | solution.py:381
  23.0 0.0 all-gather.2.cloned.1.call-start
  23.1 0.0 copy-done.3
  23.1 0.0 copy-done.4
  23.1 0.7 pad_maximum_fusion.1
  23.8 0.0 all-gather.2.cloned.1.call-update
  23.9 30.1 %all-gather.2.cloned.1.call-done.k_ref.v_ref = bf16[1024,1024]{1,0:T(8,128)(2,1)} async-done(((bf16[128,1024]{1,0:T(8,128)(2,1)}), bf16[1024,1024]{1,0:T(8,128)(2,1)}) %all-gather.2.cloned.1.call-update) | async-done | bytes 2097168 | tf_op jit(solution)/shard_map/all_gather | solution.py:417
  54.0 11.7 %shard_map.170 = (bf16[128,2048]{1,0:T(8,128)(2,1)}, f32[128,2048]{1,0:T(8,128)}, bf16[1024,2048]{1,0:T(8,128)(2,1)}) custom-call(s32[1]{0:T(128)} %bitcast.4.seq_ref, bf16[128,2048]{1,0:T(8,128)(2,1)} %bitcast.82, bf16[1024,1024]{1,0:T(8,128)(2,1)} %all-gather.2.cloned.1.call-done.k_ref.v_ref, bf16[1024,1024]{1,0:T(8,128)(2,1)} %all-gather.2.cloned.1.call-done.k_ref.v_ref, ...), custom_call_target="tpu_custom_call" | custom-call | flops 1610612736 | bytes 10485760 | tf_op jit(solution)/shard_map/pallas_call | solution.py:145
  65.7 12.6 %all-to-all-done.1 = bf16[32,32,2048]{2,1,0:T(8,128)(2,1)} async-done(((bf16[32,32,2048]{2,1,0:T(8,128)(2,1)}), bf16[32,32,2048]{2,1,0:T(8,128)(2,1)}, u32[]{:S(2)}, u32[]{:S(2)}) %all-to-all-start.1) | async-done | bytes 4194336 | tf_op jit(solution)/shard_map/all_to_all | solution.py:381
  78.3 5.1 %all-to-all-start = ((bf16[32,32,2048]{2,1,0:T(8,128)(2,1)}), bf16[32,32,2048]{2,1,0:T(8,128)(2,1)}, u32[]{:S(2)}, u32[]{:S(2)}) async-start(bf16[32,32,2048]{2,1,0:T(8,128)(2,1)} %bitcast.60), calls=%async_computation | async-start | bytes 8388608 | tf_op jit(solution)/shard_map/all_to_all | solution.py:381
  83.4 0.0 reduce-scatter.4.cloned.1.call-start
  83.5 55.2 %all-to-all-done = bf16[32,32,2048]{2,1,0:T(8,128)(2,1)} async-done(((bf16[32,32,2048]{2,1,0:T(8,128)(2,1)}), bf16[32,32,2048]{2,1,0:T(8,128)(2,1)}, u32[]{:S(2)}, u32[]{:S(2)}) %all-to-all-start) | async-done | bytes 4194336 | tf_op jit(solution)/shard_map/all_to_all | solution.py:381
  138.7 25.7 %shard_map.171 = (bf16[1024,2048]{1,0:T(8,128)(2,1)}, bf16[1024,704]{1,0:T(8,128)(2,1)}, bf16[1024,704]{1,0:T(8,128)(2,1)}, bf16[1024,704]{1,0:T(8,128)(2,1)}) custom-call(s32[1]{0:T(128)} %bitcast.3.core, bf16[1024,2048]{1,0:T(8,128)(2,1)} %bitcast.10.rows, bf16[1024,2048]{1,0:T(8,128)(2,1)} %bitcast.12.pairs, bf16[2,704,2048]{2,1,0:T(8,128)(2,1)} %bitcast.80, ...), custom_call_target="tpu_custom_call" | custom-call | flops 14763950080 | bytes 25165824 | tf_op jit(solution)/shard_map/pallas_call | solution.py:196
  164.3 13.7 %shard_map.175 = (bf16[4,704,512]{2,1,0:T(8,128)(2,1)}, bf16[4,704,512]{2,1,0:T(8,128)(2,1)}, bf16[4,704,512]{2,1,0:T(8,128)(2,1)}) custom-call(bf16[1024,2048]{1,0:T(8,128)(2,1)} %bitcast.10.rows, bf16[1024,2048]{1,0:T(8,128)(2,1)} %bitcast.12.pairs, bf16[1024,704]{1,0:T(8,128)(2,1)} %get-tuple-element.31.act, bf16[1024,704]{1,0:T(8,128)(2,1)} %get-tuple-element.40.gate, ...), custom_call_target="tpu_custom_call" | custom-call | flops 8858370048 | bytes 23068672 | tf_op jit(solution)/shard_map/pallas_call | solution.py:231
  178.0 0.0 reduce-scatter.4.cloned.1.call-update
  178.1 0.0 reduce-scatter.6.cloned.1.call-start
  178.1 0.7 reduce-scatter.6.cloned.1.call-update
  178.8 5.1 %all-to-all-start.3 = ((bf16[32,32,2048]{2,1,0:T(8,128)(2,1)}), bf16[32,32,2048]{2,1,0:T(8,128)(2,1)}, u32[]{:S(2)}, u32[]{:S(2)}) async-start(bf16[32,32,2048]{2,1,0:T(8,128)(2,1)} %bitcast.58), calls=%async_computation.3 | async-start | bytes 8388608 | tf_op jit(solution)/shard_map/all_to_all | solution.py:381
  184.0 0.2 reduce-scatter.8.cloned.1.call-start
  184.2 0.3 reduce-scatter.8.cloned.1.call-update
  184.5 7.3 %shard_map.172 = bf16[1024,2048]{1,0:T(8,128)(2,1)} custom-call(s32[1]{0:T(128)} %bitcast.3.core, bf16[1024,704]{1,0:T(8,128)(2,1)} %get-tuple-element.31.act, bf16[2,704,2048]{2,1,0:T(8,128)(2,1)} %down_w.3), custom_call_target="tpu_custom_call" | custom-call | flops 2952790016 | bytes 9437184 | tf_op jit(solution)/shard_map/pallas_call | solution.py:250
  191.9 47.3 %all-to-all-done.3 = bf16[32,32,2048]{2,1,0:T(8,128)(2,1)} async-done(((bf16[32,32,2048]{2,1,0:T(8,128)(2,1)}), bf16[32,32,2048]{2,1,0:T(8,128)(2,1)}, u32[]{:S(2)}, u32[]{:S(2)}) %all-to-all-start.3) | async-done | bytes 4194336 | tf_op jit(solution)/shard_map/all_to_all | solution.py:381
  239.2 5.1 %all-to-all-start.2 = ((bf16[32,32,2048]{2,1,0:T(8,128)(2,1)}), bf16[32,32,2048]{2,1,0:T(8,128)(2,1)}, u32[]{:S(2)}, u32[]{:S(2)}) async-start(bf16[32,32,2048]{2,1,0:T(8,128)(2,1)} %bitcast.57), calls=%async_computation.2 | async-start | bytes 8388608 | tf_op jit(solution)/shard_map/all_to_all | solution.py:381
  244.3 14.4 %shard_map.174 = (bf16[128,2048]{1,0:T(8,128)(2,1)}, bf16[128,2048]{1,0:T(8,128)(2,1)}, bf16[1024,1024]{1,0:T(8,128)(2,1)}) custom-call(s32[1]{0:T(128)} %bitcast.4.seq_ref, bf16[128,2048]{1,0:T(8,128)(2,1)} %bitcast.83, bf16[1024,1024]{1,0:T(8,128)(2,1)} %all-gather.2.cloned.1.call-done.k_ref.v_ref, ...), custom_call_target="tpu_custom_call" | custom-call | flops 3221225472 | bytes 12582912 | tf_op jit(solution)/shard_map/pallas_call | solution.py:310
  258.7 40.8 %all-to-all-done.2 = bf16[32,32,2048]{2,1,0:T(8,128)(2,1)} async-done(((bf16[32,32,2048]{2,1,0:T(8,128)(2,1)}), bf16[32,32,2048]{2,1,0:T(8,128)(2,1)}, u32[]{:S(2)}, u32[]{:S(2)}) %all-to-all-start.2) | async-done | bytes 4194336 | tf_op jit(solution)/shard_map/all_to_all | solution.py:381
  299.6 5.6 %all-to-all-start.4 = ((bf16[8,128,1024]{2,1,0:T(8,128)(2,1)}), bf16[8,128,1024]{2,1,0:T(8,128)(2,1)S(1)}, u32[]{:S(2)}, u32[]{:S(2)}) async-start(bf16[8,128,1024]{2,1,0:T(8,128)(2,1)} %bitcast.67), calls=%async_computation.4 | async-start | bytes 4194304 | tf_op jit(solution)/shard_map/all_to_all | solution.py:431
  305.2 5.9 %shard_map.173 = (bf16[128,2048]{1,0:T(8,128)(2,1)}, f32[6,128]{1,0:T(8,128)}) custom-call(s32[6,128]{1,0:T(8,128)} %bitcast.77, bf16[1024,128]{1,0:T(8,128)(2,1)} %get-tuple-element.27.pick, f32[1024,128]{1,0:T(8,128)} %get-tuple-element.28.mixed, bf16[1024,2048]{1,0:T(8,128)(2,1)} %bitcast.16.returned, bf16[128,2048]{1,0:T(8,128)(2,1)} %bitcast.73, ...), custom_call_target="tpu_custom_call" | custom-call | flops 1610612736 | bytes 8388608 | tf_op jit(solution)/shard_map/pallas_call | solution.py:366
  311.1 1.3 copy.19
  312.4 0.0 reduce-scatter.4.cloned.1.call-done
  312.4 0.0 copy-start.1
  312.4 1.9 broadcast_select_fusion.4
  314.3 0.0 collective-permute-start
  314.3 0.0 reduce-scatter.6.cloned.1.call-done
  314.3 0.0 copy-start
  314.3 1.9 broadcast_select_fusion.2
  316.3 0.5 collective-permute-start.1
  316.8 0.0 reduce-scatter.8.cloned.1.call-done
  316.8 1.9 broadcast_select_fusion
  318.6 0.0 collective-permute-start.2
  318.6 12.9 %all-to-all-done.4 = bf16[8,128,1024]{2,1,0:T(8,128)(2,1)S(1)} async-done(((bf16[8,128,1024]{2,1,0:T(8,128)(2,1)}), bf16[8,128,1024]{2,1,0:T(8,128)(2,1)S(1)}, u32[]{:S(2)}, u32[]{:S(2)}) %all-to-all-start.4) | async-done | bytes 2097184 | tf_op jit(solution)/shard_map/all_to_all | solution.py:431
  331.5 1.1 reduce_sum.12
  332.6 0.0 copy-start.2
  332.6 1.8 slice_bitcast_fusion
  334.3 0.0 collective-permute-done
  334.3 0.0 copy-done.1
  334.3 1.0 select_bitcast_fusion.5
  335.4 0.9 maximum_bitcast_fusion
  336.3 0.0 collective-permute-done.1
  336.3 0.0 copy-done
  336.3 1.0 select_bitcast_fusion.3
  337.4 0.9 maximum_bitcast_fusion.1
  338.3 0.0 collective-permute-done.2
  338.3 0.0 copy-done.2
  338.3 1.0 select_bitcast_fusion.1
  339.4 0.9 pad_maximum_fusion
Async XLA Ops:
  14.3 8.8 %copy-start.3 = (bf16[1,128,512]{2,1,0:T(8,128)(2,1)S(1)}, bf16[1,128,512]{2,1,0:T(8,128)(2,1)}, u32[]{:S(2)}) copy-start(bf16[1,128,512]{2,1,0:T(8,128)(2,1)} %param.13) | copy-start | bytes 393220
  14.3 8.9 %copy-start.4 = (bf16[1,128,512]{2,1,0:T(8,128)(2,1)S(1)}, bf16[1,128,512]{2,1,0:T(8,128)(2,1)}, u32[]{:S(2)}) copy-start(bf16[1,128,512]{2,1,0:T(8,128)(2,1)} %param.12) | copy-start | bytes 393220
  14.3 64.0 %all-to-all-start.1 = ((bf16[32,32,2048]{2,1,0:T(8,128)(2,1)}), bf16[32,32,2048]{2,1,0:T(8,128)(2,1)}, u32[]{:S(2)}, u32[]{:S(2)}) async-start(bf16[32,32,2048]{2,1,0:T(8,128)(2,1)} %bitcast.59), calls=%async_computation.1 | async-start | bytes 8388608 | tf_op jit(solution)/shard_map/all_to_all | solution.py:381
  23.0 31.0 %all-gather.2.cloned.1.call-start = ((), (), s32[]{:S(2)}) async-start(), calls=%async_computation.8 | async-start | bytes 2359296 | tf_op jit(solution)/shard_map/all_gather | solution.py:417
  78.3 60.4 %all-to-all-start = ((bf16[32,32,2048]{2,1,0:T(8,128)(2,1)}), bf16[32,32,2048]{2,1,0:T(8,128)(2,1)}, u32[]{:S(2)}, u32[]{:S(2)}) async-start(bf16[32,32,2048]{2,1,0:T(8,128)(2,1)} %bitcast.60), calls=%async_computation | async-start | bytes 8388608 | tf_op jit(solution)/shard_map/all_to_all | solution.py:381
  83.4 228.9 %reduce-scatter.4.cloned.1.call-start = ((), (), s32[]{:S(2)}) async-start(), calls=%async_computation.9 | async-start | bytes 3604480 | tf_op jit(solution)/shard_map/reduce_scatter | solution.py:436
  178.1 136.2 %reduce-scatter.6.cloned.1.call-start = ((), (), s32[]{:S(2)}) async-start(), calls=%async_computation.10 | async-start | bytes 3604480 | tf_op jit(solution)/shard_map/reduce_scatter | solution.py:436
  178.8 60.4 %all-to-all-start.3 = ((bf16[32,32,2048]{2,1,0:T(8,128)(2,1)}), bf16[32,32,2048]{2,1,0:T(8,128)(2,1)}, u32[]{:S(2)}, u32[]{:S(2)}) async-start(bf16[32,32,2048]{2,1,0:T(8,128)(2,1)} %bitcast.58), calls=%async_computation.3 | async-start | bytes 8388608 | tf_op jit(solution)/shard_map/all_to_all | solution.py:381
  184.0 132.8 %reduce-scatter.8.cloned.1.call-start = ((), (), s32[]{:S(2)}) async-start(), calls=%async_computation.11 | async-start | bytes 3604480 | tf_op jit(solution)/shard_map/reduce_scatter | solution.py:436
  239.2 60.4 %all-to-all-start.2 = ((bf16[32,32,2048]{2,1,0:T(8,128)(2,1)}), bf16[32,32,2048]{2,1,0:T(8,128)(2,1)}, u32[]{:S(2)}, u32[]{:S(2)}) async-start(bf16[32,32,2048]{2,1,0:T(8,128)(2,1)} %bitcast.57), calls=%async_computation.2 | async-start | bytes 8388608 | tf_op jit(solution)/shard_map/all_to_all | solution.py:381
  299.6 31.9 %all-to-all-start.4 = ((bf16[8,128,1024]{2,1,0:T(8,128)(2,1)}), bf16[8,128,1024]{2,1,0:T(8,128)(2,1)S(1)}, u32[]{:S(2)}, u32[]{:S(2)}) async-start(bf16[8,128,1024]{2,1,0:T(8,128)(2,1)} %bitcast.67), calls=%async_computation.4 | async-start | bytes 4194304 | tf_op jit(solution)/shard_map/all_to_all | solution.py:431
  312.4 22.0 %copy-start.1 = (bf16[1,704,512]{2,1,0:T(8,128)(2,1)S(1)}, bf16[1,704,512]{2,1,0:T(8,128)(2,1)}, u32[]{:S(2)}) copy-start(bf16[1,704,512]{2,1,0:T(8,128)(2,1)} %reduce-scatter.4.cloned.1.call-done) | copy-start | bytes 2162692
  314.3 20.0 %collective-permute-start = (bf16[704,256]{1,0:T(8,128)(2,1)}, bf16[704,256]{1,0:T(8,128)(2,1)}, u32[]{:S(2)}, u32[]{:S(2)}) collective-permute-start(bf16[704,256]{1,0:T(8,128)(2,1)} %broadcast_select_fusion.4), channel_id=1, source_target_pairs={{0,16},{16,0},{32,48},{48,32},{64,80},{80,64},{96,112},{112,96},{1... | collective-permute-start | bytes 1081352 | tf_op jit(solution)/shard_map/ppermute | solution.py:388
  314.3 22.0 %copy-start = (bf16[1,704,512]{2,1,0:T(8,128)(2,1)S(1)}, bf16[1,704,512]{2,1,0:T(8,128)(2,1)}, u32[]{:S(2)}) copy-start(bf16[1,704,512]{2,1,0:T(8,128)(2,1)} %reduce-scatter.6.cloned.1.call-done) | copy-start | bytes 2162692
  316.3 20.1 %collective-permute-start.1 = (bf16[704,256]{1,0:T(8,128)(2,1)}, bf16[704,256]{1,0:T(8,128)(2,1)}, u32[]{:S(2)}, u32[]{:S(2)}) collective-permute-start(bf16[704,256]{1,0:T(8,128)(2,1)} %broadcast_select_fusion.2), channel_id=1, source_target_pairs={{0,16},{16,0},{32,48},{48,32},{64,80},{80,64},{96,112},{112,96},{1... | collective-permute-start | bytes 1081352 | tf_op jit(solution)/shard_map/ppermute | solution.py:388
  318.6 19.7 %collective-permute-start.2 = (bf16[704,256]{1,0:T(8,128)(2,1)}, bf16[704,256]{1,0:T(8,128)(2,1)}, u32[]{:S(2)}, u32[]{:S(2)}) collective-permute-start(bf16[704,256]{1,0:T(8,128)(2,1)} %broadcast_select_fusion), channel_id=1, source_target_pairs={{0,16},{16,0},{32,48},{48,32},{64,80},{80,64},{96,112},{112,96},{1... | collective-permute-start | bytes 1081352 | tf_op jit(solution)/shard_map/ppermute | solution.py:388
  332.6 5.7 %copy-start.2 = (bf16[1,704,512]{2,1,0:T(8,128)(2,1)S(1)}, bf16[1,704,512]{2,1,0:T(8,128)(2,1)}, u32[]{:S(2)}) copy-start(bf16[1,704,512]{2,1,0:T(8,128)(2,1)} %reduce-scatter.8.cloned.1.call-done) | copy-start | bytes 2162692
Sparse Core Ops, SparseCore 0:
  26.2 27.7 all-gather.1
  178.2 36.0 reduce-scatter.3
  216.7 35.8 reduce-scatter.5
  254.9 35.8 reduce-scatter.7

commit v2 on v1

v2 whole, which is shorter than its diff:
```python
import math

import jax
import jax.numpy as jnp
from jax import lax
from jax.experimental import pallas as pl
from jax.experimental.pallas import tpu as pltpu
from jax.sharding import PartitionSpec as P

DH = 128
TOK = 128
WIDTH = 2048
HEADS = 16
KV_HEADS = 4
GROUP = 4
KV_WIDTH = 512
TOP = 6
SEQ = 8
PLANES = 4
RANKS = 16
EXPERTS = 32
SLOTS = 32
HALF = 16
ROWS = EXPERTS * SLOTS
PART = EXPERTS * HALF
OWN = WIDTH // SEQ
HIDDEN = 704
FULL = TOK * SEQ
SCALE = 1.0 / math.sqrt(DH)
NEG_BIG = -1e30
NORM_EPS = 1e-06
VMEM_BYTES = 56 * 1024 * 1024

bf16 = jnp.bfloat16
f32 = jnp.float32

PLANE_GROUPS = [
    [(2 * z + core) * RANKS + rank for core in range(2) for rank in range(RANKS)]
    for z in range(PLANES)
]
Z_GROUPS = [[2 * z + core for z in range(PLANES)] for core in range(2)]


def params(**kw):
    return pltpu.CompilerParams(vmem_limit_bytes=VMEM_BYTES, **kw)


def cost(share, flops, bytes_accessed, transcendentals):
    return pl.CostEstimate(
        flops=share * flops, bytes_accessed=share * bytes_accessed, transcendentals=transcendentals
    )


def whole(shape):
    return pl.BlockSpec(shape, lambda *_: (0,) * len(shape))


def dot_nn(a, b):
    return lax.dot_general(a, b, (((1,), (0,)), ((), ())), preferred_element_type=f32)


def dot_nt(a, b):
    return lax.dot_general(a, b, (((1,), (1,)), ((), ())), preferred_element_type=f32)


def dot_tn(a, b):
    return lax.dot_general(a, b, (((0,), (0,)), ((), ())), preferred_element_type=f32)


def expert_ids():
    row = lax.broadcasted_iota(jnp.int32, (EXPERTS, TOK), 0)
    return 2 * (row & (RANKS - 1)) + (row >> 4)


def plan_kernel(routes, mix, grad, pick_out, mixed_out, rows_out):
    ids = expert_ids()
    member = jnp.zeros((EXPERTS, TOK), f32)
    weight = jnp.zeros((EXPERTS, TOK), f32)
    for c in range(TOP):
        hit = routes[c] == ids
        member = member + jnp.where(hit, 1.0, 0.0)
        weight = weight + jnp.where(hit, mix[c], 0.0)
    before = lax.broadcasted_iota(jnp.int32, (TOK, TOK), 0) < lax.broadcasted_iota(
        jnp.int32, (TOK, TOK), 1
    )
    rank = dot_nn(member.astype(bf16), jnp.where(before, 1.0, 0.0).astype(bf16))
    slot = jnp.where(member > 0.0, rank, -1.0)
    place = lax.broadcasted_iota(jnp.int32, (EXPERTS, HALF, TOK), 1).astype(f32)
    for h in range(2):
        pick = jnp.where(slot[:, None, :] == place + float(h * HALF), 1.0, 0.0)
        mixed = (pick * weight[:, None, :]).reshape(PART, TOK)
        pick = pick.reshape(PART, TOK).astype(bf16)
        pick_out[h] = pick
        mixed_out[h] = mixed
        scale = jnp.sum(mixed, axis=1, keepdims=True)
        for i in range(0, PART, 256):
            rows = dot_nn(pick[i : i + 256], grad[...])
            rows = (rows * scale[i : i + 256]).astype(bf16)
            first = i // HALF
            rows_out[first : first + 256 // HALF, h] = rows.reshape(256 // HALF, HALF, WIDTH)


def make_plan(routes, mix, grad):
    return pl.pallas_call(
        plan_kernel,
        out_shape=(
            jax.ShapeDtypeStruct((2, PART, TOK), bf16),
            jax.ShapeDtypeStruct((2, PART, TOK), f32),
            jax.ShapeDtypeStruct((EXPERTS, 2, HALF, WIDTH), bf16),
        ),
        compiler_params=params(),
        cost_estimate=cost(5,
            flops=2 * ROWS * TOK * WIDTH, bytes_accessed=8 << 20, transcendentals=0
        ),
    )(routes, mix, grad)


def visible_keys(seq_ref):
    row = seq_ref[0] * TOK + lax.broadcasted_iota(jnp.int32, (TOK, FULL), 0)
    return lax.broadcasted_iota(jnp.int32, (TOK, FULL), 1) <= row


def norm_parts(residual, attention):
    hidden = residual.astype(f32) + attention.astype(f32)
    inv_rms = lax.rsqrt(jnp.mean(hidden * hidden, axis=1, keepdims=True) + NORM_EPS)
    return hidden, inv_rms


def attend_kernel(
    seq_ref, q_ref, k_ref, v_ref, residual, pick, att_out, lse_out, first_out, second_out
):
    head = pl.program_id(0)
    keys, values = k_ref[...], v_ref[...]
    visible = visible_keys(seq_ref)
    outs, totals = [], []
    for g in range(GROUP):
        scores = dot_nt(q_ref[:, g * DH : (g + 1) * DH], keys) * SCALE
        masked = jnp.where(visible, scores, NEG_BIG)
        row_max = jnp.max(masked, axis=1, keepdims=True)
        weights = jnp.exp(masked - row_max)
        row_sum = jnp.sum(weights, axis=1, keepdims=True)
        mixed = dot_nn(weights.astype(bf16), values)
        outs.append((mixed / row_sum).astype(bf16))
        totals.append(jnp.broadcast_to(row_max + jnp.log(row_sum), (TOK, DH)))
    columns = pl.ds(pl.multiple_of(head * GROUP * DH, GROUP * DH), GROUP * DH)
    att_out[:, columns] = jnp.concatenate(outs, axis=1)
    lse_out[...] = jnp.concatenate(totals, axis=1)

    @pl.when(head == KV_HEADS - 1)
    def _():
        hidden, inv_rms = norm_parts(residual[...], att_out[...])
        normed = (hidden * inv_rms).astype(bf16)
        for h, rows_out in enumerate((first_out, second_out)):
            for i in range(0, PART, 256):
                rows_out[i : i + 256, :] = dot_nn(pick[h, i : i + 256, :], normed).astype(bf16)


def attend(seq_index, queries, pairs, residual, pick):
    return pl.pallas_call(
        attend_kernel,
        grid_spec=pltpu.PrefetchScalarGridSpec(
            num_scalar_prefetch=1,
            grid=(KV_HEADS,),
            in_specs=[
                pl.BlockSpec((TOK, GROUP * DH), lambda h, s: (0, h)),
                pl.BlockSpec((FULL, DH), lambda h, s: (0, h)),
                pl.BlockSpec((FULL, DH), lambda h, s: (0, KV_HEADS + h)),
                whole((TOK, WIDTH)),
                whole((2, PART, TOK)),
            ],
            out_specs=[
                whole((TOK, WIDTH)),
                pl.BlockSpec((TOK, GROUP * DH), lambda h, s: (0, h)),
                whole((PART, WIDTH)),
                whole((PART, WIDTH)),
            ],
        ),
        out_shape=(
            jax.ShapeDtypeStruct((TOK, WIDTH), bf16),
            jax.ShapeDtypeStruct((TOK, WIDTH), f32),
            jax.ShapeDtypeStruct((PART, WIDTH), bf16),
            jax.ShapeDtypeStruct((PART, WIDTH), bf16),
        ),
        compiler_params=params(),
        cost_estimate=cost(5,
            flops=4 * TOK * FULL * WIDTH + 2 * ROWS * TOK * WIDTH,
            bytes_accessed=10 << 20,
            transcendentals=HEADS * TOK * FULL,
        ),
    )(seq_index, queries, pairs, pairs, residual, pick)


def expert_kernel(core, rows, pairs, gate_w, up_w, down_w, back_out, act_out, gate_out, up_out):
    step = rows.shape[0]
    gate = dot_nt(rows[...], gate_w[0])
    up = dot_nt(rows[...], up_w[0])
    sig = jax.nn.sigmoid(gate)
    silu = gate * sig
    act_out[...] = (silu * up).astype(bf16)
    act_grad = dot_nt(pairs[...].reshape(step, WIDTH), down_w[0])
    gate_grad = (act_grad * up * sig * (1.0 + gate * (1.0 - sig))).astype(bf16)
    up_grad = (act_grad * silu).astype(bf16)
    gate_out[...] = gate_grad
    up_out[...] = up_grad
    back_out[...] = (dot_nn(gate_grad, gate_w[0]) + dot_nn(up_grad, up_w[0])).astype(bf16)


def expert_rows(half, core, rows, pairs, gate_w, up_w, down_w):
    step = 256
    tile = pl.BlockSpec((step, WIDTH), lambda i, c: (i, 0))
    thin = pl.BlockSpec((step, HIDDEN), lambda i, c: (i, 0))
    weight = pl.BlockSpec(
        (1, HIDDEN, WIDTH), lambda i, c: (c[0], 0, 0), pipeline_mode=pl.Buffered(1)
    )
    return pl.pallas_call(
        expert_kernel,
        grid_spec=pltpu.PrefetchScalarGridSpec(
            num_scalar_prefetch=1,
            grid=(PART // step,),
            in_specs=[
                tile,
                pl.BlockSpec((step // HALF, 1, HALF, WIDTH), lambda i, c: (i, half, 0, 0)),
                weight,
                weight,
                weight,
            ],
            out_specs=[tile, thin, thin, thin],
        ),
        out_shape=(
            jax.ShapeDtypeStruct((PART, WIDTH), bf16),
            jax.ShapeDtypeStruct((PART, HIDDEN), bf16),
            jax.ShapeDtypeStruct((PART, HIDDEN), bf16),
            jax.ShapeDtypeStruct((PART, HIDDEN), bf16),
        ),
        compiler_params=params(),
        cost_estimate=cost(100,
            flops=10 * PART * HIDDEN * WIDTH,
            bytes_accessed=16 << 20,
            transcendentals=PART * HIDDEN,
        ),
    )(core, rows, pairs, gate_w, up_w, down_w)


def split_columns(place, total, value, keep_out, send_out):
    total[...] = value
    keep = pl.ds(pl.multiple_of(place * OWN, OWN), OWN)
    send = pl.ds(pl.multiple_of((1 - place) * OWN, OWN), OWN)
    keep_out[0] = total[:, keep].astype(bf16)
    send_out[0] = total[:, send].astype(bf16)


def down_kernel(core, pairs, act_a, act_b, keep, send, total):
    pairs_a = pairs[:, 0].reshape(PART, 2 * OWN)
    pairs_b = pairs[:, 1].reshape(PART, 2 * OWN)
    value = dot_tn(act_a[...], pairs_a) + dot_tn(act_b[...], pairs_b)
    split_columns(core[0], total, value, keep, send)


def inner_kernel(
    core, rows_a, rows_b, gate_a, gate_b, up_a, up_b, gate_keep, gate_send, up_keep, up_send, total
):
    value = dot_tn(gate_a[...], rows_a[...]) + dot_tn(gate_b[...], rows_b[...])
    split_columns(core[0], total, value, gate_keep, gate_send)
    value = dot_tn(up_a[...], rows_a[...]) + dot_tn(up_b[...], rows_b[...])
    split_columns(core[0], total, value, up_keep, up_send)


def column_sums(kernel, n_outs, core, wide, thin):
    columns = [
        pl.BlockSpec((PART, 2 * OWN), lambda i, c: (0, i))
        if w.ndim == 2
        else pl.BlockSpec((EXPERTS, 2, HALF, 2 * OWN), lambda i, c: (0, 0, 0, i))
        for w in wide
    ]
    out = pl.BlockSpec((1, HIDDEN, OWN), lambda i, c: (i, 0, 0))
    return pl.pallas_call(
        kernel,
        grid_spec=pltpu.PrefetchScalarGridSpec(
            num_scalar_prefetch=1,
            grid=(PLANES,),
            in_specs=columns + [whole((PART, HIDDEN))] * len(thin),
            out_specs=[out] * n_outs,
            scratch_shapes=[pltpu.VMEM((HIDDEN, 2 * OWN), f32)],
        ),
        out_shape=(jax.ShapeDtypeStruct((PLANES, HIDDEN, OWN), bf16),) * n_outs,
        compiler_params=params(),
        cost_estimate=cost(100,
            flops=n_outs * ROWS * HIDDEN * WIDTH,
            bytes_accessed=n_outs * (4 << 20),
            transcendentals=0,
        ),
    )(core, *wide, *thin)


def stack_kernel(core, keep, other, out):
    out[0, core[0]] = keep[0]
    out[0, 1 - core[0]] = other[0]


def stack_experts(core, keep, other):
    block = pl.BlockSpec((1, HIDDEN, OWN), lambda i, c: (i, 0, 0))
    return pl.pallas_call(
        stack_kernel,
        grid_spec=pltpu.PrefetchScalarGridSpec(
            num_scalar_prefetch=1,
            grid=(PLANES,),
            in_specs=[block, block],
            out_specs=pl.BlockSpec((1, 2, HIDDEN, OWN), lambda i, c: (i, 0, 0, 0)),
        ),
        out_shape=jax.ShapeDtypeStruct((PLANES, 2, HIDDEN, OWN), bf16),
        compiler_params=params(),
        cost_estimate=cost(100, flops=0, bytes_accessed=6 << 20, transcendentals=0),
    )(core, keep, other)


def result_kernel(core, act_a, act_b, down_w, out):
    rows = act_a.shape[0]
    out[:, 0] = dot_nn(act_a[...], down_w[0]).astype(bf16).reshape(rows // HALF, HALF, WIDTH)
    out[:, 1] = dot_nn(act_b[...], down_w[0]).astype(bf16).reshape(rows // HALF, HALF, WIDTH)


def expert_results(core, act, down_w):
    step = 128
    return pl.pallas_call(
        result_kernel,
        grid_spec=pltpu.PrefetchScalarGridSpec(
            num_scalar_prefetch=1,
            grid=(PART // step,),
            in_specs=[
                pl.BlockSpec((step, HIDDEN), lambda i, c: (i, 0)),
                pl.BlockSpec((step, HIDDEN), lambda i, c: (i, 0)),
                pl.BlockSpec((1, HIDDEN, WIDTH), lambda i, c: (c[0], 0, 0)),
            ],
            out_specs=pl.BlockSpec((step // HALF, 2, HALF, WIDTH), lambda i, c: (i, 0, 0, 0)),
        ),
        out_shape=jax.ShapeDtypeStruct((EXPERTS, 2, HALF, WIDTH), bf16),
        compiler_params=params(),
        cost_estimate=cost(100,
            flops=2 * ROWS * HIDDEN * WIDTH, bytes_accessed=9 << 20, transcendentals=0
        ),
    )(core, *act, down_w)


def attend_back_kernel(
    seq_ref,
    q_ref,
    k_ref,
    v_ref,
    lse,
    back_a,
    back_b,
    pick,
    residual,
    att,
    grad,
    res_out,
    q_out,
    keep_out,
    send_out,
    kv_sum,
):
    head = pl.program_id(0)

    @pl.when(head == 0)
    def _():
        normed_grad = dot_tn(pick[0], back_a[...]) + dot_tn(pick[1], back_b[...])
        hidden, inv_rms = norm_parts(residual[...], att[...])
        normed = hidden * inv_rms
        dot_mean = jnp.mean(normed_grad * normed, axis=1, keepdims=True)
        total = grad[...].astype(f32) + inv_rms * (normed_grad - normed * dot_mean)
        res_out[...] = total.astype(bf16)

    keys, values = k_ref[...], v_ref[...]
    visible = visible_keys(seq_ref)
    score_parts, prob_parts, query_parts, grad_parts = [], [], [], []
    for g in range(GROUP):
        query = q_ref[:, g * DH : (g + 1) * DH]
        columns = pl.ds(pl.multiple_of(head * GROUP * DH + g * DH, DH), DH)
        out_grad = res_out[:, columns]
        delta = jnp.sum(
            out_grad.astype(f32) * att[:, columns].astype(f32), axis=1, keepdims=True
        )
        scores = dot_nt(query, keys) * SCALE
        total = lse[:, g * DH : g * DH + 1]
        probs = jnp.exp(jnp.where(visible, scores - total, NEG_BIG))
        prob_grad = dot_nt(out_grad, values)
        score_grad = (probs * (prob_grad - delta)).astype(bf16)
        q_out[:, g * DH : (g + 1) * DH] = (dot_nn(score_grad, keys) * SCALE).astype(bf16)
        score_parts.append(score_grad)
        prob_parts.append(probs.astype(bf16))
        query_parts.append(query)
        grad_parts.append(out_grad)
    key_sum = dot_tn(jnp.concatenate(score_parts, axis=0), jnp.concatenate(query_parts, axis=0))
    value_sum = dot_tn(jnp.concatenate(prob_parts, axis=0), jnp.concatenate(grad_parts, axis=0))
    kv_sum[:, pl.ds(pl.multiple_of(head * DH, DH), DH)] = (key_sum * SCALE).astype(bf16)
    kv_sum[:, pl.ds(pl.multiple_of(KV_WIDTH + head * DH, DH), DH)] = value_sum.astype(bf16)

    @pl.when(head == KV_HEADS - 1)
    def _():
        plane, core = seq_ref[0] >> 1, seq_ref[0] & 1
        for d in range(PLANES):
            mine = 2 * ((plane + d) & (PLANES - 1)) + core
            keep_out[d] = kv_sum[pl.ds(pl.multiple_of(mine * TOK, TOK), TOK), :]
            send_out[d] = kv_sum[pl.ds(pl.multiple_of((mine ^ 1) * TOK, TOK), TOK), :]


def attend_back(seq_index, queries, pairs, lse, back_a, back_b, pick, residual, att, grad):
    return pl.pallas_call(
        attend_back_kernel,
        grid_spec=pltpu.PrefetchScalarGridSpec(
            num_scalar_prefetch=1,
            grid=(KV_HEADS,),
            in_specs=[
                pl.BlockSpec((TOK, GROUP * DH), lambda h, s: (0, h)),
                pl.BlockSpec((FULL, DH), lambda h, s: (0, h)),
                pl.BlockSpec((FULL, DH), lambda h, s: (0, KV_HEADS + h)),
                pl.BlockSpec((TOK, GROUP * DH), lambda h, s: (0, h)),
                whole((PART, WIDTH)),
                whole((PART, WIDTH)),
                whole((2, PART, TOK)),
                whole((TOK, WIDTH)),
                whole((TOK, WIDTH)),
                whole((TOK, WIDTH)),
            ],
            out_specs=[
                whole((TOK, WIDTH)),
                pl.BlockSpec((TOK, GROUP * DH), lambda h, s: (0, h)),
                whole((PLANES, TOK, 2 * KV_WIDTH)),
                whole((PLANES, TOK, 2 * KV_WIDTH)),
            ],
            scratch_shapes=[pltpu.VMEM((FULL, 2 * KV_WIDTH), bf16)],
        ),
        out_shape=(
            jax.ShapeDtypeStruct((TOK, WIDTH), bf16),
            jax.ShapeDtypeStruct((TOK, WIDTH), bf16),
            jax.ShapeDtypeStruct((PLANES, TOK, 2 * KV_WIDTH), bf16),
            jax.ShapeDtypeStruct((PLANES, TOK, 2 * KV_WIDTH), bf16),
        ),
        compiler_params=params(),
        cost_estimate=cost(100,
            flops=10 * TOK * FULL * WIDTH + 2 * ROWS * TOK * WIDTH,
            bytes_accessed=12 << 20,
            transcendentals=HEADS * TOK * FULL,
        ),
    )(seq_index, queries, pairs, pairs, lse, back_a, back_b, pick, residual, att, grad)


def combine_kernel(routes, pick, mixed, returned, residual, att, grad, layer_out, mix_out):
    total = residual[...].astype(f32) + att[...].astype(f32)
    by_expert = jnp.zeros((EXPERTS, TOK), f32)
    for h in range(2):
        rows = returned[:, h].reshape(PART, WIDTH)
        coarse = mixed[h].astype(bf16)
        fine = (mixed[h] - coarse.astype(f32)).astype(bf16)
        total = total + dot_tn(coarse, rows) + dot_tn(fine, rows)
        inner = dot_nt(rows, grad[...]) * pick[h].astype(f32)
        by_expert = by_expert + jnp.sum(inner.reshape(EXPERTS, HALF, TOK), axis=1)
    layer_out[...] = total.astype(bf16)
    ids = expert_ids()
    for c in range(TOP):
        hit = routes[c] == ids
        mix_out[c] = jnp.sum(jnp.where(hit, by_expert, 0.0), axis=0, keepdims=True)


def combine(routes, pick, mixed, returned, residual, att, grad):
    return pl.pallas_call(
        combine_kernel,
        out_shape=(
            jax.ShapeDtypeStruct((TOK, WIDTH), bf16),
            jax.ShapeDtypeStruct((TOP, 1, TOK), f32),
        ),
        compiler_params=params(),
        cost_estimate=cost(100,
            flops=6 * ROWS * TOK * WIDTH, bytes_accessed=8 << 20, transcendentals=0
        ),
    )(routes, pick, mixed, returned, residual, att, grad)


def pass_kernel(*refs):
    pass


def after(earlier, *values):
    anywhere = pl.BlockSpec(memory_space=pl.ANY)
    return pl.pallas_call(
        pass_kernel,
        in_specs=[anywhere] * (1 + len(values)),
        out_specs=[anywhere] * len(values),
        out_shape=[jax.ShapeDtypeStruct(v.shape, v.dtype) for v in values],
        input_output_aliases={1 + i: i for i in range(len(values))},
    )(earlier, *values)


def exchange(blocks):
    return lax.all_to_all(
        blocks, ("seq", "expert"), 0, 0, tiled=True, axis_index_groups=PLANE_GROUPS
    )


def exchange_rows(rows):
    return exchange(rows.reshape(EXPERTS, HALF, WIDTH)).reshape(PART, WIDTH)


def swap_cores(values):
    return lax.ppermute(values, "seq", [(i, i ^ 1) for i in range(SEQ)])


def send_earlier(values, planes):
    pairs = [
        (2 * z + core, 2 * (z + planes - PLANES) + core)
        for z in range(PLANES - planes, PLANES)
        for core in range(2)
    ]
    return lax.ppermute(values, "seq", pairs)


def on_device(
    residual,
    queries,
    key_input,
    value_input,
    routes,
    mix_weights,
    gate_weight,
    up_weight,
    down_weight,
    grad_out,
):
    seq = lax.axis_index("seq")
    seq_index = seq.astype(jnp.int32).reshape(1)
    core = (seq & 1).astype(jnp.int32)
    core_index = core.reshape(1)
    residual = residual.reshape(TOK, WIDTH)
    queries = queries.reshape(TOK, WIDTH)
    grad = grad_out.reshape(TOK, WIDTH)
    routes = jnp.transpose(routes, (2, 0, 1))
    mix = jnp.transpose(mix_weights, (2, 0, 1))
    gate_w = jnp.swapaxes(gate_weight, 1, 2)
    up_w = jnp.swapaxes(up_weight, 1, 2)
    pairs = jnp.concatenate(
        [key_input.reshape(TOK, KV_WIDTH), value_input.reshape(TOK, KV_WIDTH)], axis=1
    )
    pairs = lax.all_gather(pairs, "seq", axis=0, tiled=True)
    pick, mixed, grad_rows = make_plan(routes, mix, grad)
    grad_rows = exchange(grad_rows)
    att, lse, rows_a, rows_b = attend(seq_index, queries, pairs, residual, pick)
    rows_a, rows_b = after(grad_rows, rows_a, rows_b)
    rows_a, rows_b = exchange_rows(rows_a), exchange_rows(rows_b)
    weights = (gate_w, up_w, down_weight)
    back_a, act_a, gate_a, up_a = expert_rows(0, core_index, rows_a, grad_rows, *weights)
    back_a = exchange_rows(back_a)
    back_b, act_b, gate_b, up_b = expert_rows(1, core_index, rows_b, grad_rows, *weights)
    back_b = exchange_rows(back_b)
    down_keep, down_send = column_sums(down_kernel, 2, core_index, (grad_rows,), (act_a, act_b))
    down_stack = stack_experts(core_index, down_keep, swap_cores(down_send))
    gate_a, gate_b = after(down_stack, gate_a, gate_b)
    gate_keep, gate_send, up_keep, up_send = column_sums(
        inner_kernel, 4, core_index, (rows_a, rows_b), (gate_a, gate_b, up_a, up_b)
    )
    results = exchange(expert_results(core_index, (act_a, act_b), down_weight))
    gate_stack = stack_experts(core_index, gate_keep, swap_cores(gate_send))
    up_stack = stack_experts(core_index, up_keep, swap_cores(up_send))
    (lse,) = after(gate_stack, lse)
    (lse,) = after(up_stack, lse)
    res_grad, query_grad, keep, send = attend_back(
        seq_index, queries, pairs, lse, back_a, back_b, pick, residual, att, grad
    )
    other = swap_cores(send)
    parts = [
        (keep[d].astype(f32) + other[d].astype(f32)).astype(bf16) for d in range(PLANES)
    ]
    kv_grad = parts[0].astype(f32)
    for d in range(1, PLANES):
        kv_grad = kv_grad + send_earlier(parts[d], d).astype(f32)
    kv_grad = kv_grad.astype(bf16)
    layer_out, mix_grad = combine(routes, pick, mixed, results, residual, att, grad)
    weight_grads = []
    for stacked in (down_stack, gate_stack, up_stack):
        share = lax.psum_scatter(
            stacked.reshape(PLANES * 2 * HIDDEN, OWN),
            "seq",
            scatter_dimension=0,
            axis_index_groups=Z_GROUPS,
            tiled=True,
        )
        weight_grads.append(share.reshape(2, HIDDEN, OWN))
    down_grad, gate_grad, up_grad = weight_grads
    return (
        layer_out.reshape(1, TOK, WIDTH),
        res_grad.reshape(1, TOK, WIDTH),
        query_grad.reshape(1, TOK, WIDTH),
        kv_grad[:, :KV_WIDTH].reshape(1, TOK, KV_WIDTH),
        kv_grad[:, KV_WIDTH:].reshape(1, TOK, KV_WIDTH),
        jnp.transpose(mix_grad, (1, 2, 0)),
        jnp.swapaxes(gate_grad, 1, 2),
        jnp.swapaxes(up_grad, 1, 2),
        down_grad,
    )


def solution(mesh):
    rows = P("expert", "seq", None)
    weights = P("expert", None, None)
    return jax.shard_map(
        on_device,
        mesh=mesh,
        in_specs=(rows, rows, rows, rows, rows, rows, weights, weights, weights, rows),
        out_specs=(rows, rows, rows, rows, rows, rows, rows, rows, P("expert", None, "seq")),
        check_vma=False,
    )
```

time: 348 us -> 313 us (0.90)
  waiting for transfers between devices: 200 us -> 145 us
  Pallas kernels: 83.3 us -> 105 us
  starting transfers between devices: 30.6 us -> 40.1 us
  other arithmetic: 13.5 us -> 4.42 us
    all_to_all x4 -> x6, waiting for transfers between devices: 156 us -> 125 us  [exchange(): lax.all_to_all(blocks, ('seq', 'expert'), 0, 0, tiled=True, axis_index_gr...]
    pallas_call x2 -> x10, Pallas kernels: 18.2 us -> 34.4 us  [the longest x2 17.7 us: column_sums(): pl.pallas_call(kernel, grid_spec=pltpu.PrefetchScalarGridSpec(num_scalar_...]
    all_to_all x1 -> x0, waiting for transfers between devices: 12.9 us -> none  [on_device(): lax.all_to_all(kv_parts.reshape(SEQ, TOK, 2 * KV_WIDTH), 'seq', 0, 0, til...]
    all_gather x1, waiting for transfers between devices: 30.1 us -> 17.3 us  [on_device(): pairs = lax.all_gather(pairs, 'seq', axis=0, tiled=True)]
    all_to_all x4 -> x6, starting transfers between devices: 24.2 us -> 34.2 us  [exchange(): lax.all_to_all(blocks, ('seq', 'expert'), 0, 0, tiled=True, axis_index_gr...]
    select_n x3 -> x0, other arithmetic: 5.74 us -> none  [on_device(): other = swap_cores(jnp.where(core == 0, high, low))]
    all_to_all x1 -> x0, starting transfers between devices: 5.58 us -> none  [on_device(): lax.all_to_all(kv_parts.reshape(SEQ, TOK, 2 * KV_WIDTH), 'seq', 0, 0, til...]
    pallas_call x1 -> x2, Pallas kernels: 25.7 us -> 30.7 us  [expert_rows(): pl.pallas_call(expert_kernel, grid_spec=pltpu.PrefetchScalarGridSpec(num_...]
  transfers between devices with their start and end apart: 12 -> 17, of which waited for: 6 -> 8; matrix products, arithmetic and copies ran while one was open for 4% -> 1% of each run, Pallas kernels for 11% -> 26%
where the time goes in v2:
time: 313 us; the launch traced here: 312 us
  waiting for transfers between devices  145 us (46%)
  Pallas kernels  105 us (34%)
  starting transfers between devices  40.1 us (13%)
  between operations  13.9 us (4%)
  other arithmetic  4.42 us (1%)
  local copies, waits for them, and re-layouts  3.22 us (1%)
    all_to_all x6, waiting for transfers between devices, exchange(): lax.all_to_all(blocks, ('seq', 'expert'), 0, 0, tiled=True, axis_index_gr...  125 us
    all_to_all x6, starting transfers between devices, exchange(): lax.all_to_all(blocks, ('seq', 'expert'), 0, 0, tiled=True, axis_index_gr...  34.2 us
    pallas_call x2, Pallas kernels, expert_rows(): pl.pallas_call(expert_kernel, grid_spec=pltpu.PrefetchScalarGridSpec(num_...  30.7 us
    pallas_call x2, Pallas kernels, column_sums(): pl.pallas_call(kernel, grid_spec=pltpu.PrefetchScalarGridSpec(num_scalar_...  17.7 us
    all_gather x1, waiting for transfers between devices, on_device(): pairs = lax.all_gather(pairs, 'seq', axis=0, tiled=True)  17.3 us
    pallas_call x1, Pallas kernels, attend_back(): pl.pallas_call(attend_back_kernel, grid_spec=pltpu.PrefetchScalarGridSpec...  14.8 us
    pallas_call x3, Pallas kernels, stack_experts(): pl.pallas_call(stack_kernel, grid_spec=pltpu.PrefetchScalarGridSpec(num_s...  12.3 us
    pallas_call x1, Pallas kernels, attend(): pl.pallas_call(attend_kernel, grid_spec=pltpu.PrefetchScalarGridSpec(num_...  11.7 us
  transfers between devices with their start and end apart: 17, of which 8 were waited for; matrix products, arithmetic and copies ran while one was open for 1% of the time, Pallas kernels for 26%

profile of v2, /device:TPU:1, one launch (start us, length us, event | category | flops | bytes accessed | tf_op | source)
XLA Modules:
  0.0 312.1 jit_solution(12238805193661585116)
XLA Ops:
  7.2 0.0 all-gather.2.cloned.1.call-start
  7.2 1.7 pad_maximum_fusion
  8.9 0.0 all-gather.2.cloned.1.call-update
  8.9 4.5 %shard_map.169 = (bf16[2,512,128]{2,1,0:T(8,128)(2,1)}, f32[2,512,128]{2,1,0:T(8,128)}, bf16[32,2,16,2048]{3,2,1,0:T(8,128)(2,1)}) custom-call(s32[6,1,128]{2,1,0:T(1,128)} %bitcast.72, f32[6,1,128]{2,1,0:T(1,128)} %bitcast.71, bf16[128,2048]{1,0:T(8,128)(2,1)} %bitcast.65), custom_call_target="tpu_custom_call" | custom-call | flops 2684354560 | bytes 41943040 | tf_op jit(solution)/shard_map/pallas_call | solution.py:104
  13.4 8.6 %all-to-all-start = ((bf16[32,2,16,2048]{3,2,1,0:T(8,128)(2,1)}), bf16[32,2,16,2048]{3,2,1,0:T(8,128)(2,1)}, u32[]{:S(2)}, u32[]{:S(2)}) async-start(bf16[32,2,16,2048]{3,2,1,0:T(8,128)(2,1)} %get-tuple-element.42), calls=%async_computation | async-start | bytes 8388608 | tf_op jit(solution)/shard_map/all_to_all | solution.py:495
  22.1 17.3 %all-gather.2.cloned.1.call-done.k_ref.v_ref = bf16[1024,1024]{1,0:T(8,128)(2,1)} async-done(((bf16[128,1024]{1,0:T(8,128)(2,1)}), bf16[1024,1024]{1,0:T(8,128)(2,1)}) %all-gather.2.cloned.1.call-update) | async-done | bytes 2097168 | tf_op jit(solution)/shard_map/all_gather | solution.py:543
  39.3 11.7 %shard_map.170 = (bf16[128,2048]{1,0:T(8,128)(2,1)}, f32[128,2048]{1,0:T(8,128)}, bf16[512,2048]{1,0:T(8,128)(2,1)}, bf16[512,2048]{1,0:T(8,128)(2,1)}) custom-call(s32[1]{0:T(128)} %bitcast.4.seq_ref, bf16[128,2048]{1,0:T(8,128)(2,1)} %bitcast.63, bf16[1024,1024]{1,0:T(8,128)(2,1)} %all-gather.2.cloned.1.call-done.k_ref.v_ref, ...), custom_call_target="tpu_custom_call" | custom-call | flops 8053063680 | bytes 52428800 | tf_op jit(solution)/shard_map/pallas_call | solution.py:159
  51.1 26.2 %all-to-all-done.refs_0_.pairs = bf16[32,2,16,2048]{3,2,1,0:T(8,128)(2,1)} async-done(((bf16[32,2,16,2048]{3,2,1,0:T(8,128)(2,1)}), bf16[32,2,16,2048]{3,2,1,0:T(8,128)(2,1)}, u32[]{:S(2)}, u32[]{:S(2)}) %all-to-all-start) | async-done | bytes 4194336 | tf_op jit(solution)/shard_map/all_to_all | solution.py:495
  77.3 5.1 %all-to-all-start.1 = ((bf16[32,16,2048]{2,1,0:T(8,128)(2,1)}), bf16[32,16,2048]{2,1,0:T(8,128)(2,1)S(1)}, u32[]{:S(2)}, u32[]{:S(2)}) async-start(bf16[32,16,2048]{2,1,0:T(8,128)(2,1)} %bitcast.51), calls=%async_computation.1 | async-start | bytes 4194304 | tf_op jit(solution)/shard_map/all_to_all | solution.py:495
  82.4 28.4 %all-to-all-done.1 = bf16[32,16,2048]{2,1,0:T(8,128)(2,1)S(1)} async-done(((bf16[32,16,2048]{2,1,0:T(8,128)(2,1)}), bf16[32,16,2048]{2,1,0:T(8,128)(2,1)S(1)}, u32[]{:S(2)}, u32[]{:S(2)}) %all-to-all-start.1) | async-done | bytes 2097184 | tf_op jit(solution)/shard_map/all_to_all | solution.py:495
  110.8 0.0 copy-start
  110.8 1.3 copy-done
  112.1 5.3 %all-to-all-start.2 = ((bf16[32,16,2048]{2,1,0:T(8,128)(2,1)}), bf16[32,16,2048]{2,1,0:T(8,128)(2,1)}, u32[]{:S(2)}, u32[]{:S(2)}) async-start(bf16[32,16,2048]{2,1,0:T(8,128)(2,1)} %bitcast.13), calls=%async_computation.2 | async-start | bytes 4194304 | tf_op jit(solution)/shard_map/all_to_all | solution.py:495
  117.4 15.4 %shard_map.172 = (bf16[512,2048]{1,0:T(8,128)(2,1)}, bf16[512,704]{1,0:T(8,128)(2,1)}, bf16[512,704]{1,0:T(8,128)(2,1)}, bf16[512,704]{1,0:T(8,128)(2,1)}) custom-call(s32[1]{0:T(128)} %bitcast.3.core, bf16[512,2048]{1,0:T(8,128)(2,1)} %bitcast.52, bf16[32,2,16,2048]{3,2,1,0:T(8,128)(2,1)} %all-to-all-done.refs_0_.pairs, bf16[2,704,2048]{2,1,0:T(8,128)(2,1)} %bitcast.56, ...), custom_call_target="tpu_custom_call" | custom-call | flops 738197504000 | bytes 1677721600 | tf_op jit(solution)/shard_map/pallas_call | solution.py:215
  132.8 13.1 %all-to-all-done.2 = bf16[32,16,2048]{2,1,0:T(8,128)(2,1)} async-done(((bf16[32,16,2048]{2,1,0:T(8,128)(2,1)}), bf16[32,16,2048]{2,1,0:T(8,128)(2,1)}, u32[]{:S(2)}, u32[]{:S(2)}) %all-to-all-start.2) | async-done | bytes 2097184 | tf_op jit(solution)/shard_map/all_to_all | solution.py:495
  145.9 15.3 %shard_map.173 = (bf16[512,2048]{1,0:T(8,128)(2,1)}, bf16[512,704]{1,0:T(8,128)(2,1)}, bf16[512,704]{1,0:T(8,128)(2,1)}, bf16[512,704]{1,0:T(8,128)(2,1)}) custom-call(s32[1]{0:T(128)} %bitcast.3.core, bf16[512,2048]{1,0:T(8,128)(2,1)} %bitcast.14.rows.rows_b, bf16[32,2,16,2048]{3,2,1,0:T(8,128)(2,1)} %all-to-all-done.refs_0_.pairs, ...), custom_call_target="tpu_custom_call" | custom-call | flops 738197504000 | bytes 1677721600 | tf_op jit(solution)/shard_map/pallas_call | solution.py:215
  161.2 7.2 %shard_map.176 = (bf16[4,704,256]{2,1,0:T(8,128)(2,1)}, bf16[4,704,256]{2,1,0:T(8,128)(2,1)}) custom-call(s32[1]{0:T(128)} %bitcast.3.core, bf16[32,2,16,2048]{3,2,1,0:T(8,128)(2,1)} %all-to-all-done.refs_0_.pairs, bf16[512,704]{1,0:T(8,128)(2,1)} %get-tuple-element.46.act_a, bf16[512,704]{1,0:T(8,128)(2,1)} %get-tuple-element.48.act_b), custom_call_target="tpu_custom_call" | custom-call | flops 295279001600 | bytes 838860800 | tf_op jit(solution)/shard_map/pallas_call | solution.py:276
  168.5 0.8 collective-permute-start
  169.3 4.6 %all-to-all-start.4 = ((bf16[32,16,2048]{2,1,0:T(8,128)(2,1)}), bf16[32,16,2048]{2,1,0:T(8,128)(2,1)}, u32[]{:S(2)}, u32[]{:S(2)}) async-start(bf16[32,16,2048]{2,1,0:T(8,128)(2,1)} %bitcast.16), calls=%async_computation.4 | async-start | bytes 4194304 | tf_op jit(solution)/shard_map/all_to_all | solution.py:495
  173.8 0.0 reduce-scatter.8.cloned.1.call-start
  173.9 0.0 collective-permute-done.other
  173.9 0.0 copy-start.1
  173.9 1.2 copy-done.1
  175.1 4.1 %shard_map.177.refs_0_ = bf16[4,2,704,256]{3,2,1,0:T(8,128)(2,1)} custom-call(s32[1]{0:T(128)} %bitcast.3.core, bf16[4,704,256]{2,1,0:T(8,128)(2,1)} %get-tuple-element.51.keep, bf16[4,704,256]{2,1,0:T(8,128)(2,1)} %copy-done.1), custom_call_target="tpu_custom_call" | custom-call | bytes 629145600 | tf_op jit(solution)/shard_map/pallas_call | solution.py:302
  179.2 0.0 reduce-scatter.8.cloned.1.call-update
  179.2 10.4 %shard_map.179 = (bf16[4,704,256]{2,1,0:T(8,128)(2,1)}, bf16[4,704,256]{2,1,0:T(8,128)(2,1)}, bf16[4,704,256]{2,1,0:T(8,128)(2,1)}, bf16[4,704,256]{2,1,0:T(8,128)(2,1)}) custom-call(s32[1]{0:T(128)} %bitcast.3.core, bf16[512,2048]{1,0:T(8,128)(2,1)} %bitcast.53, bf16[512,2048]{1,0:T(8,128)(2,1)} %bitcast.14.rows.rows_b, ...), custom_call_target="tpu_custom_call" | custom-call | flops 590558003200 | bytes 1677721600 | tf_op jit(solution)/shard_map/pallas_call | solution.py:276
  189.6 0.2 collective-permute-start.1
  189.8 0.3 collective-permute-start.2
  190.1 12.1 %all-to-all-done.4 = bf16[32,16,2048]{2,1,0:T(8,128)(2,1)} async-done(((bf16[32,16,2048]{2,1,0:T(8,128)(2,1)}), bf16[32,16,2048]{2,1,0:T(8,128)(2,1)}, u32[]{:S(2)}, u32[]{:S(2)}) %all-to-all-start.4) | async-done | bytes 2097184 | tf_op jit(solution)/shard_map/all_to_all | solution.py:495
  202.2 5.3 %all-to-all-start.5 = ((bf16[32,16,2048]{2,1,0:T(8,128)(2,1)}), bf16[32,16,2048]{2,1,0:T(8,128)(2,1)}, u32[]{:S(2)}, u32[]{:S(2)}) async-start(bf16[32,16,2048]{2,1,0:T(8,128)(2,1)} %bitcast.18), calls=%async_computation.5 | async-start | bytes 4194304 | tf_op jit(solution)/shard_map/all_to_all | solution.py:495
  207.5 0.3 reduce-scatter.6.cloned.1.call-start
  207.8 7.5 %shard_map.174 = bf16[32,2,16,2048]{3,2,1,0:T(8,128)(2,1)} custom-call(s32[1]{0:T(128)} %bitcast.3.core, bf16[512,704]{1,0:T(8,128)(2,1)} %get-tuple-element.46.act_a, bf16[512,704]{1,0:T(8,128)(2,1)} %get-tuple-element.48.act_b, bf16[2,704,2048]{2,1,0:T(8,128)(2,1)} %down_w.5), custom_call_target="tpu_custom_call" | custom-call | flops 295279001600 | bytes 943718400 | tf_op jit(solution)/shard_map/pallas_call | solution.py:324
  215.3 0.0 collective-permute-done.2.other
  215.3 4.1 %shard_map.181.refs_0_ = bf16[4,2,704,256]{3,2,1,0:T(8,128)(2,1)} custom-call(s32[1]{0:T(128)} %bitcast.3.core, bf16[4,704,256]{2,1,0:T(8,128)(2,1)} %get-tuple-element.61.keep, bf16[4,704,256]{2,1,0:T(8,128)(2,1)} %collective-permute-done.2.other), custom_call_target="tpu_custom_call" | custom-call | bytes 629145600 | tf_op jit(solution)/shard_map/pallas_call | solution.py:302
  219.4 0.0 collective-permute-done.1.other
  219.4 4.1 %shard_map.180.refs_0_ = bf16[4,2,704,256]{3,2,1,0:T(8,128)(2,1)} custom-call(s32[1]{0:T(128)} %bitcast.3.core, bf16[4,704,256]{2,1,0:T(8,128)(2,1)} %get-tuple-element.59.keep, bf16[4,704,256]{2,1,0:T(8,128)(2,1)} %collective-permute-done.1.other), custom_call_target="tpu_custom_call" | custom-call | bytes 629145600 | tf_op jit(solution)/shard_map/pallas_call | solution.py:302
  223.5 0.0 reduce-scatter.6.cloned.1.call-update
  223.6 12.5 %all-to-all-done.5 = bf16[32,16,2048]{2,1,0:T(8,128)(2,1)} async-done(((bf16[32,16,2048]{2,1,0:T(8,128)(2,1)}), bf16[32,16,2048]{2,1,0:T(8,128)(2,1)}, u32[]{:S(2)}, u32[]{:S(2)}) %all-to-all-start.5) | async-done | bytes 2097184 | tf_op jit(solution)/shard_map/all_to_all | solution.py:495
  236.0 5.4 %all-to-all-start.3 = ((bf16[32,2,16,2048]{3,2,1,0:T(8,128)(2,1)}), bf16[32,2,16,2048]{3,2,1,0:T(8,128)(2,1)}, u32[]{:S(2)}, u32[]{:S(2)}) async-start(bf16[32,2,16,2048]{3,2,1,0:T(8,128)(2,1)} %shard_map.174), calls=%async_computation.3 | async-start | bytes 8388608 | tf_op jit(solution)/shard_map/all_to_all | solution.py:495
  241.4 0.0 reduce-scatter.4.cloned.1.call-start
  241.4 14.8 %shard_map.184 = (bf16[128,2048]{1,0:T(8,128)(2,1)}, bf16[128,2048]{1,0:T(8,128)(2,1)}, bf16[4,128,1024]{2,1,0:T(8,128)(2,1)}, bf16[4,128,1024]{2,1,0:T(8,128)(2,1)}) custom-call(s32[1]{0:T(128)} %bitcast.4.seq_ref, bf16[128,2048]{1,0:T(8,128)(2,1)} %bitcast.64, bf16[1024,1024]{1,0:T(8,128)(2,1)} %all-gather.2.cloned.1.call-done.k_ref.v_ref, ...), custom_call_target="tpu_custom_call" | custom-call | flops 322122547200 | bytes 1258291200 | tf_op jit(solution)/shard_map/pallas_call | solution.py:408
  256.2 0.0 copy-start.2
  256.2 0.4 collective-permute-start.3
  256.6 0.0 reduce-scatter.4.cloned.1.call-update
  256.6 2.5 collective-permute-done.3
  259.2 0.0 copy-start.3
  259.2 0.0 copy-done.2
  259.2 1.2 fusion.4
  260.4 1.3 collective-permute-start.4
  261.7 1.3 collective-permute-start.6
  263.0 1.3 collective-permute-start.5
  264.3 32.9 %all-to-all-done.3.returned = bf16[32,2,16,2048]{3,2,1,0:T(8,128)(2,1)} async-done(((bf16[32,2,16,2048]{3,2,1,0:T(8,128)(2,1)}), bf16[32,2,16,2048]{3,2,1,0:T(8,128)(2,1)}, u32[]{:S(2)}, u32[]{:S(2)}) %all-to-all-start.3) | async-done | bytes 4194336 | tf_op jit(solution)/shard_map/all_to_all | solution.py:495
  297.2 6.1 %shard_map.175 = (bf16[128,2048]{1,0:T(8,128)(2,1)}, f32[6,1,128]{2,1,0:T(1,128)}) custom-call(s32[6,1,128]{2,1,0:T(1,128)} %bitcast.73, bf16[2,512,128]{2,1,0:T(8,128)(2,1)} %get-tuple-element.40.pick, f32[2,512,128]{2,1,0:T(8,128)} %get-tuple-element.41.mixed, bf16[32,2,16,2048]{3,2,1,0:T(8,128)(2,1)} %all-to-all-done.3.returned, ...), custom_call_target="tpu_custom_call" | custom-call | flops 161061273600 | bytes 838860800 | tf_op jit(solution)/shard_map/pallas_call | solution.py:466
  303.3 0.0 copy-done.3
  303.3 0.0 collective-permute-done.4
  303.3 0.0 collective-permute-done.6
  303.3 0.0 collective-permute-done.5
  303.3 1.5 fusion.2
  304.8 0.7 slice_bitcast_fusion
  305.6 0.0 reduce-scatter.8.cloned.1.call-done
  305.6 0.0 reduce-scatter.6.cloned.1.call-done
  305.6 0.0 reduce-scatter.4.cloned.1.call-done
  (4 shorter events, 0.0 us)
Async XLA Ops:
  7.2 32.2 %all-gather.2.cloned.1.call-start = ((), (), s32[]{:S(2)}) async-start(), calls=%async_computation.9 | async-start | bytes 2359296 | tf_op jit(solution)/shard_map/all_gather | solution.py:543
  13.4 63.9 %all-to-all-start = ((bf16[32,2,16,2048]{3,2,1,0:T(8,128)(2,1)}), bf16[32,2,16,2048]{3,2,1,0:T(8,128)(2,1)}, u32[]{:S(2)}, u32[]{:S(2)}) async-start(bf16[32,2,16,2048]{3,2,1,0:T(8,128)(2,1)} %get-tuple-element.42), calls=%async_computation | async-start | bytes 8388608 | tf_op jit(solution)/shard_map/all_to_all | solution.py:495
  77.3 33.5 %all-to-all-start.1 = ((bf16[32,16,2048]{2,1,0:T(8,128)(2,1)}), bf16[32,16,2048]{2,1,0:T(8,128)(2,1)S(1)}, u32[]{:S(2)}, u32[]{:S(2)}) async-start(bf16[32,16,2048]{2,1,0:T(8,128)(2,1)} %bitcast.51), calls=%async_computation.1 | async-start | bytes 4194304 | tf_op jit(solution)/shard_map/all_to_all | solution.py:495
  110.8 1.3 copy-start
  112.1 33.8 %all-to-all-start.2 = ((bf16[32,16,2048]{2,1,0:T(8,128)(2,1)}), bf16[32,16,2048]{2,1,0:T(8,128)(2,1)}, u32[]{:S(2)}, u32[]{:S(2)}) async-start(bf16[32,16,2048]{2,1,0:T(8,128)(2,1)} %bitcast.13), calls=%async_computation.2 | async-start | bytes 4194304 | tf_op jit(solution)/shard_map/all_to_all | solution.py:495
  168.5 5.4 %collective-permute-start = (bf16[4,704,256]{2,1,0:T(8,128)(2,1)}, bf16[4,704,256]{2,1,0:T(8,128)(2,1)S(1)}, u32[]{:S(2)}, u32[]{:S(2)}) collective-permute-start(bf16[4,704,256]{2,1,0:T(8,128)(2,1)} %get-tuple-element.52), channel_id=1, source_target_pairs={{0,16},{16,0},{32,48},{48,32},{64,80},{80,64},{96,112},{112,96},{1... | collective-permute-start | bytes 4325384 | tf_op jit(solution)/shard_map/ppermute | solution.py:505
  169.3 33.0 %all-to-all-start.4 = ((bf16[32,16,2048]{2,1,0:T(8,128)(2,1)}), bf16[32,16,2048]{2,1,0:T(8,128)(2,1)}, u32[]{:S(2)}, u32[]{:S(2)}) async-start(bf16[32,16,2048]{2,1,0:T(8,128)(2,1)} %bitcast.16), calls=%async_computation.4 | async-start | bytes 4194304 | tf_op jit(solution)/shard_map/all_to_all | solution.py:495
  173.8 131.7 %reduce-scatter.8.cloned.1.call-start = ((), (), s32[]{:S(2)}) async-start(), calls=%async_computation.12 | async-start | bytes 3604480 | tf_op jit(solution)/shard_map/reduce_scatter | solution.py:579
  173.9 1.2 copy-start.1
  189.6 29.8 %collective-permute-start.1 = (bf16[4,704,256]{2,1,0:T(8,128)(2,1)}, bf16[4,704,256]{2,1,0:T(8,128)(2,1)}, u32[]{:S(2)}, u32[]{:S(2)}) collective-permute-start(bf16[4,704,256]{2,1,0:T(8,128)(2,1)} %get-tuple-element.60), channel_id=1, source_target_pairs={{0,16},{16,0},{32,48},{48,32},{64,80},{80,64},{96,112},{112,96},{1... | collective-permute-start | bytes 4325384 | tf_op jit(solution)/shard_map/ppermute | solution.py:505
  189.8 25.5 %collective-permute-start.2 = (bf16[4,704,256]{2,1,0:T(8,128)(2,1)}, bf16[4,704,256]{2,1,0:T(8,128)(2,1)}, u32[]{:S(2)}, u32[]{:S(2)}) collective-permute-start(bf16[4,704,256]{2,1,0:T(8,128)(2,1)} %get-tuple-element.62), channel_id=1, source_target_pairs={{0,16},{16,0},{32,48},{48,32},{64,80},{80,64},{96,112},{112,96},{1... | collective-permute-start | bytes 4325384 | tf_op jit(solution)/shard_map/ppermute | solution.py:505
  202.2 33.8 %all-to-all-start.5 = ((bf16[32,16,2048]{2,1,0:T(8,128)(2,1)}), bf16[32,16,2048]{2,1,0:T(8,128)(2,1)}, u32[]{:S(2)}, u32[]{:S(2)}) async-start(bf16[32,16,2048]{2,1,0:T(8,128)(2,1)} %bitcast.18), calls=%async_computation.5 | async-start | bytes 4194304 | tf_op jit(solution)/shard_map/all_to_all | solution.py:495
  207.5 98.1 %reduce-scatter.6.cloned.1.call-start = ((), (), s32[]{:S(2)}) async-start(), calls=%async_computation.11 | async-start | bytes 3604480 | tf_op jit(solution)/shard_map/reduce_scatter | solution.py:579
  236.0 61.2 %all-to-all-start.3 = ((bf16[32,2,16,2048]{3,2,1,0:T(8,128)(2,1)}), bf16[32,2,16,2048]{3,2,1,0:T(8,128)(2,1)}, u32[]{:S(2)}, u32[]{:S(2)}) async-start(bf16[32,2,16,2048]{3,2,1,0:T(8,128)(2,1)} %shard_map.174), calls=%async_computation.3 | async-start | bytes 8388608 | tf_op jit(solution)/shard_map/all_to_all | solution.py:495
  241.4 64.2 %reduce-scatter.4.cloned.1.call-start = ((), (), s32[]{:S(2)}) async-start(), calls=%async_computation.10 | async-start | bytes 3604480 | tf_op jit(solution)/shard_map/reduce_scatter | solution.py:579
  256.2 3.0 copy-start.2
  256.2 3.0 collective-permute-start.3
  259.2 44.2 %copy-start.3 = (bf16[4,128,1024]{2,1,0:T(8,128)(2,1)}, bf16[4,128,1024]{2,1,0:T(8,128)(2,1)S(1)}, u32[]{:S(2)}) copy-start(bf16[4,128,1024]{2,1,0:T(8,128)(2,1)S(1)} %collective-permute-done.3) | copy-start | bytes 3145732
  260.4 42.9 %collective-permute-start.4 = (bf16[128,1024]{1,0:T(8,128)(2,1)}, bf16[128,1024]{1,0:T(8,128)(2,1)}, u32[]{:S(2)}, u32[]{:S(2)}) collective-permute-start(bf16[128,1024]{1,0:T(8,128)(2,1)} %get-tuple-element.71), channel_id=1, source_target_pairs={{96,0},{112,16},{97,1},{113,17},{98,2},{114,18},{99,3},{115,19},{1... | collective-permute-start | bytes 786440 | tf_op jit(solution)/shard_map/ppermute | solution.py:514
  261.7 41.6 %collective-permute-start.6 = (bf16[128,1024]{1,0:T(8,128)(2,1)}, bf16[128,1024]{1,0:T(8,128)(2,1)}, u32[]{:S(2)}, u32[]{:S(2)}) collective-permute-start(bf16[128,1024]{1,0:T(8,128)(2,1)} %get-tuple-element.72), channel_id=1, source_target_pairs={{32,0},{48,16},{64,32},{80,48},{96,64},{112,80},{33,1},{49,17},{65... | collective-permute-start | bytes 786440 | tf_op jit(solution)/shard_map/ppermute | solution.py:514
  263.0 40.4 %collective-permute-start.5 = (bf16[128,1024]{1,0:T(8,128)(2,1)}, bf16[128,1024]{1,0:T(8,128)(2,1)}, u32[]{:S(2)}, u32[]{:S(2)}) collective-permute-start(bf16[128,1024]{1,0:T(8,128)(2,1)} %get-tuple-element.73), channel_id=1, source_target_pairs={{64,0},{80,16},{96,32},{112,48},{65,1},{81,17},{97,33},{113,49},{6... | collective-permute-start | bytes 786440 | tf_op jit(solution)/shard_map/ppermute | solution.py:514
Sparse Core Ops, SparseCore 0:
  10.3 28.9 all-gather.1
  179.3 38.2 reduce-scatter.7
  223.7 38.3 reduce-scatter.5
  264.9 37.5 reduce-scatter.3

commit v3 on v2

--- a/solution.py
+++ b/solution.py
@@ -239,6 +239,90 @@
             transcendentals=PART * HIDDEN,
         ),
     )(core, rows, pairs, gate_w, up_w, down_w)
+
+
+def forward_kernel(core, rows, gate_w, up_w, gate_out, up_out, act_out):
+    gate = dot_nt(rows[...], gate_w[0])
+    up = dot_nt(rows[...], up_w[0])
+    gate_out[...] = gate
+    up_out[...] = up
+    act_out[...] = (gate * jax.nn.sigmoid(gate) * up).astype(bf16)
+
+
+def backward_kernel(core, gate_in, up_in, pairs, gate_w, up_w, down_w, back_out, gate_out, up_out):
+    step = gate_in.shape[0]
+    gate, up = gate_in[...], up_in[...]
+    sig = jax.nn.sigmoid(gate)
+    act_grad = dot_nt(pairs[...].reshape(step, WIDTH), down_w[0])
+    gate_grad = (act_grad * up * sig * (1.0 + gate * (1.0 - sig))).astype(bf16)
+    up_grad = (act_grad * gate * sig).astype(bf16)
+    gate_out[...] = gate_grad
+    up_out[...] = up_grad
+    back_out[...] = (dot_nn(gate_grad, gate_w[0]) + dot_nn(up_grad, up_w[0])).astype(bf16)
+
+
+def expert_forward(core, rows, gate_w, up_w):
+    step = 256
+    thin = pl.BlockSpec((step, HIDDEN), lambda i, c: (i, 0))
+    weight = pl.BlockSpec(
+        (1, HIDDEN, WIDTH), lambda i, c: (c[0], 0, 0), pipeline_mode=pl.Buffered(1)
+    )
+    return pl.pallas_call(
+        forward_kernel,
+        grid_spec=pltpu.PrefetchScalarGridSpec(
+            num_scalar_prefetch=1,
+            grid=(PART // step,),
+            in_specs=[pl.BlockSpec((step, WIDTH), lambda i, c: (i, 0)), weight, weight],
+            out_specs=[thin, thin, thin],
+        ),
+        out_shape=(
+            jax.ShapeDtypeStruct((PART, HIDDEN), f32),
+            jax.ShapeDtypeStruct((PART, HIDDEN), f32),
+            jax.ShapeDtypeStruct((PART, HIDDEN), bf16),
+        ),
+        compiler_params=params(),
+        cost_estimate=cost(100,
+            flops=4 * PART * HIDDEN * WIDTH,
+            bytes_accessed=10 << 20,
+            transcendentals=PART * HIDDEN,
+        ),
+    )(core, rows, gate_w, up_w)
+
+
+def expert_backward(half, core, gate, up, pairs, gate_w, up_w, down_w):
+    step = 256
+    tile = pl.BlockSpec((step, WIDTH), lambda i, c: (i, 0))
+    thin = pl.BlockSpec((step, HIDDEN), lambda i, c: (i, 0))
+    weight = pl.BlockSpec(
+        (1, HIDDEN, WIDTH), lambda i, c: (c[0], 0, 0), pipeline_mode=pl.Buffered(1)
+    )
+    return pl.pallas_call(
+        backward_kernel,
+        grid_spec=pltpu.PrefetchScalarGridSpec(
+            num_scalar_prefetch=1,
+            grid=(PART // step,),
+            in_specs=[
+                thin,
+                thin,
+                pl.BlockSpec((step // HALF, 1, HALF, WIDTH), lambda i, c: (i, half, 0, 0)),
+                weight,
+                weight,
+                weight,
+            ],
+            out_specs=[tile, thin, thin],
+        ),
+        out_shape=(
+            jax.ShapeDtypeStruct((PART, WIDTH), bf16),
+            jax.ShapeDtypeStruct((PART, HIDDEN), bf16),
+            jax.ShapeDtypeStruct((PART, HIDDEN), bf16),
+        ),
+        compiler_params=params(),
+        cost_estimate=cost(100,
+            flops=6 * PART * HIDDEN * WIDTH,
+            bytes_accessed=16 << 20,
+            transcendentals=PART * HIDDEN,
+        ),
+    )(core, gate, up, pairs, gate_w, up_w, down_w)
 
 
 def split_columns(place, total, value, keep_out, send_out):
@@ -445,33 +529,57 @@
     )(seq_index, queries, pairs, pairs, lse, back_a, back_b, pick, residual, att, grad)
 
 
-def combine_kernel(routes, pick, mixed, returned, residual, att, grad, layer_out, mix_out):
+def combine_kernel(
+    routes, pick, mixed, returned, residual, att, grad, layer_out, mix_out, by_expert
+):
+    step = pl.program_id(0)
+
+    @pl.when(step == 0)
+    def _():
+        by_expert[...] = jnp.zeros_like(by_expert)
+
     total = residual[...].astype(f32) + att[...].astype(f32)
-    by_expert = jnp.zeros((EXPERTS, TOK), f32)
     for h in range(2):
-        rows = returned[:, h].reshape(PART, WIDTH)
+        rows = returned[:, h].reshape(PART, -1)
         coarse = mixed[h].astype(bf16)
         fine = (mixed[h] - coarse.astype(f32)).astype(bf16)
         total = total + dot_tn(coarse, rows) + dot_tn(fine, rows)
         inner = dot_nt(rows, grad[...]) * pick[h].astype(f32)
-        by_expert = by_expert + jnp.sum(inner.reshape(EXPERTS, HALF, TOK), axis=1)
+        by_expert[...] += jnp.sum(inner.reshape(EXPERTS, HALF, TOK), axis=1)
     layer_out[...] = total.astype(bf16)
-    ids = expert_ids()
-    for c in range(TOP):
-        hit = routes[c] == ids
-        mix_out[c] = jnp.sum(jnp.where(hit, by_expert, 0.0), axis=0, keepdims=True)
+
+    @pl.when(step == pl.num_programs(0) - 1)
+    def _():
+        ids = expert_ids()
+        for c in range(TOP):
+            hit = routes[c] == ids
+            mix_out[c] = jnp.sum(jnp.where(hit, by_expert[...], 0.0), axis=0, keepdims=True)
 
 
 def combine(routes, pick, mixed, returned, residual, att, grad):
+    part = WIDTH // 4
+    columns = pl.BlockSpec((TOK, part), lambda i: (0, i))
     return pl.pallas_call(
         combine_kernel,
+        grid=(4,),
+        in_specs=[
+            whole((TOP, 1, TOK)),
+            whole((2, PART, TOK)),
+            whole((2, PART, TOK)),
+            pl.BlockSpec((EXPERTS, 2, HALF, part), lambda i: (0, 0, 0, i)),
+            columns,
+            columns,
+            columns,
+        ],
+        out_specs=[columns, whole((TOP, 1, TOK))],
         out_shape=(
             jax.ShapeDtypeStruct((TOK, WIDTH), bf16),
             jax.ShapeDtypeStruct((TOP, 1, TOK), f32),
         ),
-        compiler_params=params(),
-        cost_estimate=cost(100,
-            flops=6 * ROWS * TOK * WIDTH, bytes_accessed=8 << 20, transcendentals=0
+        scratch_shapes=[pltpu.VMEM((EXPERTS, TOK), f32)],
+        compiler_params=params(),
+        cost_estimate=cost(
+            100, flops=6 * ROWS * TOK * WIDTH, bytes_accessed=8 << 20, transcendentals=0
         ),
     )(routes, pick, mixed, returned, residual, att, grad)
 
@@ -545,14 +653,18 @@
     grad_rows = exchange(grad_rows)
     att, lse, rows_a, rows_b = attend(seq_index, queries, pairs, residual, pick)
     rows_a, rows_b = after(grad_rows, rows_a, rows_b)
-    rows_a, rows_b = exchange_rows(rows_a), exchange_rows(rows_b)
+    rows_a = exchange_rows(rows_a)
+    (rows_b,) = after(rows_a, rows_b)
+    rows_b = exchange_rows(rows_b)
     weights = (gate_w, up_w, down_weight)
     back_a, act_a, gate_a, up_a = expert_rows(0, core_index, rows_a, grad_rows, *weights)
     back_a = exchange_rows(back_a)
-    back_b, act_b, gate_b, up_b = expert_rows(1, core_index, rows_b, grad_rows, *weights)
-    back_b = exchange_rows(back_b)
+    gate_pre, up_pre, act_b = expert_forward(core_index, rows_b, gate_w, up_w)
     down_keep, down_send = column_sums(down_kernel, 2, core_index, (grad_rows,), (act_a, act_b))
     down_stack = stack_experts(core_index, down_keep, swap_cores(down_send))
+    (gate_pre,) = after(down_stack, gate_pre)
+    back_b, gate_b, up_b = expert_backward(1, core_index, gate_pre, up_pre, grad_rows, *weights)
+    back_b = exchange_rows(back_b)
     gate_a, gate_b = after(down_stack, gate_a, gate_b)
     gate_keep, gate_send, up_keep, up_send = column_sums(
         inner_kernel, 4, core_index, (rows_a, rows_b), (gate_a, gate_b, up_a, up_b)

time: 313 us -> 308 us (0.984)
  waiting for transfers between devices: 145 us -> 133 us
  Pallas kernels: 105 us -> 110 us
    pallas_call x1 -> x3, Pallas kernels: 6.1 us -> 26.2 us  [the longest x1 12.3 us: expert_backward(): pl.pallas_call(backward_kernel, grid_spec=pltpu.PrefetchScalarGridSpec(nu...]
    pallas_call x2 -> x1, Pallas kernels: 30.7 us -> 15.4 us  [expert_rows(): pl.pallas_call(expert_kernel, grid_spec=pltpu.PrefetchScalarGridSpec(num_...]
    all_to_all x6, waiting for transfers between devices: 125 us -> 113 us  [exchange(): lax.all_to_all(blocks, ('seq', 'expert'), 0, 0, tiled=True, axis_index_gr...]
  transfers between devices with their start and end apart: 17 -> 17, of which waited for: 8 -> 7; matrix products, arithmetic and copies ran while one was open for 1% -> 1% of each run, Pallas kernels for 26% -> 31%
where the time goes in v3:
time: 308 us; the launch traced here: 307 us
  waiting for transfers between devices  133 us (43%)
  Pallas kernels  110 us (36%)
  starting transfers between devices  42.2 us (14%)
  between operations  13.9 us (5%)
  other arithmetic  4.44 us (1%)
  local copies, waits for them, and re-layouts  3.2 us (1%)
    all_to_all x6, waiting for transfers between devices, exchange(): lax.all_to_all(blocks, ('seq', 'expert'), 0, 0, tiled=True, axis_index_gr...  113 us
    all_to_all x6, starting transfers between devices, exchange(): lax.all_to_all(blocks, ('seq', 'expert'), 0, 0, tiled=True, axis_index_gr...  36.4 us
    pallas_call x2, Pallas kernels, column_sums(): pl.pallas_call(kernel, grid_spec=pltpu.PrefetchScalarGridSpec(num_scalar_...  17.5 us
    all_gather x1, waiting for transfers between devices, on_device(): pairs = lax.all_gather(pairs, 'seq', axis=0, tiled=True)  17.2 us
    pallas_call x1, Pallas kernels, expert_rows(): pl.pallas_call(expert_kernel, grid_spec=pltpu.PrefetchScalarGridSpec(num_...  15.4 us
    pallas_call x1, Pallas kernels, attend_back(): pl.pallas_call(attend_back_kernel, grid_spec=pltpu.PrefetchScalarGridSpec...  14.8 us
    pallas_call x1, Pallas kernels, expert_backward(): pl.pallas_call(backward_kernel, grid_spec=pltpu.PrefetchScalarGridSpec(nu...  12.3 us
    pallas_call x3, Pallas kernels, stack_experts(): pl.pallas_call(stack_kernel, grid_spec=pltpu.PrefetchScalarGridSpec(num_s...  12.2 us
  transfers between devices with their start and end apart: 17, of which 7 were waited for; matrix products, arithmetic and copies ran while one was open for 1% of the time, Pallas kernels for 31%

profile of v3, /device:TPU:1, one launch (start us, length us, event | category | flops | bytes accessed | tf_op | source)
XLA Modules:
  0.0 306.9 jit_solution(2345978147248127418)
XLA Ops:
  7.2 0.0 all-gather.2.cloned.1.call-start
  7.2 1.7 pad_maximum_fusion
  8.9 0.0 all-gather.2.cloned.1.call-update
  8.9 4.6 %shard_map.169 = (bf16[2,512,128]{2,1,0:T(8,128)(2,1)}, f32[2,512,128]{2,1,0:T(8,128)}, bf16[32,2,16,2048]{3,2,1,0:T(8,128)(2,1)}) custom-call(s32[6,1,128]{2,1,0:T(1,128)} %bitcast.76, f32[6,1,128]{2,1,0:T(1,128)} %bitcast.75, bf16[128,2048]{1,0:T(8,128)(2,1)} %bitcast.69), custom_call_target="tpu_custom_call" | custom-call | flops 2684354560 | bytes 41943040 | tf_op jit(solution)/shard_map/pallas_call | solution.py:104
  13.5 8.6 %all-to-all-start = ((bf16[32,2,16,2048]{3,2,1,0:T(8,128)(2,1)}), bf16[32,2,16,2048]{3,2,1,0:T(8,128)(2,1)}, u32[]{:S(2)}, u32[]{:S(2)}) async-start(bf16[32,2,16,2048]{3,2,1,0:T(8,128)(2,1)} %get-tuple-element.44), calls=%async_computation | async-start | bytes 8388608 | tf_op jit(solution)/shard_map/all_to_all | solution.py:603
  22.2 17.2 %all-gather.2.cloned.1.call-done.k_ref.v_ref = bf16[1024,1024]{1,0:T(8,128)(2,1)} async-done(((bf16[128,1024]{1,0:T(8,128)(2,1)}), bf16[1024,1024]{1,0:T(8,128)(2,1)}) %all-gather.2.cloned.1.call-update) | async-done | bytes 2097168 | tf_op jit(solution)/shard_map/all_gather | solution.py:651
  39.3 11.7 %shard_map.170 = (bf16[128,2048]{1,0:T(8,128)(2,1)}, f32[128,2048]{1,0:T(8,128)}, bf16[512,2048]{1,0:T(8,128)(2,1)}, bf16[512,2048]{1,0:T(8,128)(2,1)}) custom-call(s32[1]{0:T(128)} %bitcast.4.seq_ref, bf16[128,2048]{1,0:T(8,128)(2,1)} %bitcast.67, bf16[1024,1024]{1,0:T(8,128)(2,1)} %all-gather.2.cloned.1.call-done.k_ref.v_ref, ...), custom_call_target="tpu_custom_call" | custom-call | flops 8053063680 | bytes 52428800 | tf_op jit(solution)/shard_map/pallas_call | solution.py:159
  51.1 26.4 %all-to-all-done.refs_0_.pairs = bf16[32,2,16,2048]{3,2,1,0:T(8,128)(2,1)} async-done(((bf16[32,2,16,2048]{3,2,1,0:T(8,128)(2,1)}), bf16[32,2,16,2048]{3,2,1,0:T(8,128)(2,1)}, u32[]{:S(2)}, u32[]{:S(2)}) %all-to-all-start) | async-done | bytes 4194336 | tf_op jit(solution)/shard_map/all_to_all | solution.py:603
  77.4 5.1 %all-to-all-start.1 = ((bf16[32,16,2048]{2,1,0:T(8,128)(2,1)}), bf16[32,16,2048]{2,1,0:T(8,128)(2,1)S(1)}, u32[]{:S(2)}, u32[]{:S(2)}) async-start(bf16[32,16,2048]{2,1,0:T(8,128)(2,1)} %bitcast.55), calls=%async_computation.1 | async-start | bytes 4194304 | tf_op jit(solution)/shard_map/all_to_all | solution.py:603
  82.5 28.4 %all-to-all-done.1 = bf16[32,16,2048]{2,1,0:T(8,128)(2,1)S(1)} async-done(((bf16[32,16,2048]{2,1,0:T(8,128)(2,1)}), bf16[32,16,2048]{2,1,0:T(8,128)(2,1)S(1)}, u32[]{:S(2)}, u32[]{:S(2)}) %all-to-all-start.1) | async-done | bytes 2097184 | tf_op jit(solution)/shard_map/all_to_all | solution.py:603
  110.9 0.0 copy-start
  110.9 1.3 copy-done
  112.2 5.3 %all-to-all-start.2 = ((bf16[32,16,2048]{2,1,0:T(8,128)(2,1)}), bf16[32,16,2048]{2,1,0:T(8,128)(2,1)}, u32[]{:S(2)}, u32[]{:S(2)}) async-start(bf16[32,16,2048]{2,1,0:T(8,128)(2,1)} %bitcast.51), calls=%async_computation.2 | async-start | bytes 4194304 | tf_op jit(solution)/shard_map/all_to_all | solution.py:603
  117.5 15.4 %shard_map.172 = (bf16[512,2048]{1,0:T(8,128)(2,1)}, bf16[512,704]{1,0:T(8,128)(2,1)}, bf16[512,704]{1,0:T(8,128)(2,1)}, bf16[512,704]{1,0:T(8,128)(2,1)}) custom-call(s32[1]{0:T(128)} %bitcast.3.core, bf16[512,2048]{1,0:T(8,128)(2,1)} %bitcast.53, bf16[32,2,16,2048]{3,2,1,0:T(8,128)(2,1)} %all-to-all-done.refs_0_.pairs, bf16[2,704,2048]{2,1,0:T(8,128)(2,1)} %bitcast.58, ...), custom_call_target="tpu_custom_call" | custom-call | flops 738197504000 | bytes 1677721600 | tf_op jit(solution)/shard_map/pallas_call | solution.py:215
  132.9 13.1 %all-to-all-done.2 = bf16[32,16,2048]{2,1,0:T(8,128)(2,1)} async-done(((bf16[32,16,2048]{2,1,0:T(8,128)(2,1)}), bf16[32,16,2048]{2,1,0:T(8,128)(2,1)}, u32[]{:S(2)}, u32[]{:S(2)}) %all-to-all-start.2) | async-done | bytes 2097184 | tf_op jit(solution)/shard_map/all_to_all | solution.py:603
  146.0 7.7 %shard_map.174 = (f32[512,704]{1,0:T(8,128)}, f32[512,704]{1,0:T(8,128)}, bf16[512,704]{1,0:T(8,128)(2,1)}) custom-call(s32[1]{0:T(128)} %bitcast.3.core, bf16[512,2048]{1,0:T(8,128)(2,1)} %bitcast.14.rows.rows_b, bf16[2,704,2048]{2,1,0:T(8,128)(2,1)} %bitcast.59, bf16[2,704,2048]{2,1,0:T(8,128)(2,1)} %bitcast.62), custom_call_target="tpu_custom_call" | custom-call | flops 295279001600 | bytes 1048576000 | tf_op jit(solution)/shard_map/pallas_call | solution.py:270
  153.7 7.2 %shard_map.177 = (bf16[4,704,256]{2,1,0:T(8,128)(2,1)}, bf16[4,704,256]{2,1,0:T(8,128)(2,1)}) custom-call(s32[1]{0:T(128)} %bitcast.3.core, bf16[32,2,16,2048]{3,2,1,0:T(8,128)(2,1)} %all-to-all-done.refs_0_.pairs, bf16[512,704]{1,0:T(8,128)(2,1)} %get-tuple-element.48.act_a, bf16[512,704]{1,0:T(8,128)(2,1)} %get-tuple-element.50.act_b), custom_call_target="tpu_custom_call" | custom-call | flops 295279001600 | bytes 838860800 | tf_op jit(solution)/shard_map/pallas_call | solution.py:360
  160.9 0.8 collective-permute-start
  161.7 4.5 %all-to-all-start.4 = ((bf16[32,16,2048]{2,1,0:T(8,128)(2,1)}), bf16[32,16,2048]{2,1,0:T(8,128)(2,1)}, u32[]{:S(2)}, u32[]{:S(2)}) async-start(bf16[32,16,2048]{2,1,0:T(8,128)(2,1)} %bitcast.16), calls=%async_computation.4 | async-start | bytes 4194304 | tf_op jit(solution)/shard_map/all_to_all | solution.py:603
  166.3 0.0 reduce-scatter.8.cloned.1.call-start
  166.3 0.0 collective-permute-done.other
  166.3 0.0 copy-start.1
  166.3 1.1 copy-done.1
  167.5 4.1 %shard_map.178.refs_0_ = bf16[4,2,704,256]{3,2,1,0:T(8,128)(2,1)} custom-call(s32[1]{0:T(128)} %bitcast.3.core, bf16[4,704,256]{2,1,0:T(8,128)(2,1)} %get-tuple-element.53.keep, bf16[4,704,256]{2,1,0:T(8,128)(2,1)} %copy-done.1), custom_call_target="tpu_custom_call" | custom-call | bytes 629145600 | tf_op jit(solution)/shard_map/pallas_call | solution.py:386
  171.5 0.0 reduce-scatter.8.cloned.1.call-update
  171.6 12.3 %shard_map.180 = (bf16[512,2048]{1,0:T(8,128)(2,1)}, bf16[512,704]{1,0:T(8,128)(2,1)}, bf16[512,704]{1,0:T(8,128)(2,1)}) custom-call(s32[1]{0:T(128)} %bitcast.3.core, f32[512,704]{1,0:T(8,128)} %shard_map.179.gate_in, f32[512,704]{1,0:T(8,128)} %get-tuple-element.57.up_in, bf16[32,2,16,2048]{3,2,1,0:T(8,128)(2,1)} %all-to-all-done.refs_0_.pairs, ...), custom_call_target="tpu_custom_call" | custom-call | flops 442918502400 | bytes 1677721600 | tf_op jit(solution)/shard_map/pallas_call | solution.py:299
  183.9 10.4 %shard_map.182 = (bf16[4,704,256]{2,1,0:T(8,128)(2,1)}, bf16[4,704,256]{2,1,0:T(8,128)(2,1)}, bf16[4,704,256]{2,1,0:T(8,128)(2,1)}, bf16[4,704,256]{2,1,0:T(8,128)(2,1)}) custom-call(s32[1]{0:T(128)} %bitcast.3.core, bf16[512,2048]{1,0:T(8,128)(2,1)} %bitcast.54, bf16[512,2048]{1,0:T(8,128)(2,1)} %bitcast.14.rows.rows_b, ...), custom_call_target="tpu_custom_call" | custom-call | flops 590558003200 | bytes 1677721600 | tf_op jit(solution)/shard_map/pallas_call | solution.py:360
  194.2 0.2 collective-permute-start.1
  194.5 0.3 collective-permute-start.2
  194.8 0.0 all-to-all-done.4
  194.8 7.5 %all-to-all-start.5 = ((bf16[32,16,2048]{2,1,0:T(8,128)(2,1)}), bf16[32,16,2048]{2,1,0:T(8,128)(2,1)}, u32[]{:S(2)}, u32[]{:S(2)}) async-start(bf16[32,16,2048]{2,1,0:T(8,128)(2,1)} %bitcast.18), calls=%async_computation.5 | async-start | bytes 4194304 | tf_op jit(solution)/shard_map/all_to_all | solution.py:603
  202.3 0.0 reduce-scatter.6.cloned.1.call-start
  202.3 7.5 %shard_map.175 = bf16[32,2,16,2048]{3,2,1,0:T(8,128)(2,1)} custom-call(s32[1]{0:T(128)} %bitcast.3.core, bf16[512,704]{1,0:T(8,128)(2,1)} %get-tuple-element.48.act_a, bf16[512,704]{1,0:T(8,128)(2,1)} %get-tuple-element.50.act_b, bf16[2,704,2048]{2,1,0:T(8,128)(2,1)} %down_w.5), custom_call_target="tpu_custom_call" | custom-call | flops 295279001600 | bytes 943718400 | tf_op jit(solution)/shard_map/pallas_call | solution.py:408
  209.9 0.0 collective-permute-done.2.other
  209.9 4.1 %shard_map.184.refs_0_ = bf16[4,2,704,256]{3,2,1,0:T(8,128)(2,1)} custom-call(s32[1]{0:T(128)} %bitcast.3.core, bf16[4,704,256]{2,1,0:T(8,128)(2,1)} %get-tuple-element.65.keep, bf16[4,704,256]{2,1,0:T(8,128)(2,1)} %collective-permute-done.2.other), custom_call_target="tpu_custom_call" | custom-call | bytes 629145600 | tf_op jit(solution)/shard_map/pallas_call | solution.py:386
  213.9 0.0 collective-permute-done.1.other
  214.0 4.1 %shard_map.183.refs_0_ = bf16[4,2,704,256]{3,2,1,0:T(8,128)(2,1)} custom-call(s32[1]{0:T(128)} %bitcast.3.core, bf16[4,704,256]{2,1,0:T(8,128)(2,1)} %get-tuple-element.63.keep, bf16[4,704,256]{2,1,0:T(8,128)(2,1)} %collective-permute-done.1.other), custom_call_target="tpu_custom_call" | custom-call | bytes 629145600 | tf_op jit(solution)/shard_map/pallas_call | solution.py:386
  218.0 0.0 reduce-scatter.6.cloned.1.call-update
  218.1 12.6 %all-to-all-done.5 = bf16[32,16,2048]{2,1,0:T(8,128)(2,1)} async-done(((bf16[32,16,2048]{2,1,0:T(8,128)(2,1)}), bf16[32,16,2048]{2,1,0:T(8,128)(2,1)}, u32[]{:S(2)}, u32[]{:S(2)}) %all-to-all-start.5) | async-done | bytes 2097184 | tf_op jit(solution)/shard_map/all_to_all | solution.py:603
  230.7 5.4 %all-to-all-start.3 = ((bf16[32,2,16,2048]{3,2,1,0:T(8,128)(2,1)}), bf16[32,2,16,2048]{3,2,1,0:T(8,128)(2,1)}, u32[]{:S(2)}, u32[]{:S(2)}) async-start(bf16[32,2,16,2048]{3,2,1,0:T(8,128)(2,1)} %shard_map.175), calls=%async_computation.3 | async-start | bytes 8388608 | tf_op jit(solution)/shard_map/all_to_all | solution.py:603
  236.1 0.0 reduce-scatter.4.cloned.1.call-start
  236.1 14.8 %shard_map.187 = (bf16[128,2048]{1,0:T(8,128)(2,1)}, bf16[128,2048]{1,0:T(8,128)(2,1)}, bf16[4,128,1024]{2,1,0:T(8,128)(2,1)}, bf16[4,128,1024]{2,1,0:T(8,128)(2,1)}) custom-call(s32[1]{0:T(128)} %bitcast.4.seq_ref, bf16[128,2048]{1,0:T(8,128)(2,1)} %bitcast.68, bf16[1024,1024]{1,0:T(8,128)(2,1)} %all-gather.2.cloned.1.call-done.k_ref.v_ref, ...), custom_call_target="tpu_custom_call" | custom-call | flops 322122547200 | bytes 1258291200 | tf_op jit(solution)/shard_map/pallas_call | solution.py:492
  250.9 0.0 copy-start.2
  250.9 0.4 collective-permute-start.3
  251.3 0.0 reduce-scatter.4.cloned.1.call-update
  251.3 2.5 collective-permute-done.3
  253.9 0.0 copy-start.3
  253.9 0.0 copy-done.2
  253.9 1.3 fusion.4
  255.2 1.3 collective-permute-start.4
  256.4 1.3 collective-permute-start.6
  257.7 1.3 collective-permute-start.5
  259.0 32.9 %all-to-all-done.3.returned = bf16[32,2,16,2048]{3,2,1,0:T(8,128)(2,1)} async-done(((bf16[32,2,16,2048]{3,2,1,0:T(8,128)(2,1)}), bf16[32,2,16,2048]{3,2,1,0:T(8,128)(2,1)}, u32[]{:S(2)}, u32[]{:S(2)}) %all-to-all-start.3) | async-done | bytes 4194336 | tf_op jit(solution)/shard_map/all_to_all | solution.py:603
  291.9 6.2 %shard_map.176 = (bf16[128,2048]{1,0:T(8,128)(2,1)}, f32[6,1,128]{2,1,0:T(1,128)}) custom-call(s32[6,1,128]{2,1,0:T(1,128)} %bitcast.77, bf16[2,512,128]{2,1,0:T(8,128)(2,1)} %get-tuple-element.42.pick, f32[2,512,128]{2,1,0:T(8,128)} %get-tuple-element.43.mixed, bf16[32,2,16,2048]{3,2,1,0:T(8,128)(2,1)} %all-to-all-done.3.returned, ...), custom_call_target="tpu_custom_call" | custom-call | flops 161061273600 | bytes 838860800 | tf_op jit(solution)/shard_map/pallas_call | solution.py:562
  298.1 0.0 copy-done.3
  298.1 0.0 collective-permute-done.4
  298.1 0.0 collective-permute-done.6
  298.1 0.0 collective-permute-done.5
  298.1 1.5 fusion.2
  299.6 0.7 slice_bitcast_fusion
  300.3 0.0 reduce-scatter.8.cloned.1.call-done
  300.3 0.0 reduce-scatter.6.cloned.1.call-done
  300.3 0.0 reduce-scatter.4.cloned.1.call-done
  (6 shorter events, 0.0 us)
Async XLA Ops:
  7.2 32.2 %all-gather.2.cloned.1.call-start = ((), (), s32[]{:S(2)}) async-start(), calls=%async_computation.9 | async-start | bytes 2359296 | tf_op jit(solution)/shard_map/all_gather | solution.py:651
  13.5 63.9 %all-to-all-start = ((bf16[32,2,16,2048]{3,2,1,0:T(8,128)(2,1)}), bf16[32,2,16,2048]{3,2,1,0:T(8,128)(2,1)}, u32[]{:S(2)}, u32[]{:S(2)}) async-start(bf16[32,2,16,2048]{3,2,1,0:T(8,128)(2,1)} %get-tuple-element.44), calls=%async_computation | async-start | bytes 8388608 | tf_op jit(solution)/shard_map/all_to_all | solution.py:603
  77.4 33.5 %all-to-all-start.1 = ((bf16[32,16,2048]{2,1,0:T(8,128)(2,1)}), bf16[32,16,2048]{2,1,0:T(8,128)(2,1)S(1)}, u32[]{:S(2)}, u32[]{:S(2)}) async-start(bf16[32,16,2048]{2,1,0:T(8,128)(2,1)} %bitcast.55), calls=%async_computation.1 | async-start | bytes 4194304 | tf_op jit(solution)/shard_map/all_to_all | solution.py:603
  110.9 1.4 copy-start
  112.2 33.8 %all-to-all-start.2 = ((bf16[32,16,2048]{2,1,0:T(8,128)(2,1)}), bf16[32,16,2048]{2,1,0:T(8,128)(2,1)}, u32[]{:S(2)}, u32[]{:S(2)}) async-start(bf16[32,16,2048]{2,1,0:T(8,128)(2,1)} %bitcast.51), calls=%async_computation.2 | async-start | bytes 4194304 | tf_op jit(solution)/shard_map/all_to_all | solution.py:603
  160.9 5.4 %collective-permute-start = (bf16[4,704,256]{2,1,0:T(8,128)(2,1)}, bf16[4,704,256]{2,1,0:T(8,128)(2,1)S(1)}, u32[]{:S(2)}, u32[]{:S(2)}) collective-permute-start(bf16[4,704,256]{2,1,0:T(8,128)(2,1)} %get-tuple-element.54), channel_id=1, source_target_pairs={{0,16},{16,0},{32,48},{48,32},{64,80},{80,64},{96,112},{112,96},{1... | collective-permute-start | bytes 4325384 | tf_op jit(solution)/shard_map/ppermute | solution.py:613
  161.7 33.0 %all-to-all-start.4 = ((bf16[32,16,2048]{2,1,0:T(8,128)(2,1)}), bf16[32,16,2048]{2,1,0:T(8,128)(2,1)}, u32[]{:S(2)}, u32[]{:S(2)}) async-start(bf16[32,16,2048]{2,1,0:T(8,128)(2,1)} %bitcast.16), calls=%async_computation.4 | async-start | bytes 4194304 | tf_op jit(solution)/shard_map/all_to_all | solution.py:603
  166.3 134.1 %reduce-scatter.8.cloned.1.call-start = ((), (), s32[]{:S(2)}) async-start(), calls=%async_computation.12 | async-start | bytes 3604480 | tf_op jit(solution)/shard_map/reduce_scatter | solution.py:691
  166.3 1.1 copy-start.1
  194.2 19.7 %collective-permute-start.1 = (bf16[4,704,256]{2,1,0:T(8,128)(2,1)}, bf16[4,704,256]{2,1,0:T(8,128)(2,1)}, u32[]{:S(2)}, u32[]{:S(2)}) collective-permute-start(bf16[4,704,256]{2,1,0:T(8,128)(2,1)} %get-tuple-element.64), channel_id=1, source_target_pairs={{0,16},{16,0},{32,48},{48,32},{64,80},{80,64},{96,112},{112,96},{1... | collective-permute-start | bytes 4325384 | tf_op jit(solution)/shard_map/ppermute | solution.py:613
  194.5 15.4 %collective-permute-start.2 = (bf16[4,704,256]{2,1,0:T(8,128)(2,1)}, bf16[4,704,256]{2,1,0:T(8,128)(2,1)}, u32[]{:S(2)}, u32[]{:S(2)}) collective-permute-start(bf16[4,704,256]{2,1,0:T(8,128)(2,1)} %get-tuple-element.66), channel_id=1, source_target_pairs={{0,16},{16,0},{32,48},{48,32},{64,80},{80,64},{96,112},{112,96},{1... | collective-permute-start | bytes 4325384 | tf_op jit(solution)/shard_map/ppermute | solution.py:613
  194.8 36.0 %all-to-all-start.5 = ((bf16[32,16,2048]{2,1,0:T(8,128)(2,1)}), bf16[32,16,2048]{2,1,0:T(8,128)(2,1)}, u32[]{:S(2)}, u32[]{:S(2)}) async-start(bf16[32,16,2048]{2,1,0:T(8,128)(2,1)} %bitcast.18), calls=%async_computation.5 | async-start | bytes 4194304 | tf_op jit(solution)/shard_map/all_to_all | solution.py:603
  202.3 98.1 %reduce-scatter.6.cloned.1.call-start = ((), (), s32[]{:S(2)}) async-start(), calls=%async_computation.11 | async-start | bytes 3604480 | tf_op jit(solution)/shard_map/reduce_scatter | solution.py:691
  230.7 61.2 %all-to-all-start.3 = ((bf16[32,2,16,2048]{3,2,1,0:T(8,128)(2,1)}), bf16[32,2,16,2048]{3,2,1,0:T(8,128)(2,1)}, u32[]{:S(2)}, u32[]{:S(2)}) async-start(bf16[32,2,16,2048]{3,2,1,0:T(8,128)(2,1)} %shard_map.175), calls=%async_computation.3 | async-start | bytes 8388608 | tf_op jit(solution)/shard_map/all_to_all | solution.py:603
  236.1 64.2 %reduce-scatter.4.cloned.1.call-start = ((), (), s32[]{:S(2)}) async-start(), calls=%async_computation.10 | async-start | bytes 3604480 | tf_op jit(solution)/shard_map/reduce_scatter | solution.py:691
  250.9 3.0 copy-start.2
  250.9 3.0 collective-permute-start.3
  253.9 44.2 %copy-start.3 = (bf16[4,128,1024]{2,1,0:T(8,128)(2,1)}, bf16[4,128,1024]{2,1,0:T(8,128)(2,1)S(1)}, u32[]{:S(2)}) copy-start(bf16[4,128,1024]{2,1,0:T(8,128)(2,1)S(1)} %collective-permute-done.3) | copy-start | bytes 3145732
  255.2 42.9 %collective-permute-start.4 = (bf16[128,1024]{1,0:T(8,128)(2,1)}, bf16[128,1024]{1,0:T(8,128)(2,1)}, u32[]{:S(2)}, u32[]{:S(2)}) collective-permute-start(bf16[128,1024]{1,0:T(8,128)(2,1)} %get-tuple-element.75), channel_id=1, source_target_pairs={{96,0},{112,16},{97,1},{113,17},{98,2},{114,18},{99,3},{115,19},{1... | collective-permute-start | bytes 786440 | tf_op jit(solution)/shard_map/ppermute | solution.py:622
  256.4 41.7 %collective-permute-start.6 = (bf16[128,1024]{1,0:T(8,128)(2,1)}, bf16[128,1024]{1,0:T(8,128)(2,1)}, u32[]{:S(2)}, u32[]{:S(2)}) collective-permute-start(bf16[128,1024]{1,0:T(8,128)(2,1)} %get-tuple-element.76), channel_id=1, source_target_pairs={{32,0},{48,16},{64,32},{80,48},{96,64},{112,80},{33,1},{49,17},{65... | collective-permute-start | bytes 786440 | tf_op jit(solution)/shard_map/ppermute | solution.py:622
  257.7 40.4 %collective-permute-start.5 = (bf16[128,1024]{1,0:T(8,128)(2,1)}, bf16[128,1024]{1,0:T(8,128)(2,1)}, u32[]{:S(2)}, u32[]{:S(2)}) collective-permute-start(bf16[128,1024]{1,0:T(8,128)(2,1)} %get-tuple-element.77), channel_id=1, source_target_pairs={{64,0},{80,16},{96,32},{112,48},{65,1},{81,17},{97,33},{113,49},{6... | collective-permute-start | bytes 786440 | tf_op jit(solution)/shard_map/ppermute | solution.py:622
Sparse Core Ops, SparseCore 0:
  10.3 28.9 all-gather.1
  171.7 38.2 reduce-scatter.7
  218.2 38.4 reduce-scatter.5
  259.5 37.7 reduce-scatter.3

commit v4 on v3

--- a/solution.py
+++ b/solution.py
@@ -109,7 +109,7 @@
             jax.ShapeDtypeStruct((EXPERTS, 2, HALF, WIDTH), bf16),
         ),
         compiler_params=params(),
-        cost_estimate=cost(5,
+        cost_estimate=cost(1,
             flops=2 * ROWS * TOK * WIDTH, bytes_accessed=8 << 20, transcendentals=0
         ),
     )(routes, mix, grad)
@@ -182,7 +182,7 @@
             jax.ShapeDtypeStruct((PART, WIDTH), bf16),
         ),
         compiler_params=params(),
-        cost_estimate=cost(5,
+        cost_estimate=cost(1,
             flops=4 * TOK * FULL * WIDTH + 2 * ROWS * TOK * WIDTH,
             bytes_accessed=10 << 20,
             transcendentals=HEADS * TOK * FULL,
@@ -578,8 +578,7 @@
         ),
         scratch_shapes=[pltpu.VMEM((EXPERTS, TOK), f32)],
         compiler_params=params(),
-        cost_estimate=cost(
-            100, flops=6 * ROWS * TOK * WIDTH, bytes_accessed=8 << 20, transcendentals=0
+        cost_estimate=cost(100, flops=6 * ROWS * TOK * WIDTH, bytes_accessed=8 << 20, transcendentals=0
         ),
     )(routes, pick, mixed, returned, residual, att, grad)
 

time: 308 us -> 306 us (level)
    all_to_all x6, waiting for transfers between devices: 113 us -> 99.5 us  [exchange(): lax.all_to_all(blocks, ('seq', 'expert'), 0, 0, tiled=True, axis_index_gr...]
    all_gather x1, waiting for transfers between devices: 17.2 us -> 30.1 us  [on_device(): pairs = lax.all_gather(pairs, 'seq', axis=0, tiled=True)]
  transfers between devices with their start and end apart: 17 -> 17, of which waited for: 7 -> 7; matrix products, arithmetic and copies ran while one was open for 1% -> 1% of each run, Pallas kernels for 31% -> 30%
where the time goes in v4:
time: 306 us; the launch traced here: 305 us
  waiting for transfers between devices  132 us (43%)
  Pallas kernels  110 us (36%)
  starting transfers between devices  42.3 us (14%)
  between operations  13.9 us (5%)
  other arithmetic  3.54 us (1%)
  local copies, waits for them, and re-layouts  3.16 us (1%)
    all_to_all x6, waiting for transfers between devices, exchange(): lax.all_to_all(blocks, ('seq', 'expert'), 0, 0, tiled=True, axis_index_gr...  99.5 us
    all_to_all x6, starting transfers between devices, exchange(): lax.all_to_all(blocks, ('seq', 'expert'), 0, 0, tiled=True, axis_index_gr...  36.6 us
    all_gather x1, waiting for transfers between devices, on_device(): pairs = lax.all_gather(pairs, 'seq', axis=0, tiled=True)  30.1 us
    pallas_call x2, Pallas kernels, column_sums(): pl.pallas_call(kernel, grid_spec=pltpu.PrefetchScalarGridSpec(num_scalar_...  17.6 us
    pallas_call x1, Pallas kernels, expert_rows(): pl.pallas_call(expert_kernel, grid_spec=pltpu.PrefetchScalarGridSpec(num_...  15.4 us
    pallas_call x1, Pallas kernels, attend_back(): pl.pallas_call(attend_back_kernel, grid_spec=pltpu.PrefetchScalarGridSpec...  14.8 us
    pallas_call x1, Pallas kernels, expert_backward(): pl.pallas_call(backward_kernel, grid_spec=pltpu.PrefetchScalarGridSpec(nu...  12.3 us
    pallas_call x3, Pallas kernels, stack_experts(): pl.pallas_call(stack_kernel, grid_spec=pltpu.PrefetchScalarGridSpec(num_s...  12.3 us
  transfers between devices with their start and end apart: 17, of which 7 were waited for; matrix products, arithmetic and copies ran while one was open for 1% of the time, Pallas kernels for 30%

profile of v4, /device:TPU:1, one launch (start us, length us, event | category | flops | bytes accessed | tf_op | source)
XLA Modules:
  0.0 305.2 jit_solution(15368162490614347793)
XLA Ops:
  7.2 4.5 %shard_map.169 = (bf16[2,512,128]{2,1,0:T(8,128)(2,1)}, f32[2,512,128]{2,1,0:T(8,128)}, bf16[32,2,16,2048]{3,2,1,0:T(8,128)(2,1)}) custom-call(s32[6,1,128]{2,1,0:T(1,128)} %bitcast.76, f32[6,1,128]{2,1,0:T(1,128)} %bitcast.75, bf16[128,2048]{1,0:T(8,128)(2,1)} %bitcast.69), custom_call_target="tpu_custom_call" | custom-call | flops 536870912 | bytes 8388608 | tf_op jit(solution)/shard_map/pallas_call | solution.py:104
  11.7 0.0 copy-start.4
  11.7 0.0 copy-start.5
  11.7 8.8 %all-to-all-start = ((bf16[32,2,16,2048]{3,2,1,0:T(8,128)(2,1)}), bf16[32,2,16,2048]{3,2,1,0:T(8,128)(2,1)}, u32[]{:S(2)}, u32[]{:S(2)}) async-start(bf16[32,2,16,2048]{3,2,1,0:T(8,128)(2,1)} %get-tuple-element.44), calls=%async_computation | async-start | bytes 8388608 | tf_op jit(solution)/shard_map/all_to_all | solution.py:602
  20.5 0.0 all-gather.2.cloned.1.call-start
  20.5 0.0 copy-done.4
  20.5 0.0 copy-done.5
  20.6 0.7 pad_maximum_fusion
  21.3 0.0 all-gather.2.cloned.1.call-update
  21.3 30.1 %all-gather.2.cloned.1.call-done.k_ref.v_ref = bf16[1024,1024]{1,0:T(8,128)(2,1)} async-done(((bf16[128,1024]{1,0:T(8,128)(2,1)}), bf16[1024,1024]{1,0:T(8,128)(2,1)}) %all-gather.2.cloned.1.call-update) | async-done | bytes 2097168 | tf_op jit(solution)/shard_map/all_gather | solution.py:650
  51.4 11.7 %shard_map.170 = (bf16[128,2048]{1,0:T(8,128)(2,1)}, f32[128,2048]{1,0:T(8,128)}, bf16[512,2048]{1,0:T(8,128)(2,1)}, bf16[512,2048]{1,0:T(8,128)(2,1)}) custom-call(s32[1]{0:T(128)} %bitcast.4.seq_ref, bf16[128,2048]{1,0:T(8,128)(2,1)} %bitcast.67, bf16[1024,1024]{1,0:T(8,128)(2,1)} %all-gather.2.cloned.1.call-done.k_ref.v_ref, ...), custom_call_target="tpu_custom_call" | custom-call | flops 1610612736 | bytes 10485760 | tf_op jit(solution)/shard_map/pallas_call | solution.py:159
  63.1 12.6 %all-to-all-done.refs_0_.pairs = bf16[32,2,16,2048]{3,2,1,0:T(8,128)(2,1)} async-done(((bf16[32,2,16,2048]{3,2,1,0:T(8,128)(2,1)}), bf16[32,2,16,2048]{3,2,1,0:T(8,128)(2,1)}, u32[]{:S(2)}, u32[]{:S(2)}) %all-to-all-start) | async-done | bytes 4194336 | tf_op jit(solution)/shard_map/all_to_all | solution.py:602
  75.7 5.1 %all-to-all-start.1 = ((bf16[32,16,2048]{2,1,0:T(8,128)(2,1)}), bf16[32,16,2048]{2,1,0:T(8,128)(2,1)S(1)}, u32[]{:S(2)}, u32[]{:S(2)}) async-start(bf16[32,16,2048]{2,1,0:T(8,128)(2,1)} %bitcast.55), calls=%async_computation.1 | async-start | bytes 4194304 | tf_op jit(solution)/shard_map/all_to_all | solution.py:602
  80.8 28.4 %all-to-all-done.1 = bf16[32,16,2048]{2,1,0:T(8,128)(2,1)S(1)} async-done(((bf16[32,16,2048]{2,1,0:T(8,128)(2,1)}), bf16[32,16,2048]{2,1,0:T(8,128)(2,1)S(1)}, u32[]{:S(2)}, u32[]{:S(2)}) %all-to-all-start.1) | async-done | bytes 2097184 | tf_op jit(solution)/shard_map/all_to_all | solution.py:602
  109.2 0.0 copy-start
  109.2 1.3 copy-done
  110.5 5.3 %all-to-all-start.2 = ((bf16[32,16,2048]{2,1,0:T(8,128)(2,1)}), bf16[32,16,2048]{2,1,0:T(8,128)(2,1)}, u32[]{:S(2)}, u32[]{:S(2)}) async-start(bf16[32,16,2048]{2,1,0:T(8,128)(2,1)} %bitcast.51), calls=%async_computation.2 | async-start | bytes 4194304 | tf_op jit(solution)/shard_map/all_to_all | solution.py:602
  115.8 15.4 %shard_map.172 = (bf16[512,2048]{1,0:T(8,128)(2,1)}, bf16[512,704]{1,0:T(8,128)(2,1)}, bf16[512,704]{1,0:T(8,128)(2,1)}, bf16[512,704]{1,0:T(8,128)(2,1)}) custom-call(s32[1]{0:T(128)} %bitcast.3.core, bf16[512,2048]{1,0:T(8,128)(2,1)} %bitcast.53, bf16[32,2,16,2048]{3,2,1,0:T(8,128)(2,1)} %all-to-all-done.refs_0_.pairs, bf16[2,704,2048]{2,1,0:T(8,128)(2,1)} %bitcast.58, ...), custom_call_target="tpu_custom_call" | custom-call | flops 738197504000 | bytes 1677721600 | tf_op jit(solution)/shard_map/pallas_call | solution.py:215
  131.2 13.1 %all-to-all-done.2 = bf16[32,16,2048]{2,1,0:T(8,128)(2,1)} async-done(((bf16[32,16,2048]{2,1,0:T(8,128)(2,1)}), bf16[32,16,2048]{2,1,0:T(8,128)(2,1)}, u32[]{:S(2)}, u32[]{:S(2)}) %all-to-all-start.2) | async-done | bytes 2097184 | tf_op jit(solution)/shard_map/all_to_all | solution.py:602
  144.3 7.7 %shard_map.174 = (f32[512,704]{1,0:T(8,128)}, f32[512,704]{1,0:T(8,128)}, bf16[512,704]{1,0:T(8,128)(2,1)}) custom-call(s32[1]{0:T(128)} %bitcast.3.core, bf16[512,2048]{1,0:T(8,128)(2,1)} %bitcast.14.rows.rows_b, bf16[2,704,2048]{2,1,0:T(8,128)(2,1)} %bitcast.59, bf16[2,704,2048]{2,1,0:T(8,128)(2,1)} %bitcast.62), custom_call_target="tpu_custom_call" | custom-call | flops 295279001600 | bytes 1048576000 | tf_op jit(solution)/shard_map/pallas_call | solution.py:270
  152.1 7.2 %shard_map.177 = (bf16[4,704,256]{2,1,0:T(8,128)(2,1)}, bf16[4,704,256]{2,1,0:T(8,128)(2,1)}) custom-call(s32[1]{0:T(128)} %bitcast.3.core, bf16[32,2,16,2048]{3,2,1,0:T(8,128)(2,1)} %all-to-all-done.refs_0_.pairs, bf16[512,704]{1,0:T(8,128)(2,1)} %get-tuple-element.48.act_a, bf16[512,704]{1,0:T(8,128)(2,1)} %get-tuple-element.50.act_b), custom_call_target="tpu_custom_call" | custom-call | flops 295279001600 | bytes 838860800 | tf_op jit(solution)/shard_map/pallas_call | solution.py:360
  159.3 0.8 collective-permute-start
  160.1 4.5 %all-to-all-start.4 = ((bf16[32,16,2048]{2,1,0:T(8,128)(2,1)}), bf16[32,16,2048]{2,1,0:T(8,128)(2,1)}, u32[]{:S(2)}, u32[]{:S(2)}) async-start(bf16[32,16,2048]{2,1,0:T(8,128)(2,1)} %bitcast.16), calls=%async_computation.4 | async-start | bytes 4194304 | tf_op jit(solution)/shard_map/all_to_all | solution.py:602
  164.6 0.0 reduce-scatter.8.cloned.1.call-start
  164.7 0.0 collective-permute-done.other
  164.7 0.0 copy-start.1
  164.7 1.1 copy-done.1
  165.8 4.1 %shard_map.178.refs_0_ = bf16[4,2,704,256]{3,2,1,0:T(8,128)(2,1)} custom-call(s32[1]{0:T(128)} %bitcast.3.core, bf16[4,704,256]{2,1,0:T(8,128)(2,1)} %get-tuple-element.53.keep, bf16[4,704,256]{2,1,0:T(8,128)(2,1)} %copy-done.1), custom_call_target="tpu_custom_call" | custom-call | bytes 629145600 | tf_op jit(solution)/shard_map/pallas_call | solution.py:386
  169.9 0.0 reduce-scatter.8.cloned.1.call-update
  169.9 12.3 %shard_map.180 = (bf16[512,2048]{1,0:T(8,128)(2,1)}, bf16[512,704]{1,0:T(8,128)(2,1)}, bf16[512,704]{1,0:T(8,128)(2,1)}) custom-call(s32[1]{0:T(128)} %bitcast.3.core, f32[512,704]{1,0:T(8,128)} %shard_map.179.gate_in, f32[512,704]{1,0:T(8,128)} %get-tuple-element.57.up_in, bf16[32,2,16,2048]{3,2,1,0:T(8,128)(2,1)} %all-to-all-done.refs_0_.pairs, ...), custom_call_target="tpu_custom_call" | custom-call | flops 442918502400 | bytes 1677721600 | tf_op jit(solution)/shard_map/pallas_call | solution.py:299
  182.2 10.4 %shard_map.182 = (bf16[4,704,256]{2,1,0:T(8,128)(2,1)}, bf16[4,704,256]{2,1,0:T(8,128)(2,1)}, bf16[4,704,256]{2,1,0:T(8,128)(2,1)}, bf16[4,704,256]{2,1,0:T(8,128)(2,1)}) custom-call(s32[1]{0:T(128)} %bitcast.3.core, bf16[512,2048]{1,0:T(8,128)(2,1)} %bitcast.54, bf16[512,2048]{1,0:T(8,128)(2,1)} %bitcast.14.rows.rows_b, ...), custom_call_target="tpu_custom_call" | custom-call | flops 590558003200 | bytes 1677721600 | tf_op jit(solution)/shard_map/pallas_call | solution.py:360
  192.6 0.2 collective-permute-start.1
  192.8 0.3 collective-permute-start.2
  193.1 0.0 all-to-all-done.4
  193.1 7.5 %all-to-all-start.5 = ((bf16[32,16,2048]{2,1,0:T(8,128)(2,1)}), bf16[32,16,2048]{2,1,0:T(8,128)(2,1)}, u32[]{:S(2)}, u32[]{:S(2)}) async-start(bf16[32,16,2048]{2,1,0:T(8,128)(2,1)} %bitcast.18), calls=%async_computation.5 | async-start | bytes 4194304 | tf_op jit(solution)/shard_map/all_to_all | solution.py:602
  200.6 0.0 reduce-scatter.6.cloned.1.call-start
  200.6 7.5 %shard_map.175 = bf16[32,2,16,2048]{3,2,1,0:T(8,128)(2,1)} custom-call(s32[1]{0:T(128)} %bitcast.3.core, bf16[512,704]{1,0:T(8,128)(2,1)} %get-tuple-element.48.act_a, bf16[512,704]{1,0:T(8,128)(2,1)} %get-tuple-element.50.act_b, bf16[2,704,2048]{2,1,0:T(8,128)(2,1)} %down_w.5), custom_call_target="tpu_custom_call" | custom-call | flops 295279001600 | bytes 943718400 | tf_op jit(solution)/shard_map/pallas_call | solution.py:408
  208.2 0.0 collective-permute-done.2.other
  208.2 4.1 %shard_map.184.refs_0_ = bf16[4,2,704,256]{3,2,1,0:T(8,128)(2,1)} custom-call(s32[1]{0:T(128)} %bitcast.3.core, bf16[4,704,256]{2,1,0:T(8,128)(2,1)} %get-tuple-element.65.keep, bf16[4,704,256]{2,1,0:T(8,128)(2,1)} %collective-permute-done.2.other), custom_call_target="tpu_custom_call" | custom-call | bytes 629145600 | tf_op jit(solution)/shard_map/pallas_call | solution.py:386
  212.3 0.0 collective-permute-done.1.other
  212.3 4.1 %shard_map.183.refs_0_ = bf16[4,2,704,256]{3,2,1,0:T(8,128)(2,1)} custom-call(s32[1]{0:T(128)} %bitcast.3.core, bf16[4,704,256]{2,1,0:T(8,128)(2,1)} %get-tuple-element.63.keep, bf16[4,704,256]{2,1,0:T(8,128)(2,1)} %collective-permute-done.1.other), custom_call_target="tpu_custom_call" | custom-call | bytes 629145600 | tf_op jit(solution)/shard_map/pallas_call | solution.py:386
  216.4 0.0 reduce-scatter.6.cloned.1.call-update
  216.4 12.6 %all-to-all-done.5 = bf16[32,16,2048]{2,1,0:T(8,128)(2,1)} async-done(((bf16[32,16,2048]{2,1,0:T(8,128)(2,1)}), bf16[32,16,2048]{2,1,0:T(8,128)(2,1)}, u32[]{:S(2)}, u32[]{:S(2)}) %all-to-all-start.5) | async-done | bytes 2097184 | tf_op jit(solution)/shard_map/all_to_all | solution.py:602
  229.0 5.4 %all-to-all-start.3 = ((bf16[32,2,16,2048]{3,2,1,0:T(8,128)(2,1)}), bf16[32,2,16,2048]{3,2,1,0:T(8,128)(2,1)}, u32[]{:S(2)}, u32[]{:S(2)}) async-start(bf16[32,2,16,2048]{3,2,1,0:T(8,128)(2,1)} %shard_map.175), calls=%async_computation.3 | async-start | bytes 8388608 | tf_op jit(solution)/shard_map/all_to_all | solution.py:602
  234.4 0.0 reduce-scatter.4.cloned.1.call-start
  234.5 14.8 %shard_map.187 = (bf16[128,2048]{1,0:T(8,128)(2,1)}, bf16[128,2048]{1,0:T(8,128)(2,1)}, bf16[4,128,1024]{2,1,0:T(8,128)(2,1)}, bf16[4,128,1024]{2,1,0:T(8,128)(2,1)}) custom-call(s32[1]{0:T(128)} %bitcast.4.seq_ref, bf16[128,2048]{1,0:T(8,128)(2,1)} %bitcast.68, bf16[1024,1024]{1,0:T(8,128)(2,1)} %all-gather.2.cloned.1.call-done.k_ref.v_ref, ...), custom_call_target="tpu_custom_call" | custom-call | flops 322122547200 | bytes 1258291200 | tf_op jit(solution)/shard_map/pallas_call | solution.py:492
  249.3 0.0 copy-start.2
  249.3 0.4 collective-permute-start.3
  249.7 0.0 reduce-scatter.4.cloned.1.call-update
  249.7 2.5 collective-permute-done.3
  252.2 0.0 copy-start.3
  252.2 0.0 copy-done.2
  252.2 1.3 fusion.4
  253.6 1.3 collective-permute-start.4
  254.8 1.3 collective-permute-start.6
  256.1 1.3 collective-permute-start.5
  257.4 32.8 %all-to-all-done.3.returned = bf16[32,2,16,2048]{3,2,1,0:T(8,128)(2,1)} async-done(((bf16[32,2,16,2048]{3,2,1,0:T(8,128)(2,1)}), bf16[32,2,16,2048]{3,2,1,0:T(8,128)(2,1)}, u32[]{:S(2)}, u32[]{:S(2)}) %all-to-all-start.3) | async-done | bytes 4194336 | tf_op jit(solution)/shard_map/all_to_all | solution.py:602
  290.3 6.2 %shard_map.176 = (bf16[128,2048]{1,0:T(8,128)(2,1)}, f32[6,1,128]{2,1,0:T(1,128)}) custom-call(s32[6,1,128]{2,1,0:T(1,128)} %bitcast.77, bf16[2,512,128]{2,1,0:T(8,128)(2,1)} %get-tuple-element.42.pick, f32[2,512,128]{2,1,0:T(8,128)} %get-tuple-element.43.mixed, bf16[32,2,16,2048]{3,2,1,0:T(8,128)(2,1)} %all-to-all-done.3.returned, ...), custom_call_target="tpu_custom_call" | custom-call | flops 161061273600 | bytes 838860800 | tf_op jit(solution)/shard_map/pallas_call | solution.py:562
  296.4 0.0 copy-done.3
  296.4 0.0 collective-permute-done.4
  296.4 0.0 collective-permute-done.6
  296.4 0.0 collective-permute-done.5
  296.5 1.5 fusion.2
  297.9 0.7 slice_bitcast_fusion
  (9 shorter events, 0.0 us)
Async XLA Ops:
  11.7 8.8 %copy-start.4 = (bf16[1,128,512]{2,1,0:T(8,128)(2,1)S(1)}, bf16[1,128,512]{2,1,0:T(8,128)(2,1)}, u32[]{:S(2)}) copy-start(bf16[1,128,512]{2,1,0:T(8,128)(2,1)} %param.13) | copy-start | bytes 393220
  11.7 8.9 %copy-start.5 = (bf16[1,128,512]{2,1,0:T(8,128)(2,1)S(1)}, bf16[1,128,512]{2,1,0:T(8,128)(2,1)}, u32[]{:S(2)}) copy-start(bf16[1,128,512]{2,1,0:T(8,128)(2,1)} %param.12) | copy-start | bytes 393220
  11.7 64.0 %all-to-all-start = ((bf16[32,2,16,2048]{3,2,1,0:T(8,128)(2,1)}), bf16[32,2,16,2048]{3,2,1,0:T(8,128)(2,1)}, u32[]{:S(2)}, u32[]{:S(2)}) async-start(bf16[32,2,16,2048]{3,2,1,0:T(8,128)(2,1)} %get-tuple-element.44), calls=%async_computation | async-start | bytes 8388608 | tf_op jit(solution)/shard_map/all_to_all | solution.py:602
  20.5 31.0 %all-gather.2.cloned.1.call-start = ((), (), s32[]{:S(2)}) async-start(), calls=%async_computation.9 | async-start | bytes 2359296 | tf_op jit(solution)/shard_map/all_gather | solution.py:650
  75.7 33.5 %all-to-all-start.1 = ((bf16[32,16,2048]{2,1,0:T(8,128)(2,1)}), bf16[32,16,2048]{2,1,0:T(8,128)(2,1)S(1)}, u32[]{:S(2)}, u32[]{:S(2)}) async-start(bf16[32,16,2048]{2,1,0:T(8,128)(2,1)} %bitcast.55), calls=%async_computation.1 | async-start | bytes 4194304 | tf_op jit(solution)/shard_map/all_to_all | solution.py:602
  109.2 1.3 copy-start
  110.5 33.8 %all-to-all-start.2 = ((bf16[32,16,2048]{2,1,0:T(8,128)(2,1)}), bf16[32,16,2048]{2,1,0:T(8,128)(2,1)}, u32[]{:S(2)}, u32[]{:S(2)}) async-start(bf16[32,16,2048]{2,1,0:T(8,128)(2,1)} %bitcast.51), calls=%async_computation.2 | async-start | bytes 4194304 | tf_op jit(solution)/shard_map/all_to_all | solution.py:602
  159.3 5.4 %collective-permute-start = (bf16[4,704,256]{2,1,0:T(8,128)(2,1)}, bf16[4,704,256]{2,1,0:T(8,128)(2,1)S(1)}, u32[]{:S(2)}, u32[]{:S(2)}) collective-permute-start(bf16[4,704,256]{2,1,0:T(8,128)(2,1)} %get-tuple-element.54), channel_id=1, source_target_pairs={{0,16},{16,0},{32,48},{48,32},{64,80},{80,64},{96,112},{112,96},{1... | collective-permute-start | bytes 4325384 | tf_op jit(solution)/shard_map/ppermute | solution.py:612
  160.1 33.0 %all-to-all-start.4 = ((bf16[32,16,2048]{2,1,0:T(8,128)(2,1)}), bf16[32,16,2048]{2,1,0:T(8,128)(2,1)}, u32[]{:S(2)}, u32[]{:S(2)}) async-start(bf16[32,16,2048]{2,1,0:T(8,128)(2,1)} %bitcast.16), calls=%async_computation.4 | async-start | bytes 4194304 | tf_op jit(solution)/shard_map/all_to_all | solution.py:602
  164.6 134.0 %reduce-scatter.8.cloned.1.call-start = ((), (), s32[]{:S(2)}) async-start(), calls=%async_computation.12 | async-start | bytes 3604480 | tf_op jit(solution)/shard_map/reduce_scatter | solution.py:690
  164.7 1.1 copy-start.1
  192.6 19.7 %collective-permute-start.1 = (bf16[4,704,256]{2,1,0:T(8,128)(2,1)}, bf16[4,704,256]{2,1,0:T(8,128)(2,1)}, u32[]{:S(2)}, u32[]{:S(2)}) collective-permute-start(bf16[4,704,256]{2,1,0:T(8,128)(2,1)} %get-tuple-element.64), channel_id=1, source_target_pairs={{0,16},{16,0},{32,48},{48,32},{64,80},{80,64},{96,112},{112,96},{1... | collective-permute-start | bytes 4325384 | tf_op jit(solution)/shard_map/ppermute | solution.py:612
  192.8 15.4 %collective-permute-start.2 = (bf16[4,704,256]{2,1,0:T(8,128)(2,1)}, bf16[4,704,256]{2,1,0:T(8,128)(2,1)}, u32[]{:S(2)}, u32[]{:S(2)}) collective-permute-start(bf16[4,704,256]{2,1,0:T(8,128)(2,1)} %get-tuple-element.66), channel_id=1, source_target_pairs={{0,16},{16,0},{32,48},{48,32},{64,80},{80,64},{96,112},{112,96},{1... | collective-permute-start | bytes 4325384 | tf_op jit(solution)/shard_map/ppermute | solution.py:612
  193.1 35.9 %all-to-all-start.5 = ((bf16[32,16,2048]{2,1,0:T(8,128)(2,1)}), bf16[32,16,2048]{2,1,0:T(8,128)(2,1)}, u32[]{:S(2)}, u32[]{:S(2)}) async-start(bf16[32,16,2048]{2,1,0:T(8,128)(2,1)} %bitcast.18), calls=%async_computation.5 | async-start | bytes 4194304 | tf_op jit(solution)/shard_map/all_to_all | solution.py:602
  200.6 98.1 %reduce-scatter.6.cloned.1.call-start = ((), (), s32[]{:S(2)}) async-start(), calls=%async_computation.11 | async-start | bytes 3604480 | tf_op jit(solution)/shard_map/reduce_scatter | solution.py:690
  229.0 61.2 %all-to-all-start.3 = ((bf16[32,2,16,2048]{3,2,1,0:T(8,128)(2,1)}), bf16[32,2,16,2048]{3,2,1,0:T(8,128)(2,1)}, u32[]{:S(2)}, u32[]{:S(2)}) async-start(bf16[32,2,16,2048]{3,2,1,0:T(8,128)(2,1)} %shard_map.175), calls=%async_computation.3 | async-start | bytes 8388608 | tf_op jit(solution)/shard_map/all_to_all | solution.py:602
  234.4 64.2 %reduce-scatter.4.cloned.1.call-start = ((), (), s32[]{:S(2)}) async-start(), calls=%async_computation.10 | async-start | bytes 3604480 | tf_op jit(solution)/shard_map/reduce_scatter | solution.py:690
  249.3 3.0 copy-start.2
  249.3 3.0 collective-permute-start.3
  252.2 44.2 %copy-start.3 = (bf16[4,128,1024]{2,1,0:T(8,128)(2,1)}, bf16[4,128,1024]{2,1,0:T(8,128)(2,1)S(1)}, u32[]{:S(2)}) copy-start(bf16[4,128,1024]{2,1,0:T(8,128)(2,1)S(1)} %collective-permute-done.3) | copy-start | bytes 3145732
  253.6 42.9 %collective-permute-start.4 = (bf16[128,1024]{1,0:T(8,128)(2,1)}, bf16[128,1024]{1,0:T(8,128)(2,1)}, u32[]{:S(2)}, u32[]{:S(2)}) collective-permute-start(bf16[128,1024]{1,0:T(8,128)(2,1)} %get-tuple-element.75), channel_id=1, source_target_pairs={{96,0},{112,16},{97,1},{113,17},{98,2},{114,18},{99,3},{115,19},{1... | collective-permute-start | bytes 786440 | tf_op jit(solution)/shard_map/ppermute | solution.py:621
  254.8 41.6 %collective-permute-start.6 = (bf16[128,1024]{1,0:T(8,128)(2,1)}, bf16[128,1024]{1,0:T(8,128)(2,1)}, u32[]{:S(2)}, u32[]{:S(2)}) collective-permute-start(bf16[128,1024]{1,0:T(8,128)(2,1)} %get-tuple-element.76), channel_id=1, source_target_pairs={{32,0},{48,16},{64,32},{80,48},{96,64},{112,80},{33,1},{49,17},{65... | collective-permute-start | bytes 786440 | tf_op jit(solution)/shard_map/ppermute | solution.py:621
  256.1 40.3 %collective-permute-start.5 = (bf16[128,1024]{1,0:T(8,128)(2,1)}, bf16[128,1024]{1,0:T(8,128)(2,1)}, u32[]{:S(2)}, u32[]{:S(2)}) collective-permute-start(bf16[128,1024]{1,0:T(8,128)(2,1)} %get-tuple-element.77), channel_id=1, source_target_pairs={{64,0},{80,16},{96,32},{112,48},{65,1},{81,17},{97,33},{113,49},{6... | collective-permute-start | bytes 786440 | tf_op jit(solution)/shard_map/ppermute | solution.py:621
Sparse Core Ops, SparseCore 0:
  23.6 27.7 all-gather.1
  170.0 38.2 reduce-scatter.7
  216.6 38.3 reduce-scatter.5
  257.8 37.8 reduce-scatter.3
